TPU v7x, 256 devices: a whole 4x4x8 slice. The times are simulated.
256 devices in a mesh: session: 64 (over x, z, core), kvhead: 4 (over y).
Axes of the slice: x: 4, y: 4, z: 8, core: 2. Of those that a mesh axis runs over, the one named last changes fastest.
Arguments:
- queries: bfloat16 [256, 16384], P(('session', 'kvhead')), may hold values from -12 to 12
- new_keys: bfloat16 [256, 1024], P('session', 'kvhead'), may hold values from -10.5 to 10.5
- new_values: bfloat16 [256, 1024], P('session', 'kvhead'), may hold values from -24 to 24
- sink_keys: bfloat16 [256, 4, 1024], P('session', None, 'kvhead'), may hold values from -10.5 to 10.5
- sink_values: bfloat16 [256, 4, 1024], P('session', None, 'kvhead'), may hold values from -24 to 24
- window_keys: bfloat16 [256, 512, 1024], P('session', None, 'kvhead'), may hold values from -9 to 9
- window_values: bfloat16 [256, 512, 1024], P('session', None, 'kvhead'), may hold values from -24 to 24
- window_len: int32 [256], P('session'), may hold values from 1 to 512, as said below
- root_keys: bfloat16 [32768, 1024], P('session', 'kvhead'), may hold values from -6 to 6
- root_values: bfloat16 [32768, 1024], P('session', 'kvhead'), may hold values from -24 to 24
- prefix_keys: bfloat16 [65536, 1024], P('session', 'kvhead'), may hold values from -6 to 6
- prefix_values: bfloat16 [65536, 1024], P('session', 'kvhead'), may hold values from -24 to 24
- tenant_of: int32 [256], replicated, may hold values from 0 to 63, as said below
- owner: int32 [64], replicated, may hold values from 0 to 63, each once
Outputs:
- attended: bfloat16 [256, 16384], P(('session', 'kvhead'))
Inputs may be any that keep to these rules, and one draw needn't show every extreme that they name: `window_len`: every device's 4 chats include one whose window holds 512 used slots. `tenant_of`: no tenant has more than 16 chats, and one tenant has exactly 16.
All inputs are finite; a program needn't handle non-finite values.
Results may differ from a plain program's by a relative error of at most 0.007.
Values may be sent and summed in bfloat16 or wider, within the bound.
No kernel may reach another device: no remote copies, remote signals or barrier semaphores. Data moves between devices by JAX's collectives and lax.ppermute only.
A program may use at most 64 MiB of HBM per device.

v0:
```python
import math

import jax
import jax.numpy as jnp
from jax import lax
from jax.sharding import PartitionSpec as P

HD = 128
GROUP = 16


floor_score = -1e30


def partial_shared(query_block, pieces):
    factor = query_block.shape[-1] ** (-0.5)
    score_list = []
    for key_rows, value_rows, chat_mask in pieces:
        scores = (
            jnp.einsum("cgqd,kgd->cgqk", query_block, key_rows, preferred_element_type=jnp.float32)
            * factor
        )
        if chat_mask is not None:
            scores = jnp.where(chat_mask[:, None, None, None], scores, floor_score)
        score_list.append(scores)
    joined = jnp.concatenate(score_list, axis=-1)
    row_peak = jnp.max(joined, axis=-1)
    weights = jnp.exp(joined - row_peak[..., None])
    row_total = jnp.sum(weights, axis=-1)
    rounded = weights.astype(jnp.bfloat16)
    numer = jnp.zeros(query_block.shape, jnp.float32)
    offset = 0
    for key_rows, value_rows, chat_mask in pieces:
        length = key_rows.shape[0]
        numer = numer + jnp.einsum(
            "cgqk,kgd->cgqd",
            rounded[..., offset : offset + length],
            value_rows,
            preferred_element_type=jnp.float32,
        )
        offset = offset + length
    return (row_peak, row_total, numer)


def local(
    queries,
    new_keys,
    new_values,
    sink_keys,
    sink_values,
    window_keys,
    window_values,
    window_len,
    root_keys,
    root_values,
    prefix_keys,
    prefix_values,
    tenant_of,
    owner,
):
    local_q = lax.all_to_all(queries, "kvhead", split_axis=1, concat_axis=0, tiled=True)
    home_chats = local_q.shape[0]
    kv_local = root_keys.shape[1] // HD
    heads_local = kv_local * GROUP
    gathered = lax.all_gather(local_q, "session", axis=0, tiled=True)
    chats = gathered.shape[0]
    device_index = lax.axis_index("session")
    root_k = root_keys.reshape(-1, kv_local, HD)
    root_v = root_values.reshape(-1, kv_local, HD)
    prefix_k = prefix_keys.reshape(-1, kv_local, HD)
    prefix_v = prefix_values.reshape(-1, kv_local, HD)
    tenant_mine = jnp.sum(
        jnp.where(owner == device_index, jnp.arange(owner.shape[0], dtype=jnp.int32), 0)
    )
    member = tenant_of == tenant_mine
    block_size = math.gcd(chats, 32)
    blocks = gathered.reshape(chats // block_size, block_size, kv_local, GROUP, HD)

    def block_dense(operands):
        query_block, mask_block = operands
        return partial_shared(
            query_block, [(root_k, root_v, None), (prefix_k, prefix_v, mask_block)]
        )

    peak_all, total_all, numer_all = lax.map(
        block_dense, (blocks, member.reshape(chats // block_size, block_size))
    )
    peak_all = peak_all.reshape(chats, heads_local)
    total_all = total_all.reshape(chats, heads_local)
    numer_all = numer_all.reshape(chats, heads_local, HD)
    share = (numer_all / total_all[..., None]).astype(jnp.bfloat16)
    factor = HD ** (-0.5)
    query_home = local_q.reshape(home_chats, kv_local, GROUP, HD)
    sink_k = sink_keys.reshape(home_chats, -1, kv_local, HD)
    sink_v = sink_values.reshape(home_chats, -1, kv_local, HD)
    recent_k = window_keys.reshape(home_chats, -1, kv_local, HD)
    recent_v = window_values.reshape(home_chats, -1, kv_local, HD)
    fresh_k = new_keys.reshape(home_chats, kv_local, HD)
    fresh_v = new_values.reshape(home_chats, kv_local, HD)
    sink_count = sink_k.shape[1]
    slot_count = recent_k.shape[1]
    sink_scores = (
        jnp.einsum("cgqd,ckgd->cgqk", query_home, sink_k, preferred_element_type=jnp.float32)
        * factor
    )
    recent_scores = (
        jnp.einsum("cgqd,ckgd->cgqk", query_home, recent_k, preferred_element_type=jnp.float32)
        * factor
    )
    used = jnp.arange(slot_count, dtype=jnp.int32)[None, :] < window_len[:, None]
    recent_scores = jnp.where(used[:, None, None, :], recent_scores, floor_score)
    fresh_scores = (
        jnp.einsum("cgqd,cgd->cgq", query_home, fresh_k, preferred_element_type=jnp.float32)[
            ..., None
        ]
        * factor
    )
    local_scores = jnp.concatenate([sink_scores, recent_scores, fresh_scores], axis=-1)
    local_peak = jnp.max(local_scores, axis=-1)
    local_weights = jnp.exp(local_scores - local_peak[..., None])
    local_total = jnp.sum(local_weights, axis=-1)
    local_rounded = local_weights.astype(jnp.bfloat16)
    local_numer = jnp.einsum(
        "cgqk,ckgd->cgqd",
        local_rounded[..., :sink_count],
        sink_v,
        preferred_element_type=jnp.float32,
    )
    local_numer = local_numer + jnp.einsum(
        "cgqk,ckgd->cgqd",
        local_rounded[..., sink_count : sink_count + slot_count],
        recent_v,
        preferred_element_type=jnp.float32,
    )
    local_numer = local_numer + jnp.einsum(
        "cgq,cgd->cgqd", local_rounded[..., -1], fresh_v, preferred_element_type=jnp.float32
    )
    local_peak = local_peak.reshape(home_chats, heads_local)
    local_total = local_total.reshape(home_chats, heads_local)
    local_numer = local_numer.reshape(home_chats, heads_local, HD)
    global_peak = lax.pmax(peak_all, "session")
    far_weight = total_all * jnp.exp(peak_all - global_peak)
    scaled_share = (share.astype(jnp.float32) * far_weight[..., None]).reshape(
        chats, heads_local * HD
    )
    home_numer, home_total = (
        lax.psum_scatter(scaled_share, "session", scatter_dimension=0, tiled=True),
        lax.psum_scatter(far_weight, "session", scatter_dimension=0, tiled=True),
    )
    home_peak = lax.dynamic_slice_in_dim(global_peak, device_index * home_chats, home_chats, 0)
    home_numer = home_numer.reshape(home_chats, heads_local, HD)
    merged_peak = jnp.maximum(home_peak, local_peak)
    far_scale = jnp.exp(home_peak - merged_peak)
    near_scale = jnp.exp(local_peak - merged_peak)
    merged_total = home_total * far_scale + local_total * near_scale
    merged_numer = home_numer * far_scale[..., None] + local_numer * near_scale[..., None]
    finished = (
        (merged_numer / merged_total[..., None])
        .astype(jnp.bfloat16)
        .reshape(home_chats, heads_local * HD)
    )
    return lax.all_to_all(finished, "kvhead", split_axis=0, concat_axis=1, tiled=True)


def solution(mesh):
    placed = (
        P(("session", "kvhead"), None),
        P("session", "kvhead"),
        P("session", "kvhead"),
        P("session", None, "kvhead"),
        P("session", None, "kvhead"),
        P("session", None, "kvhead"),
        P("session", None, "kvhead"),
        P("session"),
        P("session", "kvhead"),
        P("session", "kvhead"),
        P("session", "kvhead"),
        P("session", "kvhead"),
        P(),
        P(),
    )
    return jax.shard_map(
        local, mesh=mesh, in_specs=placed, out_specs=P(("session", "kvhead"), None), check_vma=False
    )
```

profile of v0, /device:TPU:8, one launch (start us, length us, event | category | flops | bytes accessed | tf_op | source)
XLA Modules:
  0.0 738.8 jit_solution(12142206438175256750)
XLA Ops:
  8.9 8.7 %all_to_all.32 = bf16[4,2,2048]{2,1,0:T(2,128)(2,1)S(1)} all-to-all(bf16[4,2,2048]{2,1,0:T(2,128)(2,1)S(1)} %reshape.174), channel_id=1, replica_groups=mesh['session'=64,'kvhead'=4] {'kvhead'}, dimensions={0} | all-to-all | bytes 65536 | tf_op jit(solution)/shard_map/all_to_all | solution.py:61
  29.0 70.4 %all-gather.3.cloned.1.call-done = bf16[1,256,4096]{2,0,1:T(2,128)(2,1)} async-done(((bf16[1,4,4096]{2,0,1:T(2,128)(2,1)}), bf16[1,256,4096]{2,0,1:T(2,128)(2,1)}) %all-gather.3.cloned.1.call-update) | async-done | bytes 2097168 | tf_op jit(solution)/shard_map/all_gather | solution.py:65
  99.3 14.2 %reduce.5 = bf16[256,4096]{1,0:T(8,128)(2,1)} reduce(bf16[1,256,4096]{2,0,1:T(2,128)(2,1)} %all-gather.3.cloned.1.call-done, bf16[]{:T(256)} %constant.63), dimensions={0}, to_apply=%all-gather.reduce_sub_computation | reduce | bytes 4194306 | tf_op jit(solution)/shard_map/all_gather | solution.py:65
  113.6 3.4 copy.154
  117.0 86.4 %while.14 = (s32[]{:T(128)}, f32[8,32,2,16]{1,0,3,2:T(8,128)S(1)}, f32[8,32,2,16]{1,0,3,2:T(8,128)S(1)}, f32[8,32,2,16,128]{4,3,2,1,0:T(8,128)}, bf16[8,32,2,16,...) while((s32[]{:T(128)}, f32[8,32,2,16]{1,0,3,2:T(8,128)S(1)}, ...), condition=%wide.region_5.6_spmd, body=%wide.region_1.5_spmd.sunk | while | flops 815921152 | bytes 23654644 | solution.py:85
  120.3 2.4 fusion.60
  122.9 2.3 fusion.61
  131.0 2.4 fusion.60
  133.7 2.3 fusion.61
  141.9 2.4 fusion.60
  144.5 2.3 fusion.61
  152.7 2.4 fusion.60
  163.5 2.4 fusion.60
  166.2 2.3 fusion.61
  174.3 2.4 fusion.60
  177.0 2.3 fusion.61
  185.1 2.4 fusion.60
  187.8 2.3 fusion.61
  195.9 2.4 fusion.60
  203.4 5.0 reshape.143
  208.8 248.7 %pmax.7 = f32[256,32]{1,0:T(8,128)S(1)} all-reduce(f32[256,32]{1,0:T(8,128)S(1)} %copy.123), channel_id=1, replica_groups=mesh['session'=64,'kvhead'=4] {'session'}, use_global_device_ids=true, to_apply=%region_6.7 | all-reduce | flops 8192 | bytes 65536 | tf_op jit(solution)/shard_map/pmax | solution.py:141
  459.8 10.2 %bitcast_multiply_fusion = f32[256,4096]{1,0:T(8,128)} fusion(f32[32,8,32,128]{3,2,1,0:T(8,128)S(1)} %bitcast.174, f32[256,4096]{1,0:T(8,128)S(1)} %copy-done.1, f32[32,8,32,128]{3,2,1,0:T(8,128)S(1)} %bitcast.175), kind=kLoop, calls=%fused_computation.19 | loop fusion | flops 4194304 | bytes 16777216 | tf_op jit(solution)/shard_map/mul | solution.py:143
  473.6 246.9 %all-reduce.1 = f32[256,32]{0,1:T(8,128)S(1)} all-reduce(f32[256,32]{0,1:T(8,128)S(1)} %copy.132), channel_id=4, replica_groups=mesh['session'=64,'kvhead'=4] {'session'}, use_global_device_ids=true, to_apply=%region_10.11.clone | all-reduce | flops 8192 | bytes 65536
  722.8 8.5 %all_to_all.33 = bf16[4,2,2048]{2,1,0:T(2,128)(2,1)S(1)} all-to-all(bf16[4,2,2048]{2,1,0:T(2,128)(2,1)S(1)} %reshape.176), channel_id=1, replica_groups=mesh['session'=64,'kvhead'=4] {'kvhead'}, dimensions={0} | all-to-all | bytes 65536 | tf_op jit(solution)/shard_map/all_to_all | solution.py:162
  (156 shorter events, 75.5 us)
Async XLA Ops:
  6.5 22.0 %copy-start = (bf16[4,512,256]{2,1,0:T(8,128)(2,1)S(1)}, bf16[4,512,256]{2,1,0:T(8,128)(2,1)}, u32[]{:S(2)}) copy-start(bf16[4,512,256]{2,1,0:T(8,128)(2,1)} %param.21) | copy-start | bytes 3145732
  6.5 20.5 %copy-start.7 = (u32[256]{0:T(256)S(1)}, u32[256]{0:T(256)}, u32[]{:S(2)}) copy-start(u32[256]{0:T(256)} %constant.57) | copy-start | bytes 3076
  6.5 20.0 %copy-start.3 = (bf16[1024,256]{1,0:T(8,128)(2,1)S(1)}, bf16[1024,256]{1,0:T(8,128)(2,1)}, u32[]{:S(2)}) copy-start(bf16[1024,256]{1,0:T(8,128)(2,1)} %param.27) | copy-start | bytes 1572868
  6.5 21.7 %copy-start.6 = (s32[4]{0:T(128)S(1)}, s32[4]{0:T(128)}, u32[]{:S(2)}) copy-start(s32[4]{0:T(128)} %param.23) | copy-start | bytes 52
  6.5 92.8 %all-gather.3.cloned.1.call-start = ((), (), s32[]{:S(2)}) async-start(), calls=%async_computation.2 | async-start | bytes 4259840 | tf_op jit(solution)/shard_map/all_gather | solution.py:65
  18.3 10.0 %copy-start.2 = (bf16[4,1,4096]{2,1,0:T(2,128)(2,1)S(1)}, bf16[4,1,4096]{2,1,0:T(2,128)(2,1)}, u32[]{:S(2)}) copy-start(bf16[4,1,4096]{2,1,0:T(2,128)(2,1)} %reshape.175) | copy-start | bytes 98308
  18.3 702.6 %all-reduce.4.cloned.1.call-start = ((), (), s32[]{:S(2)}) async-start(), calls=%async_computation.3 | async-start | bytes 8388608
  457.5 2.3 copy-start.1
  470.0 0.7 copy-start.4
  470.0 1.9 copy-start.5
Sparse Core Ops, SparseCore 0:
  18.5 80.8 all-gather.2
  470.1 189.6 all-reduce.3
where the time goes:
time: 741 us; the launch traced here: 739 us
  blocking collectives  513 us (69%)
  waiting for transfers between devices  70.4 us (10%)
  matrix products  59.9 us (8%)
  other arithmetic  50.2 us (7%)
  local copies, waits for them, and re-layouts  30.8 us (4%)
  between operations  14.2 us (2%)
    pmax x1, blocking collectives, local(): global_peak = lax.pmax(peak_all, 'session')  249 us
    unnamed x1, blocking collectives  247 us
    all_gather x1, waiting for transfers between devices, local(): gathered = lax.all_gather(local_q, 'session', axis=0, tiled=True)  70.4 us
    dot_general x16, matrix products, partial_shared(): jnp.einsum('cgqk,kgd->cgqd', rounded[..., offset:offset + length], value_...  31.7 us
    dot_general x16, matrix products, partial_shared(): jnp.einsum('cgqd,kgd->cgqk', query_block, key_rows, preferred_element_typ...  25.9 us
    convert_element_type x8, other arithmetic, partial_shared(): rounded = weights.astype(jnp.bfloat16)  19 us
  transfers between devices with their start and end apart: 2, of which 1 were waited for; matrix products, arithmetic and copies ran while one was open for 2% of the time, Pallas kernels for 0%

commit v1 on v0

v1 whole, which is shorter than its diff:
```python
import functools
import math

import jax
import jax.numpy as jnp
from jax import lax
from jax.experimental import pallas as pl
from jax.experimental.pallas import tpu as pltpu
from jax.sharding import Mesh, PartitionSpec as P

HD = 128
GROUP = 16
KV = 2
HEADS = KV * GROUP
HOME = 4
NX, NZ, NC, NY = 4, 8, 2, 4
ROWS = 40
SCALE2 = HD**-0.5 * math.log2(math.e)
FLOOR = -1e30
COLUMN = NZ * HOME
MEMBER = 8
ROOM = 8
MIB = 2**20

NT = (((1,), (1,)), ((), ()))
VMEM = pl.BlockSpec(memory_space=pltpu.VMEM)
SMEM = pl.BlockSpec(memory_space=pltpu.SMEM)
BF16 = jnp.bfloat16
F32 = jnp.float32


def scores_of(query, keys):
    return lax.dot_general(query, keys, NT, preferred_element_type=F32)


def dot(a, b):
    return jnp.dot(a, b, preferred_element_type=F32)


def iota(shape, dim):
    return lax.broadcasted_iota(jnp.int32, shape, dim)


def head_diagonal():
    return (iota((HEADS, HD), 1) % HEADS) == iota((HEADS, HD), 0)


def level_parts(level):
    first = level.astype(BF16).astype(F32)
    second = (level - first).astype(BF16).astype(F32)
    third = level - first - second
    row = iota((1, 8, HD), 1)
    parts = jnp.where(row == 2, third[:, None], 0.0)
    parts = jnp.where(row == 1, second[:, None], parts)
    return jnp.where(row == 0, first[:, None], parts).astype(BF16)


def prepare_kernel(tenant_ref, owner_ref, t_row, o_row, plan, rounds):
    x, z, c = lax.axis_index("x"), lax.axis_index("z"), lax.axis_index("c")
    zero = jnp.int32(0)

    def clear(i, _):
        for t in range(NX):
            plan[t, i] = zero
        return 0

    lax.fori_loop(0, COLUMN + 1, clear, 0, unroll=11)

    def slot_of(s, i):
        return owner_ref[tenant_ref[((s * NZ + (i >> 2)) * 2 + c) * HOME + (i & 3)]]

    def scan_send(i, found):
        slot = slot_of(x, i)
        target = jnp.where(((slot >> 1) & (NZ - 1)) == z, slot >> 4, NX)
        new = []
        for t in range(NX):
            plan[t, found[t]] = i
            new.append(found[t] + (target == t).astype(jnp.int32))
        return tuple(new)

    found = lax.fori_loop(0, COLUMN, scan_send, (zero,) * NX, unroll=8)
    for t in range(NX):
        plan[2 * NX, t] = found[t]

    mine = x * NZ + z

    def scan_recv(i, found):
        new = []
        for s in range(NX):
            slot = slot_of(s, i)
            plan[NX + s, found[s]] = (slot & 1) ^ c
            new.append(found[s] + ((slot >> 1) == mine).astype(jnp.int32))
        return tuple(new)

    found = lax.fori_loop(0, COLUMN, scan_recv, (zero,) * NX, unroll=4)
    for s in range(NX):
        plan[2 * NX, NX + s] = found[s]

    chats = NX * NC * COLUMN
    tenants = o_row.shape[1]
    o_col = jnp.sum(
        jnp.where(iota((tenants, tenants), 0) == iota((tenants, tenants), 1), o_row[...] >> 1, 0),
        axis=1,
        keepdims=True,
    )
    by_row = jnp.sum(
        jnp.where(t_row[...] == iota((tenants, chats), 0), o_col, 0), axis=0, keepdims=True
    )

    def key(chip, chat):
        place = chat >> 2
        return (((place >> 4) * 2 + (place & 1)) << 5) + chip

    row = key(by_row, iota((1, chats), 1))
    square = (chats, chats)
    col = jnp.sum(
        jnp.where(iota(square, 0) == iota(square, 1), row, 0), axis=1, keepdims=True
    )
    fullest = jnp.max(jnp.sum(jnp.where(col == row, 1.0, 0.0), axis=1, keepdims=True))
    rounds[0] = (fullest.astype(jnp.int32) + ROOM - 1) >> 3


def root_part(q_ref, blocks, values, out):
    for g in range(KV):
        for n, (_, _, v0, v1) in enumerate(blocks):
            for i, v in enumerate((v0, v1)):
                rows = slice(n * 1024 + i * 512, n * 1024 + (i + 1) * 512)
                values[g, rows, :HD] = v[:, g * HD : (g + 1) * HD]
                values[g, rows, HD:] = jnp.ones((512, HD), BF16)
    diagonal = head_diagonal()
    rows = COLUMN // 2
    for h in range(2):
        chats = slice(h * rows, (h + 1) * rows)
        line = None
        for g in range(KV):
            heads = slice(g * GROUP, (g + 1) * GROUP)
            lanes = slice(g * HD, (g + 1) * HD)
            query = q_ref[chats, heads, :].reshape(rows * GROUP, HD)
            scores = [scores_of(query, k[:, lanes]) for block in blocks for k in block[:2]]
            peak = functools.reduce(
                jnp.maximum, [jnp.max(s, axis=1, keepdims=True) for s in scores]
            )
            numer = None
            for n, s in enumerate(scores):
                weights = jnp.exp2((s - peak) * SCALE2).astype(BF16)
                part = dot(weights, values[g, n * 512 : (n + 1) * 512, :])
                numer = part if numer is None else numer + part
            total = numer[:, HD:]
            share = (numer[:, :HD] / total).astype(BF16)
            out[chats, heads, :] = share.reshape(rows, GROUP, HD)
            level = (peak * SCALE2 + jnp.log2(total)).reshape(rows, GROUP, HD)
            part = jnp.sum(jnp.where(diagonal[None, heads], level, 0.0), axis=1)
            line = part if line is None else line + part
        out[chats, HEADS:, :] = level_parts(line)


def home_part(length_ref, q_ref, wk, wv, sk, sv, nk, nv, share_ref, level_ref):
    diagonal = head_diagonal()
    first = lax.axis_index("z") * HOME
    pad = jnp.zeros((3, KV * HD), F32)
    few_k, few_v = (
        [
            jnp.concatenate([s[j].astype(F32), n[j : j + 1].astype(F32), pad]).astype(BF16)
            for j in range(HOME)
        ]
        for s, n in ((sk, nk), (sv, nv))
    )
    pairs = [(g, j) for g in range(KV) for j in range(HOME)]
    recent, few = [], []
    for g, j in pairs:
        lanes = slice(g * HD, (g + 1) * HD)
        query = q_ref[first + j, g * GROUP : (g + 1) * GROUP, :]
        used = iota((GROUP, 512), 1) < length_ref[j]
        recent.append(jnp.where(used, scores_of(query, wk[j, :, lanes]), FLOOR))
        few.append(scores_of(query, few_k[j][:, lanes]))
    recent = jnp.concatenate(recent, axis=0)
    few = jnp.concatenate(few, axis=0)
    few = jnp.where(iota(few.shape, 1) < 5, few, FLOOR)
    peak = jnp.maximum(jnp.max(recent, axis=1, keepdims=True), jnp.max(few, axis=1, keepdims=True))
    recent = jnp.exp2((recent - peak) * SCALE2)
    few = jnp.exp2((few - peak) * SCALE2)
    total = jnp.sum(recent, axis=1, keepdims=True) + jnp.sum(few, axis=1, keepdims=True)
    recent, few = recent.astype(BF16), few.astype(BF16)
    level = jnp.broadcast_to(peak * SCALE2 + jnp.log2(total), (KV * HOME * GROUP, HD))
    level = level.reshape(KV, HOME, GROUP, HD)
    line = None
    for g in range(KV):
        part = jnp.where(diagonal[None, g * GROUP : (g + 1) * GROUP], level[g], 0.0)
        part = jnp.sum(part, axis=1)
        line = part if line is None else line + part
    level_ref[...] = line
    for n, (g, j) in enumerate(pairs):
        lanes = slice(g * HD, (g + 1) * HD)
        rows = slice(n * GROUP, (n + 1) * GROUP)
        numer = dot(recent[rows], wv[j, :, lanes]) + dot(few[rows], few_v[j][:, lanes])
        share_ref[j, g * GROUP : (g + 1) * GROUP, :] = numer / total[rows]


def near_kernel(
    length_ref, q_ref, k0, k1, v0, v1, wk, wv, sk, sv, nk, nv, out, share, level, values, wks, wvs, sems
):
    copies = [
        pltpu.make_async_copy(wk, wks, sems.at[0]),
        pltpu.make_async_copy(wv, wvs, sems.at[1]),
    ]
    for copy in copies:
        copy.start()
    root_part(q_ref, [(k0, k1, v0, v1)], values, out)
    for copy in copies:
        copy.wait()
    home_part(length_ref, q_ref, wks, wvs, sk, sv, nk, nv, share, level)


def far_kernel(q_ref, *refs):
    out, values = refs[-2:]
    root_part(q_ref, [refs[4 * n : 4 * n + 4] for n in range(NX - 1)], values, out)


def select_kernel(plan, turn, q_ref, out):
    start = turn if isinstance(turn, int) else turn[0] * ROOM
    chats = [plan[t, start + e] for t in range(NX) for e in range(ROOM)]
    for n, chat in enumerate(chats):
        out[n] = q_ref[chat]


def prefix_kernel(plan, turn, q_ref, pk0, pk1, pv0, pv1, out, qs, lists):
    start = turn if isinstance(turn, int) else turn[0] * ROOM
    diagonal = head_diagonal()
    zero = jnp.int32(0)
    lists[0, 0] = zero
    lists[1, 0] = zero
    n0, n1 = zero, zero
    for s in range(NX):

        def scan(e, found, s=s):
            slot = plan[NX + s, start + e]
            lists[0, found[0]] = s * ROOM + e
            lists[1, found[1]] = s * ROOM + e
            return found[0] + 1 - slot, found[1] + slot

        left = jnp.clip(plan[2 * NX, NX + s] - start, 0, ROOM)
        n0, n1 = lax.fori_loop(0, left, scan, (n0, n1))
    slots = ((pk0, pv0, n0), (pk1, pv1, n1))

    def step(b, _):
        results = []
        for i, (pk, pv, count) in enumerate(slots):
            last = jnp.maximum(count - 1, 0)
            chats = [lists[i, jnp.minimum(b * MEMBER + j, last)] for j in range(MEMBER)]
            line = None
            shares = []
            for g in range(KV):
                heads = slice(g * GROUP, (g + 1) * GROUP)
                lanes = slice(g * HD, (g + 1) * HD)
                for j, chat in enumerate(chats):
                    qs[i, g, j] = q_ref[chat, heads, :]
                scores = scores_of(qs[i, g].reshape(MEMBER * GROUP, HD), pk[:, lanes])
                peak = jnp.max(scores, axis=1, keepdims=True)
                weights = jnp.exp2((scores - peak) * SCALE2)
                total = jnp.sum(weights, axis=1, keepdims=True)
                numer = dot(weights.astype(BF16), pv[:, lanes])
                shares.append((numer / total).astype(BF16))
                level = jnp.broadcast_to(peak * SCALE2 + jnp.log2(total), (MEMBER * GROUP, HD))
                level = level.reshape(MEMBER, GROUP, HD)
                part = jnp.sum(jnp.where(diagonal[None, heads], level, 0.0), axis=1)
                line = part if line is None else line + part
            results.append((chats, shares, level_parts(line)))
        for (chats, shares, parts), (_, _, count) in zip(results, slots):

            @pl.when(b * MEMBER < count)
            def _(chats=chats, shares=shares, parts=parts):
                for j, chat in enumerate(chats):
                    for g in range(KV):
                        rows = slice(j * GROUP, (j + 1) * GROUP)
                        out[chat, g * GROUP : (g + 1) * GROUP, :] = shares[g][rows]
                    out[chat, HEADS:, :] = parts[j]

        return 0

    lax.fori_loop(0, (jnp.maximum(n0, n1) + MEMBER - 1) >> 3, step, 0)


def place_answers(plan, start, back, out):
    for t in range(NX):

        def place(e, _, t=t):
            out[plan[t, start + e]] = back[t * ROOM + e]
            return 0

        lax.fori_loop(0, jnp.clip(plan[2 * NX, t] - start, 0, ROOM), place, 0)


def scatter_kernel(plan, turn, back, before, out):
    out[...] = before[...]
    place_answers(plan, turn[0] * ROOM, back, out)


def weights_of(levels):
    top = functools.reduce(jnp.maximum, levels)
    weights = [jnp.exp2(v - top) for v in levels]
    total = functools.reduce(jnp.add, weights)
    return [w / total for w in weights], top + jnp.log2(total)


def read_level(ref):
    return jnp.sum(ref[:, HEADS:, :].astype(F32), axis=1)


def four_lines(weights):
    quarter = iota((1, HD), 1) // HEADS
    return functools.reduce(
        jnp.add, [jnp.where(quarter == i, w, 0.0) for i, w in enumerate(weights)]
    )


def mix(diagonal, line, shares):
    spread = jnp.where(diagonal, line, 0.0)
    high = spread.astype(BF16)
    low = (spread - high.astype(F32)).astype(BF16)
    return dot(high, shares) + dot(low, shares)


def merge_row_kernel(plan, near, far, back, before, share_ref, level_ref, out, prefix, lines, levels):
    diagonal = head_diagonal()
    prefix[...] = before[...]
    place_answers(plan, 0, back, prefix)
    level = [read_level(r) for r in (near, far, prefix)]
    weights, total = weights_of(level)
    line = four_lines(weights)
    for n, v in enumerate(level):
        levels[n] = v
    out[:, HEADS:, :] = level_parts(total)
    empty = jnp.zeros((HEADS, HD), BF16)

    def parts(i, fourth):
        sources = [near[i, :HEADS, :], far[i, :HEADS, :], prefix[i, :HEADS, :], fourth]
        return jnp.concatenate(sources, axis=0)

    for i in range(COLUMN):
        out[i, :HEADS, :] = mix(diagonal, line[i : i + 1], parts(i, empty)).astype(BF16)

    first = lax.axis_index("z") * HOME
    own = pl.ds(first, HOME)
    weights, total = weights_of([levels[n, own, :] for n in range(3)] + [level_ref[...]])
    line = four_lines(weights)
    rest = four_lines(weights[3:])
    out[own, HEADS:, :] = level_parts(total)
    nothing = jnp.zeros((3 * HEADS, HD), BF16)
    for j in range(HOME):
        home = share_ref[j]
        high = home.astype(BF16)
        low = jnp.concatenate([(home - high.astype(F32)).astype(BF16), nothing], axis=0)
        total = mix(diagonal, line[j : j + 1], parts(first + j, high))
        total = total + mix(diagonal, rest[j : j + 1], low)
        out[first + j, :HEADS, :] = total.astype(BF16)


def merge_kernel(in_ref, out):
    diagonal = head_diagonal()
    for y in range(NY):
        level = jnp.sum(in_ref[:, y, HEADS:, :].astype(F32), axis=1)
        weights = jnp.exp2(level - jnp.max(level, axis=0, keepdims=True))
        weights = weights / jnp.sum(weights, axis=0, keepdims=True)
        total = jnp.zeros((HEADS, HD), F32)
        for k in range(0, NZ, 4):
            line = four_lines([weights[k + i : k + i + 1] for i in range(4)])
            shares = in_ref[k : k + 4, y, :HEADS, :].reshape(4 * HEADS, HD)
            total = total + mix(diagonal, line, shares)
        out[y] = total.astype(BF16)


def kernel(
    body, name, outs, args, scalars=0, scratch=(), limit=8, us=0.5, in_specs=None, out_specs=None
):
    return pl.pallas_call(
        body,
        out_shape=outs,
        in_specs=in_specs or [SMEM] * scalars + [VMEM] * (len(args) - scalars),
        out_specs=out_specs if out_specs is not None else jax.tree.map(lambda _: VMEM, outs),
        scratch_shapes=list(scratch),
        compiler_params=pltpu.CompilerParams(vmem_limit_bytes=limit * MIB),
        cost_estimate=pl.CostEstimate(
            flops=int(us * 8e8), bytes_accessed=int(us * 1e6), transcendentals=0
        ),
        name=name,
    )(*args)


def send(array, axis, shift):
    size = {"x": NX, "z": NZ, "c": NC, "y": NY}[axis]
    return lax.ppermute(array, axis, [(i, (i + shift) % size) for i in range(size)])


def shaped(*shape, dtype=BF16):
    return jax.ShapeDtypeStruct(shape, dtype)


def local(
    queries,
    new_keys,
    new_values,
    sink_keys,
    sink_values,
    window_keys,
    window_values,
    window_len,
    root_keys,
    root_values,
    prefix_keys,
    prefix_values,
    tenant_of,
    owner,
):
    spread = jnp.broadcast_to(queries.reshape(1, NY, HEADS, HD), (NZ, NY, HEADS, HD))
    q = lax.all_to_all(
        spread.reshape(COLUMN, HEADS, HD), ("z", "y"), split_axis=0, concat_axis=0, tiled=True
    )

    k_left, v_left = send(root_keys, "x", 1), send(root_values, "x", 1)
    k_right, v_right = send(root_keys, "x", -1), send(root_values, "x", -1)
    k_far, v_far = send(k_left, "x", 1), send(v_right, "x", -1)
    (rk, rv, pk, pv), (k_left, v_left, k_right, v_right) = lax.optimization_barrier(
        (
            (root_keys, root_values, prefix_keys, prefix_values),
            (k_left, v_left, k_right, v_right),
        )
    )
    own, *others = [
        (k, send(k, "c", 1), v, send(v, "c", 1))
        for k, v in ((rk, rv), (k_left, v_left), (k_right, v_right), (k_far, v_far))
    ]
    pk1, pv1 = send(pk, "c", 1), send(pv, "c", 1)

    i32 = jnp.int32
    plan, rounds = kernel(
        prepare_kernel,
        "prepare",
        [shaped(2 * NX + 1, COLUMN + 1, dtype=i32), shaped(1, dtype=i32)],
        [tenant_of, owner, tenant_of.reshape(1, -1), owner.reshape(1, -1)],
        scalars=2,
        out_specs=[SMEM] * 2,
        us=2,
    )
    anywhere = pl.BlockSpec(memory_space=pl.ANY)
    near, home_share, home_level = kernel(
        near_kernel,
        "near",
        [
            shaped(COLUMN, ROWS, HD),
            shaped(HOME, HEADS, HD, dtype=F32),
            shaped(HOME, HD, dtype=F32),
        ],
        [
            window_len,
            q,
            *own,
            window_keys,
            window_values,
            sink_keys,
            sink_values,
            new_keys,
            new_values,
        ],
        in_specs=[SMEM] + [VMEM] * 5 + [anywhere] * 2 + [VMEM] * 4,
        scratch=[
            pltpu.VMEM((KV, 1024, 2 * HD), BF16),
            pltpu.VMEM(window_keys.shape, BF16),
            pltpu.VMEM(window_values.shape, BF16),
            pltpu.SemaphoreType.DMA((2,)),
        ],
        limit=24,
        us=4,
    )

    def scalar_kernel(body, name, outs, turn, args, **options):
        if isinstance(turn, int):
            return kernel(
                lambda plan, *refs: body(plan, turn, *refs),
                name,
                outs,
                [plan, *args],
                scalars=1,
                **options,
            )
        return kernel(body, name, outs, [plan, turn, *args], scalars=2, **options)

    def prefix_answers(turn):
        picked = scalar_kernel(
            select_kernel, "select", shaped(NX * ROOM, HEADS, HD), turn, [q]
        )
        asked = lax.all_to_all(picked, "x", split_axis=0, concat_axis=0, tiled=True)
        answer = scalar_kernel(
            prefix_kernel,
            "prefix",
            shaped(NX * ROOM, ROWS, HD),
            turn,
            [asked, pk, pk1, pv, pv1],
            scratch=[
                pltpu.VMEM((2, KV, MEMBER, GROUP, HD), BF16),
                pltpu.SMEM((2, NX * ROOM + 1), i32),
            ],
            us=2,
        )
        return lax.all_to_all(answer, "x", split_axis=0, concat_axis=0, tiled=True)

    def more(state):
        turn, before = state
        after = scalar_kernel(
            scatter_kernel,
            "scatter",
            shaped(COLUMN, ROWS, HD),
            turn,
            [prefix_answers(turn), before],
        )
        return turn + 1, after

    row = lax.broadcasted_iota(i32, (COLUMN, ROWS, HD), 1)
    none = jnp.where(row == HEADS, FLOOR, 0.0).astype(BF16)
    answers = prefix_answers(0)
    _, later = lax.while_loop(
        lambda state: state[0][0] < rounds[0], more, (jnp.ones((1,), i32), none)
    )
    far = kernel(
        far_kernel,
        "far",
        shaped(COLUMN, ROWS, HD),
        [q, *(ref for block in others for ref in block)],
        scratch=[pltpu.VMEM((KV, (NX - 1) * 1024, 2 * HD), BF16)],
        limit=32,
        us=6,
    )
    merged = kernel(
        merge_row_kernel,
        "merge_row",
        shaped(COLUMN, ROWS, HD),
        [plan, near, far, answers, later, home_share, home_level],
        scalars=1,
        scratch=[
            pltpu.VMEM((COLUMN, ROWS, HD), BF16),
            pltpu.VMEM((COLUMN, HD), F32),
            pltpu.VMEM((3, COLUMN, HD), F32),
        ],
        us=1.5,
    )
    back = lax.all_to_all(merged, ("z", "y"), split_axis=0, concat_axis=0, tiled=True)
    out = kernel(
        merge_kernel, "merge", shaped(NY, HEADS, HD), [back.reshape(NZ, NY, ROWS, HD)]
    )
    return out.reshape(1, NY * HEADS * HD)


def solution(mesh):
    fine = Mesh(mesh.devices.reshape(NX, NZ, NC, NY), ("x", "z", "c", "y"))
    session = ("x", "z", "c")
    placed = (
        P(("x", "z", "c", "y"), None),
        P(session, "y"),
        P(session, "y"),
        P(session, None, "y"),
        P(session, None, "y"),
        P(session, None, "y"),
        P(session, None, "y"),
        P(session),
        P(session, "y"),
        P(session, "y"),
        P(session, "y"),
        P(session, "y"),
        P(),
        P(),
    )
    return jax.shard_map(
        local,
        mesh=fine,
        in_specs=placed,
        out_specs=P(("x", "z", "c", "y"), None),
        check_vma=False,
    )
```

time: 741 us -> 85.3 us (0.12)
  the two profiles are of different devices: /device:TPU:8 before, /device:TPU:2 now
where the time goes in v1:
time: 85.3 us; the launch traced here: 85 us
  starting transfers between devices  32.8 us (38%)
  Pallas kernels  20.2 us (24%)
  blocking collectives  18.4 us (22%)
  waiting for transfers between devices  7.25 us (8%)
  local copies, waits for them, and re-layouts  4.59 us (5%)
  other arithmetic  1.02 us (1%)
    pallas_call x7, Pallas kernels, kernel(): pl.pallas_call(body, out_shape=outs, in_specs=in_specs or [SMEM] * scalar...  20.2 us
    all_to_all x1, blocking collectives, local(): lax.all_to_all(merged, ('z', 'y'), split_axis=0, concat_axis=0, tiled=True)  18.4 us
    ppermute x16, starting transfers between devices, send(): lax.ppermute(array, axis, [(i, (i + shift) % size) for i in range(size)])  11.1 us
    all_to_all x1, starting transfers between devices, local(): lax.all_to_all(spread.reshape(COLUMN, HEADS, HD), ('z', 'y'), split_axis=...  10.3 us
    all_to_all x1, waiting for transfers between devices, local(): lax.all_to_all(spread.reshape(COLUMN, HEADS, HD), ('z', 'y'), split_axis=...  7.2 us
    all_to_all x1, starting transfers between devices, prefix_answers(): asked = lax.all_to_all(picked, 'x', split_axis=0, concat_axis=0, tiled=True)  6.6 us
    all_to_all x1, starting transfers between devices, prefix_answers(): return lax.all_to_all(answer, 'x', split_axis=0, concat_axis=0, tiled=True)  4.81 us
    unnamed x30, local copies, waits for them, and re-layouts  3.07 us
  transfers between devices with their start and end apart: 19, of which 1 were waited for; matrix products, arithmetic and copies ran while one was open for 2% of the time, Pallas kernels for 22%

profile of v1, /device:TPU:2, one launch (start us, length us, event | category | flops | bytes accessed | tf_op | source)
XLA Modules:
  0.0 85.0 jit_solution(14714011442318256641)
XLA Ops:
  0.0 1.5 %collective-permute-start = (bf16[512,256]{1,0:T(8,128)(2,1)}, bf16[512,256]{1,0:T(8,128)(2,1)S(1)}, u32[]{:S(2)}, u32[]{:S(2)}) collective-permute-start(bf16[512,256]{1,0:T(8,128)(2,1)} %k0), channel_id=1, source_target_pairs={{0,64},{64,128},{128,192},{192,0},{1,65},{65,129},{129,193},{193,1... | collective-permute-start | bytes 786440 | tf_op jit(solution)/shard_map/ppermute | solution.py:391
  1.5 0.8 collective-permute-start.3
  2.3 1.2 %collective-permute-start.1 = (bf16[512,256]{1,0:T(8,128)(2,1)}, bf16[512,256]{1,0:T(8,128)(2,1)}, u32[]{:S(2)}, u32[]{:S(2)}) collective-permute-start(bf16[512,256]{1,0:T(8,128)(2,1)} %v0), channel_id=1, source_target_pairs={{0,64},{64,128},{128,192},{192,0},{1,65},{65,129},{129,193},{193,1... | collective-permute-start | bytes 786440 | tf_op jit(solution)/shard_map/ppermute | solution.py:391
  3.5 2.0 %collective-permute-start.2 = (bf16[512,256]{1,0:T(8,128)(2,1)}, bf16[512,256]{1,0:T(8,128)(2,1)}, u32[]{:S(2)}, u32[]{:S(2)}) collective-permute-start(bf16[512,256]{1,0:T(8,128)(2,1)} %k0), channel_id=1, source_target_pairs={{0,192},{64,0},{128,64},{192,128},{1,193},{65,1},{129,65},{193,129... | collective-permute-start | bytes 786440 | tf_op jit(solution)/shard_map/ppermute | solution.py:391
  5.5 1.0 %reduce = bf16[16384]{0:T(1024)(128)(2,1)S(1)} reduce(bf16[1,16384]{1,0:T(2,128)(2,1)} %param.16, bf16[]{:T(256)} %constant.18), dimensions={0}, to_apply=%param.16.reduce_sub_computation | reduce | bytes 65538 | tf_op args[0]
  6.5 0.7 broadcast_in_dim.16
  7.3 10.3 %all-to-all-start.2 = ((bf16[32,32,128]{2,1,0:T(8,128)(2,1)}), bf16[32,32,128]{2,1,0:T(8,128)(2,1)}, u32[]{:S(2)}, u32[]{:S(2)}) async-start(bf16[32,32,128]{2,1,0:T(8,128)(2,1)} %bitcast.3), calls=%async_computation.2 | async-start | bytes 524288 | tf_op jit(solution)/shard_map/all_to_all | solution.py:415
  18.7 0.7 copy-done.10
  19.4 2.8 %prepare.1 = (s32[9,33]{1,0:T(8,128)S(1)}, s32[1]{0:T(128)}) custom-call(s32[256]{0:T(256)S(1)} %copy-done.10, s32[64]{0:T(128)S(1)} %copy-done.11, s32[1,256]{1,0:T(1,128)S(1)} %bitcast.8, s32[1,64]{1,0:T(1,128)S(1)} %bitcast.9), custom_call_target="tpu_custom_call" | custom-call | flops 1600000000 | bytes 2000000 | tf_op jit(solution)/shard_map/prepare/pallas_call | solution.py:375
  22.4 7.2 %all-to-all-done.2.q_ref.refs_0_ = bf16[32,32,128]{2,1,0:T(8,128)(2,1)} async-done(((bf16[32,32,128]{2,1,0:T(8,128)(2,1)}), bf16[32,32,128]{2,1,0:T(8,128)(2,1)}, u32[]{:S(2)}, u32[]{:S(2)}) %all-to-all-start.2) | async-done | bytes 262176 | tf_op jit(solution)/shard_map/all_to_all | solution.py:415
  29.6 1.7 %select.2 = bf16[32,32,128]{2,1,0:T(8,128)(2,1)} custom-call(s32[9,33]{1,0:T(8,128)S(1)} %get-tuple-element.148.plan, bf16[32,32,128]{2,1,0:T(8,128)(2,1)} %all-to-all-done.2.q_ref.refs_0_), custom_call_target="tpu_custom_call" | custom-call | flops 400000000 | bytes 500000 | tf_op jit(solution)/shard_map/select/pallas_call | solution.py:375
  31.4 0.7 copy-done.4
  32.1 1.5 %collective-permute-start.10 = (bf16[512,256]{1,0:T(8,128)(2,1)S(1)}, bf16[512,256]{1,0:T(8,128)(2,1)}, u32[]{:S(2)}, u32[]{:S(2)}) collective-permute-start(bf16[512,256]{1,0:T(8,128)(2,1)S(1)} %collective-permute-done.refs_0_), channel_id=1, source_target_pairs={{0,64},{64,128},{128,192},{192,0},{1,65},{65,129},{129,193},{193,1... | collective-permute-start | bytes 786440 | tf_op jit(solution)/shard_map/ppermute | solution.py:391
  33.6 1.5 %collective-permute-start.12 = (bf16[512,256]{1,0:T(8,128)(2,1)S(1)}, bf16[512,256]{1,0:T(8,128)(2,1)}, u32[]{:S(2)}, u32[]{:S(2)}) collective-permute-start(bf16[512,256]{1,0:T(8,128)(2,1)S(1)} %collective-permute-done.3.refs_6_), channel_id=1, source_target_pairs={{0,192},{64,0},{128,64},{192,128},{1,193},{65,1},{129,65},{193,129... | collective-permute-start | bytes 786440 | tf_op jit(solution)/shard_map/ppermute | solution.py:391
  35.0 6.6 %all-to-all-start.3 = ((bf16[32,32,128]{2,1,0:T(8,128)(2,1)}), bf16[32,32,128]{2,1,0:T(8,128)(2,1)S(1)}, u32[]{:S(2)}, u32[]{:S(2)}) async-start(bf16[32,32,128]{2,1,0:T(8,128)(2,1)} %select.2), calls=%async_computation.3 | async-start | bytes 524288 | tf_op jit(solution)/shard_map/all_to_all | solution.py:491
  41.7 0.9 %copy-done.5 = bf16[512,256]{1,0:T(8,128)(2,1)S(1)} copy-done((bf16[512,256]{1,0:T(8,128)(2,1)S(1)}, bf16[512,256]{1,0:T(8,128)(2,1)}, u32[]{:S(2)}) %copy-start.5) | copy-done | bytes 262168
  42.6 3.7 %near.1 = (bf16[32,40,128]{2,1,0:T(8,128)(2,1)S(1)}, f32[4,32,128]{2,1,0:T(8,128)S(1)}, f32[4,128]{1,0:T(4,128)S(1)}) custom-call(s32[4]{0:T(128)S(1)} %copy-done.12, bf16[32,32,128]{2,1,0:T(8,128)(2,1)} %all-to-all-done.2.q_ref.refs_0_, bf16[512,256]{1,0:T(8,128)(2,1)S(1)} %copy-done.2, bf16[512,256]{1,0:T(8,128)(2,1)S(1)} %copy-done.5, ...), custom_call_target="tpu_custom_call" | custom-call | flops 3200000000 | bytes 4000000 | tf_op jit(solution)/shard_map/near/pallas_call | solution.py:375
  46.4 0.7 copy-done.13
  47.6 3.9 %prefix.2 = bf16[32,40,128]{2,1,0:T(8,128)(2,1)} custom-call(s32[9,33]{1,0:T(8,128)S(1)} %get-tuple-element.148.plan, bf16[32,32,128]{2,1,0:T(8,128)(2,1)S(1)} %all-to-all-done.3.refs_0_, bf16[1024,256]{1,0:T(8,128)(2,1)} %refs_1_, bf16[1024,256]{1,0:T(8,128)(2,1)} %collective-permute-done.14.refs_2_, bf16[1024,256]{1,0:T(8,128)(2,1)} %refs_3_, ...), custom_call_target="tpu_custom_call" | custom-call | flops 1600000000 | bytes 2000000 | tf_op jit(solution)/shard_map/prefix/pallas_call | solution.py:375
  53.1 4.8 %all-to-all-start.4 = ((bf16[32,40,128]{2,1,0:T(8,128)(2,1)}), bf16[32,40,128]{2,1,0:T(8,128)(2,1)S(1)}, u32[]{:S(2)}, u32[]{:S(2)}) async-start(bf16[32,40,128]{2,1,0:T(8,128)(2,1)} %prefix.2), calls=%async_computation.4 | async-start | bytes 655360 | tf_op jit(solution)/shard_map/all_to_all | solution.py:504
  57.9 6.4 %far.1 = bf16[32,40,128]{2,1,0:T(8,128)(2,1)S(1)} custom-call(bf16[32,32,128]{2,1,0:T(8,128)(2,1)} %all-to-all-done.2.q_ref.refs_0_, bf16[512,256]{1,0:T(8,128)(2,1)S(1)} %collective-permute-done.refs_0_, bf16[512,256]{1,0:T(8,128)(2,1)} %collective-permute-done.6.refs_1_, bf16[512,256]{1,0:T(8,128)(2,1)} %collective-permute-done.1.refs_2_, ...), custom_call_target="tpu_custom_call" | custom-call | flops 4800000000 | bytes 6000000 | tf_op jit(solution)/shard_map/far/pallas_call | solution.py:375
  64.3 1.4 %merge_row.1 = bf16[32,40,128]{2,1,0:T(8,128)(2,1)S(1)} custom-call(s32[9,33]{1,0:T(8,128)S(1)} %get-tuple-element.196, bf16[32,40,128]{2,1,0:T(8,128)(2,1)S(1)} %copy-done.14, bf16[32,40,128]{2,1,0:T(8,128)(2,1)S(1)} %far.1, bf16[32,40,128]{2,1,0:T(8,128)(2,1)S(1)} %all-to-all-done.4.back, bf16[32,40,128]{2,1,0:T(8,128)(2,1)S(1)} %get-tuple-element.77.before, ...), custom_call_target="tpu_custom_call" | custom-call | flops 1200000000 | bytes 1500000 | tf_op jit(solution)/shard_map/merge_row/pallas_call | solution.py:375
  65.7 18.4 %all_to_all.30 = bf16[32,40,128]{2,1,0:T(8,128)(2,1)S(1)} all-to-all(bf16[32,40,128]{2,1,0:T(8,128)(2,1)S(1)} %merge_row.1), channel_id=1, replica_groups=mesh['x'=4,'z'=8,'c'=2,'y'=4] {'z','y'}, dimensions={0} | all-to-all | bytes 655360 | tf_op jit(solution)/shard_map/all_to_all | solution.py:545
  84.4 0.7 reshape.22
  (58 shorter events, 3.7 us)
Async XLA Ops:
  0.0 17.6 %collective-permute-start = (bf16[512,256]{1,0:T(8,128)(2,1)}, bf16[512,256]{1,0:T(8,128)(2,1)S(1)}, u32[]{:S(2)}, u32[]{:S(2)}) collective-permute-start(bf16[512,256]{1,0:T(8,128)(2,1)} %k0), channel_id=1, source_target_pairs={{0,64},{64,128},{128,192},{192,0},{1,65},{65,129},{129,193},{193,1... | collective-permute-start | bytes 786440 | tf_op jit(solution)/shard_map/ppermute | solution.py:391
  1.5 16.1 %collective-permute-start.3 = (bf16[512,256]{1,0:T(8,128)(2,1)}, bf16[512,256]{1,0:T(8,128)(2,1)S(1)}, u32[]{:S(2)}, u32[]{:S(2)}) collective-permute-start(bf16[512,256]{1,0:T(8,128)(2,1)} %v0), channel_id=1, source_target_pairs={{0,192},{64,0},{128,64},{192,128},{1,193},{65,1},{129,65},{193,129... | collective-permute-start | bytes 786440 | tf_op jit(solution)/shard_map/ppermute | solution.py:391
  2.3 15.3 %collective-permute-start.1 = (bf16[512,256]{1,0:T(8,128)(2,1)}, bf16[512,256]{1,0:T(8,128)(2,1)}, u32[]{:S(2)}, u32[]{:S(2)}) collective-permute-start(bf16[512,256]{1,0:T(8,128)(2,1)} %v0), channel_id=1, source_target_pairs={{0,64},{64,128},{128,192},{192,0},{1,65},{65,129},{129,193},{193,1... | collective-permute-start | bytes 786440 | tf_op jit(solution)/shard_map/ppermute | solution.py:391
  3.5 14.1 %collective-permute-start.2 = (bf16[512,256]{1,0:T(8,128)(2,1)}, bf16[512,256]{1,0:T(8,128)(2,1)}, u32[]{:S(2)}, u32[]{:S(2)}) collective-permute-start(bf16[512,256]{1,0:T(8,128)(2,1)} %k0), channel_id=1, source_target_pairs={{0,192},{64,0},{128,64},{192,128},{1,193},{65,1},{129,65},{193,129... | collective-permute-start | bytes 786440 | tf_op jit(solution)/shard_map/ppermute | solution.py:391
  7.3 10.9 %copy-start.2 = (bf16[512,256]{1,0:T(8,128)(2,1)S(1)}, bf16[512,256]{1,0:T(8,128)(2,1)}, u32[]{:S(2)}) copy-start(bf16[512,256]{1,0:T(8,128)(2,1)} %k0) | copy-start | bytes 786436
  7.3 11.0 %copy-start.3 = (bf16[512,256]{1,0:T(8,128)(2,1)S(1)}, bf16[512,256]{1,0:T(8,128)(2,1)}, u32[]{:S(2)}) copy-start(bf16[512,256]{1,0:T(8,128)(2,1)} %v0) | copy-start | bytes 786436
  7.3 22.4 %all-to-all-start.2 = ((bf16[32,32,128]{2,1,0:T(8,128)(2,1)}), bf16[32,32,128]{2,1,0:T(8,128)(2,1)}, u32[]{:S(2)}, u32[]{:S(2)}) async-start(bf16[32,32,128]{2,1,0:T(8,128)(2,1)} %bitcast.3), calls=%async_computation.2 | async-start | bytes 524288 | tf_op jit(solution)/shard_map/all_to_all | solution.py:415
  17.6 29.5 %collective-permute-start.14 = (bf16[1024,256]{1,0:T(8,128)(2,1)}, bf16[1024,256]{1,0:T(8,128)(2,1)}, u32[]{:S(2)}, u32[]{:S(2)}) collective-permute-start(bf16[1024,256]{1,0:T(8,128)(2,1)} %refs_1_), channel_id=1, source_target_pairs={{0,4},{4,0},{1,5},{5,1},{2,6},{6,2},{3,7},{7,3},{8,12},{12,8},{9,1... | collective-permute-start | bytes 1572872 | tf_op jit(solution)/shard_map/ppermute | solution.py:391
  17.7 29.4 %collective-permute-start.15 = (bf16[1024,256]{1,0:T(8,128)(2,1)}, bf16[1024,256]{1,0:T(8,128)(2,1)}, u32[]{:S(2)}, u32[]{:S(2)}) collective-permute-start(bf16[1024,256]{1,0:T(8,128)(2,1)} %refs_3_), channel_id=1, source_target_pairs={{0,4},{4,0},{1,5},{5,1},{2,6},{6,2},{3,7},{7,3},{8,12},{12,8},{9,1... | collective-permute-start | bytes 1572872 | tf_op jit(solution)/shard_map/ppermute | solution.py:391
  18.2 13.2 %collective-permute-start.4 = (bf16[512,256]{1,0:T(8,128)(2,1)S(1)}, bf16[512,256]{1,0:T(8,128)(2,1)S(1)}, u32[]{:S(2)}, u32[]{:S(2)}) collective-permute-start(bf16[512,256]{1,0:T(8,128)(2,1)S(1)} %copy-done.2), channel_id=1, source_target_pairs={{0,4},{4,0},{1,5},{5,1},{2,6},{6,2},{3,7},{7,3},{8,12},{12,8},{9,1... | collective-permute-start | bytes 786440 | tf_op jit(solution)/shard_map/ppermute | solution.py:391
  18.3 15.2 %collective-permute-start.5 = (bf16[512,256]{1,0:T(8,128)(2,1)S(1)}, bf16[512,256]{1,0:T(8,128)(2,1)}, u32[]{:S(2)}, u32[]{:S(2)}) collective-permute-start(bf16[512,256]{1,0:T(8,128)(2,1)S(1)} %copy-done.3), channel_id=1, source_target_pairs={{0,4},{4,0},{1,5},{5,1},{2,6},{6,2},{3,7},{7,3},{8,12},{12,8},{9,1... | collective-permute-start | bytes 786440 | tf_op jit(solution)/shard_map/ppermute | solution.py:391
  19.4 22.2 %copy-start.1 = (bf16[4,512,256]{2,1,0:T(8,128)(2,1)S(1)}, bf16[4,512,256]{2,1,0:T(8,128)(2,1)}, u32[]{:S(2)}) copy-start(bf16[4,512,256]{2,1,0:T(8,128)(2,1)} %wv.1) | copy-start | bytes 3145732
  22.2 19.4 %copy-start = (bf16[4,512,256]{2,1,0:T(8,128)(2,1)S(1)}, bf16[4,512,256]{2,1,0:T(8,128)(2,1)}, u32[]{:S(2)}) copy-start(bf16[4,512,256]{2,1,0:T(8,128)(2,1)} %wk.1) | copy-start | bytes 3145732
  22.2 29.3 %collective-permute-start.6 = (bf16[512,256]{1,0:T(8,128)(2,1)S(1)}, bf16[512,256]{1,0:T(8,128)(2,1)}, u32[]{:S(2)}, u32[]{:S(2)}) collective-permute-start(bf16[512,256]{1,0:T(8,128)(2,1)S(1)} %collective-permute-done.refs_0_), channel_id=1, source_target_pairs={{0,4},{4,0},{1,5},{5,1},{2,6},{6,2},{3,7},{7,3},{8,12},{12,8},{9,1... | collective-permute-start | bytes 786440 | tf_op jit(solution)/shard_map/ppermute | solution.py:391
  31.4 10.3 %copy-start.12 = (s32[4]{0:T(128)S(1)}, s32[4]{0:T(128)}, u32[]{:S(2)}) copy-start(s32[4]{0:T(128)} %length_ref.1) | copy-start | bytes 52
  32.1 19.8 %collective-permute-start.10 = (bf16[512,256]{1,0:T(8,128)(2,1)S(1)}, bf16[512,256]{1,0:T(8,128)(2,1)}, u32[]{:S(2)}, u32[]{:S(2)}) collective-permute-start(bf16[512,256]{1,0:T(8,128)(2,1)S(1)} %collective-permute-done.refs_0_), channel_id=1, source_target_pairs={{0,64},{64,128},{128,192},{192,0},{1,65},{65,129},{129,193},{193,1... | collective-permute-start | bytes 786440 | tf_op jit(solution)/shard_map/ppermute | solution.py:391
  33.6 18.5 %collective-permute-start.12 = (bf16[512,256]{1,0:T(8,128)(2,1)S(1)}, bf16[512,256]{1,0:T(8,128)(2,1)}, u32[]{:S(2)}, u32[]{:S(2)}) collective-permute-start(bf16[512,256]{1,0:T(8,128)(2,1)S(1)} %collective-permute-done.3.refs_6_), channel_id=1, source_target_pairs={{0,192},{64,0},{128,64},{192,128},{1,193},{65,1},{129,65},{193,129... | collective-permute-start | bytes 786440 | tf_op jit(solution)/shard_map/ppermute | solution.py:391
  35.0 12.6 %all-to-all-start.3 = ((bf16[32,32,128]{2,1,0:T(8,128)(2,1)}), bf16[32,32,128]{2,1,0:T(8,128)(2,1)S(1)}, u32[]{:S(2)}, u32[]{:S(2)}) async-start(bf16[32,32,128]{2,1,0:T(8,128)(2,1)} %select.2), calls=%async_computation.3 | async-start | bytes 524288 | tf_op jit(solution)/shard_map/all_to_all | solution.py:491
  47.1 10.8 %collective-permute-start.7 = (bf16[512,256]{1,0:T(8,128)(2,1)}, bf16[512,256]{1,0:T(8,128)(2,1)S(1)}, u32[]{:S(2)}, u32[]{:S(2)}) collective-permute-start(bf16[512,256]{1,0:T(8,128)(2,1)} %collective-permute-done.1.refs_2_), channel_id=1, source_target_pairs={{0,4},{4,0},{1,5},{5,1},{2,6},{6,2},{3,7},{7,3},{8,12},{12,8},{9,1... | collective-permute-start | bytes 786440 | tf_op jit(solution)/shard_map/ppermute | solution.py:391
  47.1 10.7 %collective-permute-start.8 = (bf16[512,256]{1,0:T(8,128)(2,1)}, bf16[512,256]{1,0:T(8,128)(2,1)S(1)}, u32[]{:S(2)}, u32[]{:S(2)}) collective-permute-start(bf16[512,256]{1,0:T(8,128)(2,1)} %collective-permute-done.2.refs_4_), channel_id=1, source_target_pairs={{0,4},{4,0},{1,5},{5,1},{2,6},{6,2},{3,7},{7,3},{8,12},{12,8},{9,1... | collective-permute-start | bytes 786440 | tf_op jit(solution)/shard_map/ppermute | solution.py:391
  51.6 6.3 %collective-permute-start.9 = (bf16[512,256]{1,0:T(8,128)(2,1)S(1)}, bf16[512,256]{1,0:T(8,128)(2,1)S(1)}, u32[]{:S(2)}, u32[]{:S(2)}) collective-permute-start(bf16[512,256]{1,0:T(8,128)(2,1)S(1)} %collective-permute-done.3.refs_6_), channel_id=1, source_target_pairs={{0,4},{4,0},{1,5},{5,1},{2,6},{6,2},{3,7},{7,3},{8,12},{12,8},{9,1... | collective-permute-start | bytes 786440 | tf_op jit(solution)/shard_map/ppermute | solution.py:391
  51.9 6.0 %collective-permute-start.11 = (bf16[512,256]{1,0:T(8,128)(2,1)}, bf16[512,256]{1,0:T(8,128)(2,1)S(1)}, u32[]{:S(2)}, u32[]{:S(2)}) collective-permute-start(bf16[512,256]{1,0:T(8,128)(2,1)} %collective-permute-done.10.refs_8_), channel_id=1, source_target_pairs={{0,4},{4,0},{1,5},{5,1},{2,6},{6,2},{3,7},{7,3},{8,12},{12,8},{9,1... | collective-permute-start | bytes 786440 | tf_op jit(solution)/shard_map/ppermute | solution.py:391
  52.1 5.8 %collective-permute-start.13 = (bf16[512,256]{1,0:T(8,128)(2,1)}, bf16[512,256]{1,0:T(8,128)(2,1)S(1)}, u32[]{:S(2)}, u32[]{:S(2)}) collective-permute-start(bf16[512,256]{1,0:T(8,128)(2,1)} %collective-permute-done.12.refs_10_), channel_id=1, source_target_pairs={{0,4},{4,0},{1,5},{5,1},{2,6},{6,2},{3,7},{7,3},{8,12},{12,8},{9,1... | collective-permute-start | bytes 786440 | tf_op jit(solution)/shard_map/ppermute | solution.py:391
  53.1 11.2 %all-to-all-start.4 = ((bf16[32,40,128]{2,1,0:T(8,128)(2,1)}), bf16[32,40,128]{2,1,0:T(8,128)(2,1)S(1)}, u32[]{:S(2)}, u32[]{:S(2)}) async-start(bf16[32,40,128]{2,1,0:T(8,128)(2,1)} %prefix.2), calls=%async_computation.4 | async-start | bytes 655360 | tf_op jit(solution)/shard_map/all_to_all | solution.py:504
  (10 other events, 51.4 us)

commit v2 on v1

--- a/solution.py
+++ b/solution.py
@@ -120,23 +120,27 @@
     rounds[0] = (fullest.astype(jnp.int32) + ROOM - 1) >> 3
 
 
-def root_part(q_ref, blocks, values, out):
-    for g in range(KV):
-        for n, (_, _, v0, v1) in enumerate(blocks):
-            for i, v in enumerate((v0, v1)):
-                rows = slice(n * 1024 + i * 512, n * 1024 + (i + 1) * 512)
-                values[g, rows, :HD] = v[:, g * HD : (g + 1) * HD]
-                values[g, rows, HD:] = jnp.ones((512, HD), BF16)
+def root_part(q_ref, blocks, ready, values, out):
     diagonal = head_diagonal()
     rows = COLUMN // 2
+
+    def score(h, g, block):
+        query = q_ref[h * rows : (h + 1) * rows, g * GROUP : (g + 1) * GROUP, :]
+        return scores_of(query.reshape(rows * GROUP, HD), block[:512, g * HD : (g + 1) * HD])
+
+    first = []
+    for n, block in enumerate(blocks):
+        ready(n)
+        first.append(score(0, 0, block))
+        for g in range(KV):
+            values[g, n * 512 : (n + 1) * 512, :HD] = block[512:, g * HD : (g + 1) * HD]
+            values[g, n * 512 : (n + 1) * 512, HD:] = jnp.ones((512, HD), BF16)
     for h in range(2):
         chats = slice(h * rows, (h + 1) * rows)
         line = None
         for g in range(KV):
             heads = slice(g * GROUP, (g + 1) * GROUP)
-            lanes = slice(g * HD, (g + 1) * HD)
-            query = q_ref[chats, heads, :].reshape(rows * GROUP, HD)
-            scores = [scores_of(query, k[:, lanes]) for block in blocks for k in block[:2]]
+            scores = first if h + g == 0 else [score(h, g, block) for block in blocks]
             peak = functools.reduce(
                 jnp.maximum, [jnp.max(s, axis=1, keepdims=True) for s in scores]
             )
@@ -152,6 +156,16 @@
             part = jnp.sum(jnp.where(diagonal[None, heads], level, 0.0), axis=1)
             line = part if line is None else line + part
         out[chats, HEADS:, :] = level_parts(line)
+
+
+def fetch(sources, targets, sems):
+    copies = [
+        pltpu.make_async_copy(source, target, sems.at[n])
+        for n, (source, target) in enumerate(zip(sources, targets))
+    ]
+    for copy in copies:
+        copy.start()
+    return copies
 
 
 def home_part(length_ref, q_ref, wk, wv, sk, sv, nk, nv, share_ref, level_ref):
@@ -197,34 +211,57 @@
 
 
 def near_kernel(
-    length_ref, q_ref, k0, k1, v0, v1, wk, wv, sk, sv, nk, nv, out, share, level, values, wks, wvs, sems
+    length_ref, q_hbm, own, other, wk, wv, sk, sv, nk, nv, out_hbm, share_hbm, level, *scratch
 ):
-    copies = [
-        pltpu.make_async_copy(wk, wks, sems.at[0]),
-        pltpu.make_async_copy(wv, wvs, sems.at[1]),
-    ]
-    for copy in copies:
-        copy.start()
-    root_part(q_ref, [(k0, k1, v0, v1)], values, out)
+    q_ref, blocks, values, wks, wvs, out, share, sems = scratch
+    copies = fetch(
+        (q_hbm, own, other, wk, wv), (q_ref, blocks.at[0], blocks.at[1], wks, wvs), sems
+    )
+    copies[0].wait()
+    root_part(
+        q_ref, [blocks.at[n] for n in range(2)], lambda n: copies[n + 1].wait(), values, out
+    )
+    leave = [pltpu.make_async_copy(out, out_hbm, sems.at[5])]
+    leave[0].start()
+    copies[3].wait()
+    copies[4].wait()
+    home_part(length_ref, q_ref, wks, wvs, sk, sv, nk, nv, share, level)
+    leave.append(pltpu.make_async_copy(share, share_hbm, sems.at[6]))
+    leave[1].start()
+    for copy in leave:
+        copy.wait()
+
+
+def far_kernel(q_hbm, *refs):
+    *sources, out, q_ref, blocks, values, sems = refs
+    targets = [blocks.at[n] for n in range(4)]
+    targets += [blocks.at[n, pl.ds(i * 512, 512)] for n in (4, 5) for i in range(2)]
+    copies = fetch((q_hbm, *sources), (q_ref, *targets), sems)
+    copies[0].wait()
+
+    def ready(n):
+        for i in (n + 1,) if n < 4 else (2 * n - 3, 2 * n - 2):
+            copies[i].wait()
+
+    root_part(q_ref, [blocks.at[n] for n in range(6)], ready, values, out)
+
+
+def select_kernel(plan, turn, q_hbm, out, sems):
+    start = turn if isinstance(turn, int) else turn[0] * ROOM
+    chats = [plan[t, start + e] for t in range(NX) for e in range(ROOM)]
+    copies = fetch(
+        [q_hbm.at[chat] for chat in chats], [out.at[n] for n in range(NX * ROOM)], sems
+    )
     for copy in copies:
         copy.wait()
-    home_part(length_ref, q_ref, wks, wvs, sk, sv, nk, nv, share, level)
-
-
-def far_kernel(q_ref, *refs):
-    out, values = refs[-2:]
-    root_part(q_ref, [refs[4 * n : 4 * n + 4] for n in range(NX - 1)], values, out)
-
-
-def select_kernel(plan, turn, q_ref, out):
+
+
+def prefix_kernel(plan, turn, q_hbm, pk0, pk1, pv0, pv1, out, q_ref, prefixes, qs, lists, sems):
     start = turn if isinstance(turn, int) else turn[0] * ROOM
-    chats = [plan[t, start + e] for t in range(NX) for e in range(ROOM)]
-    for n, chat in enumerate(chats):
-        out[n] = q_ref[chat]
-
-
-def prefix_kernel(plan, turn, q_ref, pk0, pk1, pv0, pv1, out, qs, lists):
-    start = turn if isinstance(turn, int) else turn[0] * ROOM
+    copies = fetch(
+        (q_hbm, pk0, pk1, pv0, pv1), (q_ref, *(prefixes.at[n] for n in range(4))), sems
+    )
+    pk0, pk1, pv0, pv1 = (prefixes.at[n] for n in range(4))
     diagonal = head_diagonal()
     zero = jnp.int32(0)
     lists[0, 0] = zero
@@ -241,6 +278,8 @@
         left = jnp.clip(plan[2 * NX, NX + s] - start, 0, ROOM)
         n0, n1 = lax.fori_loop(0, left, scan, (n0, n1))
     slots = ((pk0, pv0, n0), (pk1, pv1, n1))
+    for copy in copies:
+        copy.wait()
 
     def step(b, _):
         results = []
@@ -416,22 +455,15 @@
         spread.reshape(COLUMN, HEADS, HD), ("z", "y"), split_axis=0, concat_axis=0, tiled=True
     )
 
-    k_left, v_left = send(root_keys, "x", 1), send(root_values, "x", 1)
-    k_right, v_right = send(root_keys, "x", -1), send(root_values, "x", -1)
-    k_far, v_far = send(k_left, "x", 1), send(v_right, "x", -1)
-    (rk, rv, pk, pv), (k_left, v_left, k_right, v_right) = lax.optimization_barrier(
-        (
-            (root_keys, root_values, prefix_keys, prefix_values),
-            (k_left, v_left, k_right, v_right),
-        )
-    )
-    own, *others = [
-        (k, send(k, "c", 1), v, send(v, "c", 1))
-        for k, v in ((rk, rv), (k_left, v_left), (k_right, v_right), (k_far, v_far))
-    ]
-    pk1, pv1 = send(pk, "c", 1), send(pv, "c", 1)
+    root = jnp.concatenate([root_keys, root_values], axis=0)
+    left, right = send(root, "x", 1), send(root, "x", -1)
+    root1, pk1, pv1 = (send(a, "c", 1) for a in (root, prefix_keys, prefix_values))
+    left, right, root1, tenant_of = lax.optimization_barrier((left, right, root1, tenant_of))
+    far = [send(left[:512], "x", 1), send(right[512:], "x", -1)]
+    left1, right1 = send(left, "c", 1), send(right, "c", 1)
 
     i32 = jnp.int32
+    tenant_of, owner, _ = lax.optimization_barrier((tenant_of, owner, spread))
     plan, rounds = kernel(
         prepare_kernel,
         "prepare",
@@ -441,7 +473,7 @@
         out_specs=[SMEM] * 2,
         us=2,
     )
-    anywhere = pl.BlockSpec(memory_space=pl.ANY)
+    anywhere = pl.BlockSpec(memory_space=pltpu.HBM)
     near, home_share, home_level = kernel(
         near_kernel,
         "near",
@@ -453,7 +485,8 @@
         [
             window_len,
             q,
-            *own,
+            root,
+            root1,
             window_keys,
             window_values,
             sink_keys,
@@ -461,44 +494,58 @@
             new_keys,
             new_values,
         ],
-        in_specs=[SMEM] + [VMEM] * 5 + [anywhere] * 2 + [VMEM] * 4,
+        in_specs=[SMEM] + [anywhere] * 5 + [VMEM] * 4,
+        out_specs=[anywhere, anywhere, VMEM],
         scratch=[
+            pltpu.VMEM((COLUMN, HEADS, HD), BF16),
+            pltpu.VMEM((2, 1024, KV * HD), BF16),
             pltpu.VMEM((KV, 1024, 2 * HD), BF16),
             pltpu.VMEM(window_keys.shape, BF16),
             pltpu.VMEM(window_values.shape, BF16),
-            pltpu.SemaphoreType.DMA((2,)),
+            pltpu.VMEM((COLUMN, ROWS, HD), BF16),
+            pltpu.VMEM((HOME, HEADS, HD), F32),
+            pltpu.SemaphoreType.DMA((7,)),
         ],
-        limit=24,
+        limit=16,
         us=4,
     )
 
-    def scalar_kernel(body, name, outs, turn, args, **options):
+    def scalar_kernel(body, name, outs, turn, args, rest=anywhere, **options):
         if isinstance(turn, int):
-            return kernel(
-                lambda plan, *refs: body(plan, turn, *refs),
-                name,
-                outs,
-                [plan, *args],
-                scalars=1,
-                **options,
-            )
-        return kernel(body, name, outs, [plan, turn, *args], scalars=2, **options)
-
-    def prefix_answers(turn):
+            whole, args = (lambda plan, *refs: body(plan, turn, *refs)), [plan, *args]
+            scalars = 1
+        else:
+            whole, args, scalars = body, [plan, turn, *args], 2
+        specs = [SMEM] * scalars + [rest] * (len(args) - scalars)
+        return kernel(whole, name, outs, args, in_specs=specs, **options)
+
+    def prefix_asked(turn):
         picked = scalar_kernel(
-            select_kernel, "select", shaped(NX * ROOM, HEADS, HD), turn, [q]
+            select_kernel,
+            "select",
+            shaped(NX * ROOM, HEADS, HD),
+            turn,
+            [q],
+            out_specs=anywhere,
+            scratch=[pltpu.SemaphoreType.DMA((NX * ROOM,))],
         )
-        asked = lax.all_to_all(picked, "x", split_axis=0, concat_axis=0, tiled=True)
+        return lax.all_to_all(picked, "x", split_axis=0, concat_axis=0, tiled=True)
+
+    def prefix_answers(turn, asked):
         answer = scalar_kernel(
             prefix_kernel,
             "prefix",
             shaped(NX * ROOM, ROWS, HD),
             turn,
-            [asked, pk, pk1, pv, pv1],
+            [asked, prefix_keys, pk1, prefix_values, pv1],
             scratch=[
+                pltpu.VMEM((NX * ROOM, HEADS, HD), BF16),
+                pltpu.VMEM((4, *prefix_keys.shape), BF16),
                 pltpu.VMEM((2, KV, MEMBER, GROUP, HD), BF16),
                 pltpu.SMEM((2, NX * ROOM + 1), i32),
+                pltpu.SemaphoreType.DMA((5,)),
             ],
+            limit=12,
             us=2,
         )
         return lax.all_to_all(answer, "x", split_axis=0, concat_axis=0, tiled=True)
@@ -510,30 +557,39 @@
             "scatter",
             shaped(COLUMN, ROWS, HD),
             turn,
-            [prefix_answers(turn), before],
+            [prefix_answers(turn, prefix_asked(turn)), before],
+            rest=VMEM,
         )
         return turn + 1, after
 
     row = lax.broadcasted_iota(i32, (COLUMN, ROWS, HD), 1)
     none = jnp.where(row == HEADS, FLOOR, 0.0).astype(BF16)
-    answers = prefix_answers(0)
+    asked = prefix_asked(0)
+    others = [left, left1, right, right1, *far, *(send(f, "c", 1) for f in far)]
+    answers = prefix_answers(0, asked)
     _, later = lax.while_loop(
         lambda state: state[0][0] < rounds[0], more, (jnp.ones((1,), i32), none)
     )
-    far = kernel(
+    rest = kernel(
         far_kernel,
         "far",
         shaped(COLUMN, ROWS, HD),
-        [q, *(ref for block in others for ref in block)],
-        scratch=[pltpu.VMEM((KV, (NX - 1) * 1024, 2 * HD), BF16)],
-        limit=32,
+        [q, *others],
+        in_specs=[anywhere] * 9,
+        scratch=[
+            pltpu.VMEM((COLUMN, HEADS, HD), BF16),
+            pltpu.VMEM((6, 1024, KV * HD), BF16),
+            pltpu.VMEM((KV, 6 * 512, 2 * HD), BF16),
+            pltpu.SemaphoreType.DMA((9,)),
+        ],
+        limit=24,
         us=6,
     )
     merged = kernel(
         merge_row_kernel,
         "merge_row",
         shaped(COLUMN, ROWS, HD),
-        [plan, near, far, answers, later, home_share, home_level],
+        [plan, near, rest, answers, later, home_share, home_level],
         scalars=1,
         scratch=[
             pltpu.VMEM((COLUMN, ROWS, HD), BF16),

time: 85.3 us -> 92.8 us (1.088)
  Pallas kernels: 20.2 us -> 30.5 us
  starting transfers between devices: 32.8 us -> 27.6 us
  local copies, waits for them, and re-layouts: 4.59 us -> 8.33 us
  waiting for transfers between devices: 7.25 us -> 5.81 us
    pallas_call x7, Pallas kernels: 20.2 us -> 30.5 us  [kernel(): pl.pallas_call(body, out_shape=outs, in_specs=in_specs or [SMEM] * scalar...]
    ppermute x16 -> x11, starting transfers between devices: 11.1 us -> 6.25 us  [send(): lax.ppermute(array, axis, [(i, (i + shift) % size) for i in range(size)])]
    unnamed x30 -> x37, local copies, waits for them, and re-layouts: 3.07 us -> 5.37 us
    all_to_all x1, waiting for transfers between devices: 7.2 us -> 5.77 us  [local(): lax.all_to_all(spread.reshape(COLUMN, HEADS, HD), ('z', 'y'), split_axis=...]
    slice x0 -> x2, local copies, waits for them, and re-layouts: none -> 1.42 us  [local(): far = [send(left[:512], 'x', 1), send(right[512:], 'x', -1)]]
    all_to_all x1, starting transfers between devices: 6.6 us -> 5.26 us  [prefix_asked(): return lax.all_to_all(picked, 'x', split_axis=0, concat_axis=0, tiled=True)]
    all_to_all x1, starting transfers between devices: 10.3 us -> 11.3 us  [local(): lax.all_to_all(spread.reshape(COLUMN, HEADS, HD), ('z', 'y'), split_axis=...]
  transfers between devices with their start and end apart: 19 -> 14, of which waited for: 1 -> 1; matrix products, arithmetic and copies ran while one was open for 2% -> 3% of each run, Pallas kernels for 22% -> 31%
where the time goes in v2:
time: 92.8 us; the launch traced here: 92.2 us
  Pallas kernels  30.5 us (33%)
  starting transfers between devices  27.6 us (30%)
  blocking collectives  18.8 us (20%)
  local copies, waits for them, and re-layouts  8.33 us (9%)
  waiting for transfers between devices  5.81 us (6%)
    pallas_call x7, Pallas kernels, kernel(): pl.pallas_call(body, out_shape=outs, in_specs=in_specs or [SMEM] * scalar...  30.5 us
    all_to_all x1, blocking collectives, local(): lax.all_to_all(merged, ('z', 'y'), split_axis=0, concat_axis=0, tiled=True)  18.8 us
    all_to_all x1, starting transfers between devices, local(): lax.all_to_all(spread.reshape(COLUMN, HEADS, HD), ('z', 'y'), split_axis=...  11.3 us
    ppermute x11, starting transfers between devices, send(): lax.ppermute(array, axis, [(i, (i + shift) % size) for i in range(size)])  6.25 us
    all_to_all x1, waiting for transfers between devices, local(): lax.all_to_all(spread.reshape(COLUMN, HEADS, HD), ('z', 'y'), split_axis=...  5.77 us
    unnamed x37, local copies, waits for them, and re-layouts  5.37 us
    all_to_all x1, starting transfers between devices, prefix_asked(): return lax.all_to_all(picked, 'x', split_axis=0, concat_axis=0, tiled=True)  5.26 us
    all_to_all x1, starting transfers between devices, prefix_answers(): return lax.all_to_all(answer, 'x', split_axis=0, concat_axis=0, tiled=True)  4.79 us
  transfers between devices with their start and end apart: 14, of which 1 were waited for; matrix products, arithmetic and copies ran while one was open for 3% of the time, Pallas kernels for 31%

profile of v2, /device:TPU:2, one launch (start us, length us, event | category | flops | bytes accessed | tf_op | source)
XLA Modules:
  0.0 92.2 jit_solution(6849543696364298169)
XLA Ops:
  0.0 1.0 %constant_dynamic-update-slice_fusion.1 = bf16[1024,256]{1,0:T(8,128)(2,1)S(1)} fusion(bf16[512,256]{1,0:T(8,128)(2,1)} %param.24), kind=kLoop, calls=%fused_computation.1 | loop fusion | bytes 524288
  1.1 1.6 %collective-permute-start = (bf16[1024,256]{1,0:T(8,128)(2,1)S(1)}, bf16[1024,256]{1,0:T(8,128)(2,1)S(1)}, u32[]{:S(2)}, u32[]{:S(2)}) collective-permute-start(bf16[1024,256]{1,0:T(8,128)(2,1)S(1)} %constant_dynamic-update-slice_fusion.own), channel_id=1, source_target_pairs={{0,64},{64,128},{128,192},{192,0},{1,65},{65,129},{129,193},{193,1... | collective-permute-start | bytes 1572872 | tf_op jit(solution)/shard_map/ppermute | solution.py:430
  2.6 0.9 collective-permute-start.1
  3.7 0.7 broadcast_in_dim.16
  4.4 11.3 %all-to-all-start.2 = ((bf16[32,32,128]{2,1,0:T(8,128)(2,1)}), bf16[32,32,128]{2,1,0:T(8,128)(2,1)}, u32[]{:S(2)}, u32[]{:S(2)}) async-start(bf16[32,32,128]{2,1,0:T(8,128)(2,1)} %bitcast.3), calls=%async_computation.2 | async-start | bytes 524288 | tf_op jit(solution)/shard_map/all_to_all | solution.py:454
  16.7 0.7 slice.6
  17.4 1.5 %collective-permute-start.5 = (bf16[512,256]{1,0:T(8,128)(2,1)}, bf16[512,256]{1,0:T(8,128)(2,1)S(1)}, u32[]{:S(2)}, u32[]{:S(2)}) collective-permute-start(bf16[512,256]{1,0:T(8,128)(2,1)} %slice.6), channel_id=1, source_target_pairs={{0,64},{64,128},{128,192},{192,0},{1,65},{65,129},{129,193},{193,1... | collective-permute-start | bytes 786440 | tf_op jit(solution)/shard_map/ppermute | solution.py:430
  18.9 0.7 slice.7
  20.1 0.7 copy-done.8
  20.8 2.8 %prepare.1 = (s32[9,33]{1,0:T(8,128)S(1)}, s32[1]{0:T(128)}) custom-call(s32[256]{0:T(256)S(1)} %copy-done.8, s32[64]{0:T(128)S(1)} %copy-done.9, s32[1,256]{1,0:T(1,128)S(1)} %bitcast.8, s32[1,64]{1,0:T(1,128)S(1)} %bitcast.9), custom_call_target="tpu_custom_call" | custom-call | flops 1600000000 | bytes 2000000 | tf_op jit(solution)/shard_map/prepare/pallas_call | solution.py:414
  23.6 5.8 %all-to-all-done.2.q_hbm.refs_0_ = bf16[32,32,128]{2,1,0:T(8,128)(2,1)} async-done(((bf16[32,32,128]{2,1,0:T(8,128)(2,1)}), bf16[32,32,128]{2,1,0:T(8,128)(2,1)}, u32[]{:S(2)}, u32[]{:S(2)}) %all-to-all-start.2) | async-done | bytes 262176 | tf_op jit(solution)/shard_map/all_to_all | solution.py:454
  29.4 10.0 %select.2 = bf16[32,32,128]{2,1,0:T(8,128)(2,1)} custom-call(s32[9,33]{1,0:T(8,128)S(1)} %get-tuple-element.144.plan, bf16[32,32,128]{2,1,0:T(8,128)(2,1)} %all-to-all-done.2.q_hbm.refs_0_), custom_call_target="tpu_custom_call" | custom-call | flops 400000000 | bytes 500000 | tf_op jit(solution)/shard_map/select/pallas_call | solution.py:414
  39.5 5.3 %all-to-all-start.3 = ((bf16[32,32,128]{2,1,0:T(8,128)(2,1)}), bf16[32,32,128]{2,1,0:T(8,128)(2,1)S(1)}, u32[]{:S(2)}, u32[]{:S(2)}) async-start(bf16[32,32,128]{2,1,0:T(8,128)(2,1)} %select.2), calls=%async_computation.3 | async-start | bytes 524288 | tf_op jit(solution)/shard_map/all_to_all | solution.py:532
  44.8 1.2 %copy-done.1 = bf16[4,512,256]{2,1,0:T(8,128)(2,1)S(1)} copy-done((bf16[4,512,256]{2,1,0:T(8,128)(2,1)S(1)}, bf16[4,512,256]{2,1,0:T(8,128)(2,1)}, u32[]{:S(2)}) %copy-start.1) | copy-done | bytes 1048600
  46.0 1.0 %copy-done.3 = bf16[1024,256]{1,0:T(8,128)(2,1)S(1)} copy-done((bf16[1024,256]{1,0:T(8,128)(2,1)S(1)}, bf16[1024,256]{1,0:T(8,128)(2,1)}, u32[]{:S(2)}) %copy-start.3) | copy-done | bytes 524312
  47.1 4.4 %near.1 = (bf16[32,40,128]{2,1,0:T(8,128)(2,1)S(1)}, f32[4,32,128]{2,1,0:T(8,128)S(1)}, f32[4,128]{1,0:T(4,128)S(1)}) custom-call(s32[4]{0:T(128)S(1)} %copy-done.10, bf16[32,32,128]{2,1,0:T(8,128)(2,1)} %all-to-all-done.2.q_hbm.refs_0_, bf16[1024,256]{1,0:T(8,128)(2,1)S(1)} %constant_dynamic-update-slice_fusion.own, bf16[1024,256]{1,0:T(8,128)(2,1)S(1)} %copy-done.3, ...), custom_call_target="tpu_custom_call" | custom-call | flops 3200000000 | bytes 4000000 | tf_op jit(solution)/shard_map/near/pallas_call | solution.py:414
  52.1 4.5 %prefix.2 = bf16[32,40,128]{2,1,0:T(8,128)(2,1)} custom-call(s32[9,33]{1,0:T(8,128)S(1)} %get-tuple-element.144.plan, bf16[32,32,128]{2,1,0:T(8,128)(2,1)S(1)} %all-to-all-done.3.refs_0_, bf16[1024,256]{1,0:T(8,128)(2,1)} %refs_1_.1, bf16[1024,256]{1,0:T(8,128)(2,1)} %collective-permute-done.9.refs_2_, bf16[1024,256]{1,0:T(8,128)(2,1)} %refs_3_.1, ...), custom_call_target="tpu_custom_call" | custom-call | flops 1600000000 | bytes 2000000 | tf_op jit(solution)/shard_map/prefix/pallas_call | solution.py:414
  57.7 0.7 while.10
  58.4 0.7 copy-done.15
  59.1 4.8 %all-to-all-start.4 = ((bf16[32,40,128]{2,1,0:T(8,128)(2,1)}), bf16[32,40,128]{2,1,0:T(8,128)(2,1)S(1)}, u32[]{:S(2)}, u32[]{:S(2)}) async-start(bf16[32,40,128]{2,1,0:T(8,128)(2,1)} %prefix.2), calls=%async_computation.4 | async-start | bytes 655360 | tf_op jit(solution)/shard_map/all_to_all | solution.py:551
  64.0 6.7 %far.1 = bf16[32,40,128]{2,1,0:T(8,128)(2,1)S(1)} custom-call(bf16[32,32,128]{2,1,0:T(8,128)(2,1)} %all-to-all-done.2.q_hbm.refs_0_, bf16[1024,256]{1,0:T(8,128)(2,1)S(1)} %collective-permute-done.refs_0_, bf16[1024,256]{1,0:T(8,128)(2,1)} %collective-permute-done.3.refs_1_, bf16[1024,256]{1,0:T(8,128)(2,1)S(1)} %collective-permute-done.1.refs_2_, ...), custom_call_target="tpu_custom_call" | custom-call | flops 4800000000 | bytes 6000000 | tf_op jit(solution)/shard_map/far/pallas_call | solution.py:414
  70.7 1.7 %merge_row.1 = bf16[32,40,128]{2,1,0:T(8,128)(2,1)S(1)} custom-call(s32[9,33]{1,0:T(8,128)S(1)} %get-tuple-element.187, bf16[32,40,128]{2,1,0:T(8,128)(2,1)S(1)} %copy-done.12, bf16[32,40,128]{2,1,0:T(8,128)(2,1)S(1)} %far.1, bf16[32,40,128]{2,1,0:T(8,128)(2,1)S(1)} %all-to-all-done.4.back, bf16[32,40,128]{2,1,0:T(8,128)(2,1)} %copy-done.15, ...), custom_call_target="tpu_custom_call" | custom-call | flops 1200000000 | bytes 1500000 | tf_op jit(solution)/shard_map/merge_row/pallas_call | solution.py:414
  72.5 18.8 %all_to_all.30 = bf16[32,40,128]{2,1,0:T(8,128)(2,1)S(1)} all-to-all(bf16[32,40,128]{2,1,0:T(8,128)(2,1)S(1)} %merge_row.1), channel_id=1, replica_groups=mesh['x'=4,'z'=8,'c'=2,'y'=4] {'z','y'}, dimensions={0} | all-to-all | bytes 655360 | tf_op jit(solution)/shard_map/all_to_all | solution.py:601
  91.5 0.7 reshape.22
  (58 shorter events, 3.7 us)
Async XLA Ops:
  1.1 15.3 %collective-permute-start = (bf16[1024,256]{1,0:T(8,128)(2,1)S(1)}, bf16[1024,256]{1,0:T(8,128)(2,1)S(1)}, u32[]{:S(2)}, u32[]{:S(2)}) collective-permute-start(bf16[1024,256]{1,0:T(8,128)(2,1)S(1)} %constant_dynamic-update-slice_fusion.own), channel_id=1, source_target_pairs={{0,64},{64,128},{128,192},{192,0},{1,65},{65,129},{129,193},{193,1... | collective-permute-start | bytes 1572872 | tf_op jit(solution)/shard_map/ppermute | solution.py:430
  2.6 13.7 %collective-permute-start.1 = (bf16[1024,256]{1,0:T(8,128)(2,1)S(1)}, bf16[1024,256]{1,0:T(8,128)(2,1)S(1)}, u32[]{:S(2)}, u32[]{:S(2)}) collective-permute-start(bf16[1024,256]{1,0:T(8,128)(2,1)S(1)} %constant_dynamic-update-slice_fusion.own), channel_id=1, source_target_pairs={{0,192},{64,0},{128,64},{192,128},{1,193},{65,1},{129,65},{193,129... | collective-permute-start | bytes 1572872 | tf_op jit(solution)/shard_map/ppermute | solution.py:430
  3.5 12.8 %collective-permute-start.2 = (bf16[1024,256]{1,0:T(8,128)(2,1)S(1)}, bf16[1024,256]{1,0:T(8,128)(2,1)S(1)}, u32[]{:S(2)}, u32[]{:S(2)}) collective-permute-start(bf16[1024,256]{1,0:T(8,128)(2,1)S(1)} %constant_dynamic-update-slice_fusion.own), channel_id=1, source_target_pairs={{0,4},{4,0},{1,5},{5,1},{2,6},{6,2},{3,7},{7,3},{8,12},{12,8},{9,1... | collective-permute-start | bytes 1572872 | tf_op jit(solution)/shard_map/ppermute | solution.py:430
  4.4 25.0 %all-to-all-start.2 = ((bf16[32,32,128]{2,1,0:T(8,128)(2,1)}), bf16[32,32,128]{2,1,0:T(8,128)(2,1)}, u32[]{:S(2)}, u32[]{:S(2)}) async-start(bf16[32,32,128]{2,1,0:T(8,128)(2,1)} %bitcast.3), calls=%async_computation.2 | async-start | bytes 524288 | tf_op jit(solution)/shard_map/all_to_all | solution.py:454
  15.7 36.4 %collective-permute-start.9 = (bf16[1024,256]{1,0:T(8,128)(2,1)}, bf16[1024,256]{1,0:T(8,128)(2,1)}, u32[]{:S(2)}, u32[]{:S(2)}) collective-permute-start(bf16[1024,256]{1,0:T(8,128)(2,1)} %refs_1_.1), channel_id=1, source_target_pairs={{0,4},{4,0},{1,5},{5,1},{2,6},{6,2},{3,7},{7,3},{8,12},{12,8},{9,1... | collective-permute-start | bytes 1572872 | tf_op jit(solution)/shard_map/ppermute | solution.py:430
  16.0 36.1 %collective-permute-start.10 = (bf16[1024,256]{1,0:T(8,128)(2,1)}, bf16[1024,256]{1,0:T(8,128)(2,1)}, u32[]{:S(2)}, u32[]{:S(2)}) collective-permute-start(bf16[1024,256]{1,0:T(8,128)(2,1)} %refs_3_.1), channel_id=1, source_target_pairs={{0,4},{4,0},{1,5},{5,1},{2,6},{6,2},{3,7},{7,3},{8,12},{12,8},{9,1... | collective-permute-start | bytes 1572872 | tf_op jit(solution)/shard_map/ppermute | solution.py:430
  16.3 3.8 %copy-start.2 = (bf16[1024,256]{1,0:T(8,128)(2,1)}, bf16[1024,256]{1,0:T(8,128)(2,1)S(1)}, u32[]{:S(2)}) copy-start(bf16[1024,256]{1,0:T(8,128)(2,1)S(1)} %collective-permute-done.2.other) | copy-start | bytes 1572868
  16.4 47.6 %collective-permute-start.3 = (bf16[1024,256]{1,0:T(8,128)(2,1)S(1)}, bf16[1024,256]{1,0:T(8,128)(2,1)}, u32[]{:S(2)}, u32[]{:S(2)}) collective-permute-start(bf16[1024,256]{1,0:T(8,128)(2,1)S(1)} %collective-permute-done.refs_0_), channel_id=1, source_target_pairs={{0,4},{4,0},{1,5},{5,1},{2,6},{6,2},{3,7},{7,3},{8,12},{12,8},{9,1... | collective-permute-start | bytes 1572872 | tf_op jit(solution)/shard_map/ppermute | solution.py:430
  17.4 39.3 %collective-permute-start.5 = (bf16[512,256]{1,0:T(8,128)(2,1)}, bf16[512,256]{1,0:T(8,128)(2,1)S(1)}, u32[]{:S(2)}, u32[]{:S(2)}) collective-permute-start(bf16[512,256]{1,0:T(8,128)(2,1)} %slice.6), channel_id=1, source_target_pairs={{0,64},{64,128},{128,192},{192,0},{1,65},{65,129},{129,193},{193,1... | collective-permute-start | bytes 786440 | tf_op jit(solution)/shard_map/ppermute | solution.py:430
  19.6 37.7 %collective-permute-start.6 = (bf16[512,256]{1,0:T(8,128)(2,1)}, bf16[512,256]{1,0:T(8,128)(2,1)}, u32[]{:S(2)}, u32[]{:S(2)}) collective-permute-start(bf16[512,256]{1,0:T(8,128)(2,1)} %slice.7), channel_id=1, source_target_pairs={{0,192},{64,0},{128,64},{192,128},{1,193},{65,1},{129,65},{193,129... | collective-permute-start | bytes 786440 | tf_op jit(solution)/shard_map/ppermute | solution.py:430
  23.6 21.1 %copy-start = (bf16[4,512,256]{2,1,0:T(8,128)(2,1)S(1)}, bf16[4,512,256]{2,1,0:T(8,128)(2,1)}, u32[]{:S(2)}) copy-start(bf16[4,512,256]{2,1,0:T(8,128)(2,1)} %wk.1) | copy-start | bytes 3145732
  39.4 5.3 %copy-start.4 = (bf16[4,4,256]{2,1,0:T(4,128)(2,1)S(1)}, bf16[4,4,256]{2,1,0:T(4,128)(2,1)}, u32[]{:S(2)}) copy-start(bf16[4,4,256]{2,1,0:T(4,128)(2,1)} %sk.1) | copy-start | bytes 24580
  39.4 5.3 %copy-start.5 = (bf16[4,4,256]{2,1,0:T(4,128)(2,1)S(1)}, bf16[4,4,256]{2,1,0:T(4,128)(2,1)}, u32[]{:S(2)}) copy-start(bf16[4,4,256]{2,1,0:T(4,128)(2,1)} %sv.1) | copy-start | bytes 24580
  39.5 5.3 %copy-start.6 = (bf16[4,256]{1,0:T(4,128)(2,1)S(1)}, bf16[4,256]{1,0:T(4,128)(2,1)}, u32[]{:S(2)}) copy-start(bf16[4,256]{1,0:T(4,128)(2,1)} %nk.1) | copy-start | bytes 6148
  39.5 5.3 %copy-start.7 = (bf16[4,256]{1,0:T(4,128)(2,1)S(1)}, bf16[4,256]{1,0:T(4,128)(2,1)}, u32[]{:S(2)}) copy-start(bf16[4,256]{1,0:T(4,128)(2,1)} %nv.1) | copy-start | bytes 6148
  39.5 5.3 %copy-start.10 = (s32[4]{0:T(128)S(1)}, s32[4]{0:T(128)}, u32[]{:S(2)}) copy-start(s32[4]{0:T(128)} %length_ref.1) | copy-start | bytes 52
  39.5 12.6 %all-to-all-start.3 = ((bf16[32,32,128]{2,1,0:T(8,128)(2,1)}), bf16[32,32,128]{2,1,0:T(8,128)(2,1)S(1)}, u32[]{:S(2)}, u32[]{:S(2)}) async-start(bf16[32,32,128]{2,1,0:T(8,128)(2,1)} %select.2), calls=%async_computation.3 | async-start | bytes 524288 | tf_op jit(solution)/shard_map/all_to_all | solution.py:532
  52.1 4.6 %copy-start.11 = (bf16[32,40,128]{2,1,0:T(8,128)(2,1)}, bf16[32,40,128]{2,1,0:T(8,128)(2,1)S(1)}, u32[]{:S(2)}) copy-start(bf16[32,40,128]{2,1,0:T(8,128)(2,1)S(1)} %get-tuple-element.69.near) | copy-start | bytes 983044
  52.1 11.8 %collective-permute-start.4 = (bf16[1024,256]{1,0:T(8,128)(2,1)S(1)}, bf16[1024,256]{1,0:T(8,128)(2,1)S(1)}, u32[]{:S(2)}, u32[]{:S(2)}) collective-permute-start(bf16[1024,256]{1,0:T(8,128)(2,1)S(1)} %collective-permute-done.1.refs_2_), channel_id=1, source_target_pairs={{0,4},{4,0},{1,5},{5,1},{2,6},{6,2},{3,7},{7,3},{8,12},{12,8},{9,1... | collective-permute-start | bytes 1572872 | tf_op jit(solution)/shard_map/ppermute | solution.py:430
  56.7 7.2 %collective-permute-start.7 = (bf16[512,256]{1,0:T(8,128)(2,1)S(1)}, bf16[512,256]{1,0:T(8,128)(2,1)S(1)}, u32[]{:S(2)}, u32[]{:S(2)}) collective-permute-start(bf16[512,256]{1,0:T(8,128)(2,1)S(1)} %collective-permute-done.5.refs_4_), channel_id=1, source_target_pairs={{0,4},{4,0},{1,5},{5,1},{2,6},{6,2},{3,7},{7,3},{8,12},{12,8},{9,1... | collective-permute-start | bytes 786440 | tf_op jit(solution)/shard_map/ppermute | solution.py:430
  57.3 6.7 %collective-permute-start.8 = (bf16[512,256]{1,0:T(8,128)(2,1)}, bf16[512,256]{1,0:T(8,128)(2,1)S(1)}, u32[]{:S(2)}, u32[]{:S(2)}) collective-permute-start(bf16[512,256]{1,0:T(8,128)(2,1)} %collective-permute-done.6.refs_5_), channel_id=1, source_target_pairs={{0,4},{4,0},{1,5},{5,1},{2,6},{6,2},{3,7},{7,3},{8,12},{12,8},{9,1... | collective-permute-start | bytes 786440 | tf_op jit(solution)/shard_map/ppermute | solution.py:430
  59.1 11.6 %all-to-all-start.4 = ((bf16[32,40,128]{2,1,0:T(8,128)(2,1)}), bf16[32,40,128]{2,1,0:T(8,128)(2,1)S(1)}, u32[]{:S(2)}, u32[]{:S(2)}) async-start(bf16[32,40,128]{2,1,0:T(8,128)(2,1)} %prefix.2), calls=%async_computation.4 | async-start | bytes 655360 | tf_op jit(solution)/shard_map/all_to_all | solution.py:551
  63.9 6.8 %copy-start.12 = (bf16[32,40,128]{2,1,0:T(8,128)(2,1)S(1)}, bf16[32,40,128]{2,1,0:T(8,128)(2,1)}, u32[]{:S(2)}) copy-start(bf16[32,40,128]{2,1,0:T(8,128)(2,1)} %copy-done.11) | copy-start | bytes 983044
  63.9 6.8 %copy-start.14 = (f32[4,32,128]{2,1,0:T(8,128)S(1)}, f32[4,32,128]{2,1,0:T(8,128)}, u32[]{:S(2)}) copy-start(f32[4,32,128]{2,1,0:T(8,128)} %copy-done.13) | copy-start | bytes 196612
  (8 other events, 8.5 us)

commit v3 on v1

--- a/solution.py
+++ b/solution.py
@@ -55,6 +55,12 @@
     return jnp.where(row == 0, first[:, None], parts).astype(BF16)
 
 
+def spread_kernel(q_ref, out):
+    rows = q_ref[...].astype(F32).reshape(NY * HEADS, HD).astype(BF16).reshape(NY, HEADS, HD)
+    for z in range(NZ):
+        out[z] = rows
+
+
 def prepare_kernel(tenant_ref, owner_ref, t_row, o_row, plan, rounds):
     x, z, c = lax.axis_index("x"), lax.axis_index("z"), lax.axis_index("c")
     zero = jnp.int32(0)
@@ -122,11 +128,10 @@
 
 def root_part(q_ref, blocks, values, out):
     for g in range(KV):
-        for n, (_, _, v0, v1) in enumerate(blocks):
-            for i, v in enumerate((v0, v1)):
-                rows = slice(n * 1024 + i * 512, n * 1024 + (i + 1) * 512)
-                values[g, rows, :HD] = v[:, g * HD : (g + 1) * HD]
-                values[g, rows, HD:] = jnp.ones((512, HD), BF16)
+        for n, (_, v) in enumerate(blocks):
+            rows = slice(n * 512, (n + 1) * 512)
+            values[g, rows, :HD] = v[:, g * HD : (g + 1) * HD]
+            values[g, rows, HD:] = jnp.ones((512, HD), BF16)
     diagonal = head_diagonal()
     rows = COLUMN // 2
     for h in range(2):
@@ -136,7 +141,7 @@
             heads = slice(g * GROUP, (g + 1) * GROUP)
             lanes = slice(g * HD, (g + 1) * HD)
             query = q_ref[chats, heads, :].reshape(rows * GROUP, HD)
-            scores = [scores_of(query, k[:, lanes]) for block in blocks for k in block[:2]]
+            scores = [scores_of(query, k[:, lanes]) for k, _ in blocks]
             peak = functools.reduce(
                 jnp.maximum, [jnp.max(s, axis=1, keepdims=True) for s in scores]
             )
@@ -196,24 +201,22 @@
         share_ref[j, g * GROUP : (g + 1) * GROUP, :] = numer / total[rows]
 
 
-def near_kernel(
-    length_ref, q_ref, k0, k1, v0, v1, wk, wv, sk, sv, nk, nv, out, share, level, values, wks, wvs, sems
-):
+def near_kernel(q_ref, k, v, out, values):
+    root_part(q_ref, [(k, v)], values, out)
+
+
+def far_kernel(length_ref, q_ref, *refs):
+    *blocks, sk, sv, nk, nv, wk, wv, out, share, level, values, wks, wvs, sems = refs
     copies = [
         pltpu.make_async_copy(wk, wks, sems.at[0]),
         pltpu.make_async_copy(wv, wvs, sems.at[1]),
     ]
     for copy in copies:
         copy.start()
-    root_part(q_ref, [(k0, k1, v0, v1)], values, out)
+    root_part(q_ref, list(zip(blocks[::2], blocks[1::2])), values, out)
     for copy in copies:
         copy.wait()
     home_part(length_ref, q_ref, wks, wvs, sk, sv, nk, nv, share, level)
-
-
-def far_kernel(q_ref, *refs):
-    out, values = refs[-2:]
-    root_part(q_ref, [refs[4 * n : 4 * n + 4] for n in range(NX - 1)], values, out)
 
 
 def select_kernel(plan, turn, q_ref, out):
@@ -357,6 +360,7 @@
 
 def merge_kernel(in_ref, out):
     diagonal = head_diagonal()
+    merged = []
     for y in range(NY):
         level = jnp.sum(in_ref[:, y, HEADS:, :].astype(F32), axis=1)
         weights = jnp.exp2(level - jnp.max(level, axis=0, keepdims=True))
@@ -366,11 +370,12 @@
             line = four_lines([weights[k + i : k + i + 1] for i in range(4)])
             shares = in_ref[k : k + 4, y, :HEADS, :].reshape(4 * HEADS, HD)
             total = total + mix(diagonal, line, shares)
-        out[y] = total.astype(BF16)
+        merged.append(total)
+    out[...] = jnp.concatenate(merged, axis=0).reshape(1, NY * HEADS * HD).astype(BF16)
 
 
 def kernel(
-    body, name, outs, args, scalars=0, scratch=(), limit=8, us=0.5, in_specs=None, out_specs=None
+    body, name, outs, args, scalars=0, scratch=(), limit=58, us=0.5, in_specs=None, out_specs=None
 ):
     return pl.pallas_call(
         body,
@@ -411,25 +416,17 @@
     tenant_of,
     owner,
 ):
-    spread = jnp.broadcast_to(queries.reshape(1, NY, HEADS, HD), (NZ, NY, HEADS, HD))
+    spread = kernel(spread_kernel, "spread", shaped(NZ, NY, HEADS, HD), [queries])
     q = lax.all_to_all(
         spread.reshape(COLUMN, HEADS, HD), ("z", "y"), split_axis=0, concat_axis=0, tiled=True
     )
 
-    k_left, v_left = send(root_keys, "x", 1), send(root_values, "x", 1)
-    k_right, v_right = send(root_keys, "x", -1), send(root_values, "x", -1)
-    k_far, v_far = send(k_left, "x", 1), send(v_right, "x", -1)
-    (rk, rv, pk, pv), (k_left, v_left, k_right, v_right) = lax.optimization_barrier(
-        (
-            (root_keys, root_values, prefix_keys, prefix_values),
-            (k_left, v_left, k_right, v_right),
-        )
-    )
-    own, *others = [
-        (k, send(k, "c", 1), v, send(v, "c", 1))
-        for k, v in ((rk, rv), (k_left, v_left), (k_right, v_right), (k_far, v_far))
-    ]
-    pk1, pv1 = send(pk, "c", 1), send(pv, "c", 1)
+    swapped = [send(a, "c", 1) for a in (root_keys, root_values, prefix_keys, prefix_values)]
+    (rk, rv), (rk1, rv1, pk1, pv1) = lax.optimization_barrier(
+        ((root_keys, root_values), swapped)
+    )
+    k_left, v_left = send(rk, "x", 1), send(rv, "x", 1)
+    k_right, v_right = send(rk, "x", -1), send(rv, "x", -1)
 
     i32 = jnp.int32
     plan, rounds = kernel(
@@ -441,37 +438,6 @@
         out_specs=[SMEM] * 2,
         us=2,
     )
-    anywhere = pl.BlockSpec(memory_space=pl.ANY)
-    near, home_share, home_level = kernel(
-        near_kernel,
-        "near",
-        [
-            shaped(COLUMN, ROWS, HD),
-            shaped(HOME, HEADS, HD, dtype=F32),
-            shaped(HOME, HD, dtype=F32),
-        ],
-        [
-            window_len,
-            q,
-            *own,
-            window_keys,
-            window_values,
-            sink_keys,
-            sink_values,
-            new_keys,
-            new_values,
-        ],
-        in_specs=[SMEM] + [VMEM] * 5 + [anywhere] * 2 + [VMEM] * 4,
-        scratch=[
-            pltpu.VMEM((KV, 1024, 2 * HD), BF16),
-            pltpu.VMEM(window_keys.shape, BF16),
-            pltpu.VMEM(window_values.shape, BF16),
-            pltpu.SemaphoreType.DMA((2,)),
-        ],
-        limit=24,
-        us=4,
-    )
-
     def scalar_kernel(body, name, outs, turn, args, **options):
         if isinstance(turn, int):
             return kernel(
@@ -484,21 +450,40 @@
             )
         return kernel(body, name, outs, [plan, turn, *args], scalars=2, **options)
 
-    def prefix_answers(turn):
-        picked = scalar_kernel(
-            select_kernel, "select", shaped(NX * ROOM, HEADS, HD), turn, [q]
-        )
+    def prefix_picked(turn):
+        return scalar_kernel(select_kernel, "select", shaped(NX * ROOM, HEADS, HD), turn, [q])
+
+    picked = prefix_picked(0)
+    near_q, _ = lax.optimization_barrier((q, picked))
+    near = kernel(
+        near_kernel,
+        "near",
+        shaped(COLUMN, ROWS, HD),
+        [near_q, root_keys, root_values],
+        scratch=[pltpu.VMEM((KV, 512, 2 * HD), BF16)],
+        us=1.5,
+    )
+    moved = (k_left, v_left, k_right, v_right)
+    moved, near = lax.optimization_barrier((moved, near))
+    k_left, v_left, k_right, v_right = moved
+    k_far, v_far = send(k_left, "x", 1), send(v_right, "x", -1)
+    others = [(rk1, rv1)]
+    for k, v in ((k_left, v_left), (k_right, v_right), (k_far, v_far)):
+        others += [(k, v), (send(k, "c", 1), send(v, "c", 1))]
+
+    def prefix_answers(turn, picked):
         asked = lax.all_to_all(picked, "x", split_axis=0, concat_axis=0, tiled=True)
         answer = scalar_kernel(
             prefix_kernel,
             "prefix",
             shaped(NX * ROOM, ROWS, HD),
             turn,
-            [asked, pk, pk1, pv, pv1],
+            [asked, prefix_keys, pk1, prefix_values, pv1],
             scratch=[
                 pltpu.VMEM((2, KV, MEMBER, GROUP, HD), BF16),
                 pltpu.SMEM((2, NX * ROOM + 1), i32),
             ],
+            limit=12,
             us=2,
         )
         return lax.all_to_all(answer, "x", split_axis=0, concat_axis=0, tiled=True)
@@ -510,24 +495,43 @@
             "scatter",
             shaped(COLUMN, ROWS, HD),
             turn,
-            [prefix_answers(turn), before],
+            [prefix_answers(turn, prefix_picked(turn)), before],
         )
         return turn + 1, after
 
     row = lax.broadcasted_iota(i32, (COLUMN, ROWS, HD), 1)
     none = jnp.where(row == HEADS, FLOOR, 0.0).astype(BF16)
-    answers = prefix_answers(0)
+    answers = prefix_answers(0, picked)
     _, later = lax.while_loop(
         lambda state: state[0][0] < rounds[0], more, (jnp.ones((1,), i32), none)
     )
-    far = kernel(
+    far, home_share, home_level = kernel(
         far_kernel,
         "far",
-        shaped(COLUMN, ROWS, HD),
-        [q, *(ref for block in others for ref in block)],
-        scratch=[pltpu.VMEM((KV, (NX - 1) * 1024, 2 * HD), BF16)],
-        limit=32,
-        us=6,
+        [
+            shaped(COLUMN, ROWS, HD),
+            shaped(HOME, HEADS, HD, dtype=F32),
+            shaped(HOME, HD, dtype=F32),
+        ],
+        [
+            window_len,
+            q,
+            *(ref for block in others for ref in block),
+            sink_keys,
+            sink_values,
+            new_keys,
+            new_values,
+            window_keys,
+            window_values,
+        ],
+        in_specs=[SMEM] + [VMEM] * (4 * NX + 3) + [pl.BlockSpec(memory_space=pl.ANY)] * 2,
+        scratch=[
+            pltpu.VMEM((KV, (2 * NX - 1) * 512, 2 * HD), BF16),
+            pltpu.VMEM(window_keys.shape, BF16),
+            pltpu.VMEM(window_values.shape, BF16),
+            pltpu.SemaphoreType.DMA((2,)),
+        ],
+        us=8,
     )
     merged = kernel(
         merge_row_kernel,
@@ -544,9 +548,9 @@
     )
     back = lax.all_to_all(merged, ("z", "y"), split_axis=0, concat_axis=0, tiled=True)
     out = kernel(
-        merge_kernel, "merge", shaped(NY, HEADS, HD), [back.reshape(NZ, NY, ROWS, HD)]
-    )
-    return out.reshape(1, NY * HEADS * HD)
+        merge_kernel, "merge", shaped(1, NY * HEADS * HD), [back.reshape(NZ, NY, ROWS, HD)]
+    )
+    return out
 
 
 def solution(mesh):

time: 85.3 us -> 88.6 us (1.039)
  Pallas kernels: 20.2 us -> 25.4 us
  blocking collectives: 18.4 us -> 22.4 us
  local copies, waits for them, and re-layouts: 4.59 us -> 0.85 us
  starting transfers between devices: 32.8 us -> 29.2 us
  waiting for transfers between devices: 7.25 us -> 9.52 us
  other arithmetic: 1.02 us -> 0.01 us
    ppermute x16, waiting for transfers between devices: 0.04 us -> 5.6 us  [send(): lax.ppermute(array, axis, [(i, (i + shift) % size) for i in range(size)])]
    pallas_call x7 -> x8, Pallas kernels: 20.2 us -> 25.4 us  [kernel(): pl.pallas_call(body, out_shape=outs, in_specs=in_specs or [SMEM] * scalar...]
    all_to_all x1, blocking collectives: 18.4 us -> 22.4 us  [local(): lax.all_to_all(merged, ('z', 'y'), split_axis=0, concat_axis=0, tiled=True)]
    all_to_all x1, waiting for transfers between devices: 7.2 us -> 3.84 us  [local(): lax.all_to_all(spread.reshape(COLUMN, HEADS, HD), ('z', 'y'), split_axis=...]
    ppermute x16, starting transfers between devices: 11.1 us -> 8.2 us  [send(): lax.ppermute(array, axis, [(i, (i + shift) % size) for i in range(size)])]
    unnamed x30 -> x18, local copies, waits for them, and re-layouts: 3.07 us -> 0.74 us
    all_to_all x1, starting transfers between devices: 6.6 us -> 4.82 us  [prefix_answers(): asked = lax.all_to_all(picked, 'x', split_axis=0, concat_axis=0, tiled=True)]
    all_to_all x1, starting transfers between devices: 10.3 us -> 11.6 us  [local(): lax.all_to_all(spread.reshape(COLUMN, HEADS, HD), ('z', 'y'), split_axis=...]
  transfers between devices with their start and end apart: 19 -> 19, of which waited for: 1 -> 6; matrix products, arithmetic and copies ran while one was open for 2% -> 0% of each run, Pallas kernels for 22% -> 24%
where the time goes in v3:
time: 88.6 us; the launch traced here: 88 us
  starting transfers between devices  29.2 us (33%)
  Pallas kernels  25.4 us (29%)
  blocking collectives  22.4 us (25%)
  waiting for transfers between devices  9.52 us (11%)
    pallas_call x8, Pallas kernels, kernel(): pl.pallas_call(body, out_shape=outs, in_specs=in_specs or [SMEM] * scalar...  25.4 us
    all_to_all x1, blocking collectives, local(): lax.all_to_all(merged, ('z', 'y'), split_axis=0, concat_axis=0, tiled=True)  22.4 us
    all_to_all x1, starting transfers between devices, local(): lax.all_to_all(spread.reshape(COLUMN, HEADS, HD), ('z', 'y'), split_axis=...  11.6 us
    ppermute x16, starting transfers between devices, send(): lax.ppermute(array, axis, [(i, (i + shift) % size) for i in range(size)])  8.2 us
    ppermute x16, waiting for transfers between devices, send(): lax.ppermute(array, axis, [(i, (i + shift) % size) for i in range(size)])  5.6 us
    all_to_all x1, starting transfers between devices, prefix_answers(): asked = lax.all_to_all(picked, 'x', split_axis=0, concat_axis=0, tiled=True)  4.82 us
    all_to_all x1, starting transfers between devices, prefix_answers(): return lax.all_to_all(answer, 'x', split_axis=0, concat_axis=0, tiled=True)  4.53 us
    all_to_all x1, waiting for transfers between devices, local(): lax.all_to_all(spread.reshape(COLUMN, HEADS, HD), ('z', 'y'), split_axis=...  3.84 us
  transfers between devices with their start and end apart: 19, of which 6 were waited for; matrix products, arithmetic and copies ran while one was open for 0% of the time, Pallas kernels for 24%

profile of v3, /device:TPU:2, one launch (start us, length us, event | category | flops | bytes accessed | tf_op | source)
XLA Modules:
  0.0 88.0 jit_solution(8708104919696599263)
XLA Ops:
  0.5 1.6 %spread.1 = bf16[8,4,32,128]{3,2,1,0:T(8,128)(2,1)} custom-call(bf16[1,16384]{1,0:T(2,128)(2,1)} %q_ref.1), custom_call_target="tpu_custom_call" | custom-call | flops 400000000 | bytes 500000 | tf_op jit(solution)/shard_map/spread/pallas_call | solution.py:380
  2.1 11.6 %all-to-all-start.2 = ((bf16[32,32,128]{2,1,0:T(8,128)(2,1)}), bf16[32,32,128]{2,1,0:T(8,128)(2,1)S(1)}, u32[]{:S(2)}, u32[]{:S(2)}) async-start(bf16[32,32,128]{2,1,0:T(8,128)(2,1)} %bitcast.7), calls=%async_computation.2 | async-start | bytes 524288 | tf_op jit(solution)/shard_map/all_to_all | solution.py:420
  14.3 1.0 %collective-permute-done.refs_0_ = bf16[512,256]{1,0:T(8,128)(2,1)S(1)} collective-permute-done((bf16[512,256]{1,0:T(8,128)(2,1)S(1)}, bf16[512,256]{1,0:T(8,128)(2,1)S(1)}, u32[]{:S(2)}, u32[]{:S(2)}) %collective-permute-start) | collective-permute-done | bytes 262176 | tf_op jit(solution)/shard_map/ppermute | solution.py:396
  15.7 0.6 collective-permute-start.6
  16.3 1.5 %collective-permute-start.4 = (bf16[512,256]{1,0:T(8,128)(2,1)S(1)}, bf16[512,256]{1,0:T(8,128)(2,1)}, u32[]{:S(2)}, u32[]{:S(2)}) collective-permute-start(bf16[512,256]{1,0:T(8,128)(2,1)S(1)} %copy-done.4), channel_id=1, source_target_pairs={{0,64},{64,128},{128,192},{192,0},{1,65},{65,129},{129,193},{193,1... | collective-permute-start | bytes 786440 | tf_op jit(solution)/shard_map/ppermute | solution.py:396
  17.8 1.3 %collective-permute-start.7 = (bf16[512,256]{1,0:T(8,128)(2,1)S(1)}, bf16[512,256]{1,0:T(8,128)(2,1)}, u32[]{:S(2)}, u32[]{:S(2)}) collective-permute-start(bf16[512,256]{1,0:T(8,128)(2,1)S(1)} %copy-done.5), channel_id=1, source_target_pairs={{0,192},{64,0},{128,64},{192,128},{1,193},{65,1},{129,65},{193,129... | collective-permute-start | bytes 786440 | tf_op jit(solution)/shard_map/ppermute | solution.py:396
  19.1 0.8 collective-permute-start.5
  19.8 3.0 %prepare.1 = (s32[9,33]{1,0:T(8,128)S(1)}, s32[1]{0:T(128)}) custom-call(s32[256]{0:T(256)} %tenant_ref.1, s32[64]{0:T(128)} %owner_ref.1, s32[1,256]{1,0:T(1,128)} %bitcast.8, s32[1,64]{1,0:T(1,128)} %bitcast.9), custom_call_target="tpu_custom_call" | custom-call | flops 1600000000 | bytes 2000000 | tf_op jit(solution)/shard_map/prepare/pallas_call | solution.py:380
  22.8 3.8 %all-to-all-done.2.refs_0_.q_ref = bf16[32,32,128]{2,1,0:T(8,128)(2,1)S(1)} async-done(((bf16[32,32,128]{2,1,0:T(8,128)(2,1)}), bf16[32,32,128]{2,1,0:T(8,128)(2,1)S(1)}, u32[]{:S(2)}, u32[]{:S(2)}) %all-to-all-start.2) | async-done | bytes 262176 | tf_op jit(solution)/shard_map/all_to_all | solution.py:420
  26.7 1.4 %select.2 = bf16[32,32,128]{2,1,0:T(8,128)(2,1)} custom-call(s32[9,33]{1,0:T(8,128)S(1)} %get-tuple-element.156.plan, bf16[32,32,128]{2,1,0:T(8,128)(2,1)S(1)} %all-to-all-done.2.refs_0_.q_ref), custom_call_target="tpu_custom_call" | custom-call | flops 400000000 | bytes 500000 | tf_op jit(solution)/shard_map/select/pallas_call | solution.py:380
  28.1 4.8 %all-to-all-start.3 = ((bf16[32,32,128]{2,1,0:T(8,128)(2,1)}), bf16[32,32,128]{2,1,0:T(8,128)(2,1)S(1)}, u32[]{:S(2)}, u32[]{:S(2)}) async-start(bf16[32,32,128]{2,1,0:T(8,128)(2,1)} %select.2), calls=%async_computation.3 | async-start | bytes 524288 | tf_op jit(solution)/shard_map/all_to_all | solution.py:475
  32.9 2.9 %near.1 = bf16[32,40,128]{2,1,0:T(8,128)(2,1)} custom-call(bf16[32,32,128]{2,1,0:T(8,128)(2,1)S(1)} %all-to-all-done.2.refs_0_.q_ref, bf16[512,256]{1,0:T(8,128)(2,1)} %k.1, bf16[512,256]{1,0:T(8,128)(2,1)} %v.1), custom_call_target="tpu_custom_call" | custom-call | flops 1200000000 | bytes 1500000 | tf_op jit(solution)/shard_map/near/pallas_call | solution.py:380
  35.9 1.5 %collective-permute-start.12 = (bf16[512,256]{1,0:T(8,128)(2,1)}, bf16[512,256]{1,0:T(8,128)(2,1)S(1)}, u32[]{:S(2)}, u32[]{:S(2)}) collective-permute-start(bf16[512,256]{1,0:T(8,128)(2,1)} %collective-permute-done.4.refs_2_), channel_id=1, source_target_pairs={{0,64},{64,128},{128,192},{192,0},{1,65},{65,129},{129,193},{193,1... | collective-permute-start | bytes 786440 | tf_op jit(solution)/shard_map/ppermute | solution.py:396
  37.5 0.6 collective-permute-start.13
  38.1 3.1 %prefix.2 = bf16[32,40,128]{2,1,0:T(8,128)(2,1)} custom-call(s32[9,33]{1,0:T(8,128)S(1)} %get-tuple-element.156.plan, bf16[32,32,128]{2,1,0:T(8,128)(2,1)S(1)} %all-to-all-done.3.refs_0_, bf16[1024,256]{1,0:T(8,128)(2,1)S(1)} %copy-done.2, bf16[1024,256]{1,0:T(8,128)(2,1)S(1)} %collective-permute-done.2.refs_2_, bf16[1024,256]{1,0:T(8,128)(2,1)S(1)} %copy-done.3, ...), custom_call_target="tpu_custom_call" | custom-call | flops 1600000000 | bytes 2000000 | tf_op jit(solution)/shard_map/prefix/pallas_call | solution.py:380
  42.0 2.9 %collective-permute-done.12.refs_10_ = bf16[512,256]{1,0:T(8,128)(2,1)S(1)} collective-permute-done((bf16[512,256]{1,0:T(8,128)(2,1)}, bf16[512,256]{1,0:T(8,128)(2,1)S(1)}, u32[]{:S(2)}, u32[]{:S(2)}) %collective-permute-start.12) | collective-permute-done | bytes 262176 | tf_op jit(solution)/shard_map/ppermute | solution.py:396
  44.9 1.3 %collective-permute-done.13.refs_11_ = bf16[512,256]{1,0:T(8,128)(2,1)} collective-permute-done((bf16[512,256]{1,0:T(8,128)(2,1)}, bf16[512,256]{1,0:T(8,128)(2,1)}, u32[]{:S(2)}, u32[]{:S(2)}) %collective-permute-start.13) | collective-permute-done | bytes 262176 | tf_op jit(solution)/shard_map/ppermute | solution.py:396
  46.3 0.6 while.10
  46.9 4.5 %all-to-all-start.4 = ((bf16[32,40,128]{2,1,0:T(8,128)(2,1)}), bf16[32,40,128]{2,1,0:T(8,128)(2,1)S(1)}, u32[]{:S(2)}, u32[]{:S(2)}) async-start(bf16[32,40,128]{2,1,0:T(8,128)(2,1)} %prefix.2), calls=%async_computation.4 | async-start | bytes 655360 | tf_op jit(solution)/shard_map/all_to_all | solution.py:489
  51.4 8.9 %far.1 = (bf16[32,40,128]{2,1,0:T(8,128)(2,1)}, f32[4,32,128]{2,1,0:T(8,128)}, f32[4,128]{1,0:T(4,128)}) custom-call(s32[4]{0:T(128)} %length_ref.1, bf16[32,32,128]{2,1,0:T(8,128)(2,1)S(1)} %get-tuple-element.187, bf16[512,256]{1,0:T(8,128)(2,1)} %copy-done.6, bf16[512,256]{1,0:T(8,128)(2,1)} %copy-done.7, bf16[512,256]{1,0:T(8,128)(2,1)} %collective-permute-done.4.refs_2_, ...), custom_call_target="tpu_custom_call" | custom-call | flops 6400000000 | bytes 8000000 | tf_op jit(solution)/shard_map/far/pallas_call | solution.py:380
  60.3 0.7 copy-done.1
  61.1 2.7 %merge_row.1 = bf16[32,40,128]{2,1,0:T(8,128)(2,1)} custom-call(s32[9,33]{1,0:T(8,128)S(1)} %get-tuple-element.207, bf16[32,40,128]{2,1,0:T(8,128)(2,1)} %near.1, bf16[32,40,128]{2,1,0:T(8,128)(2,1)} %get-tuple-element.81.far, bf16[32,40,128]{2,1,0:T(8,128)(2,1)} %copy-done.1, bf16[32,40,128]{2,1,0:T(8,128)(2,1)S(1)} %get-tuple-element.85.before, ...), custom_call_target="tpu_custom_call" | custom-call | flops 1200000000 | bytes 1500000 | tf_op jit(solution)/shard_map/merge_row/pallas_call | solution.py:380
  63.8 22.4 %all_to_all.30 = bf16[32,40,128]{2,1,0:T(8,128)(2,1)} all-to-all(bf16[32,40,128]{2,1,0:T(8,128)(2,1)} %merge_row.1), channel_id=1, replica_groups=mesh['x'=4,'z'=8,'c'=2,'y'=4] {'z','y'}, dimensions={0} | all-to-all | bytes 655360 | tf_op jit(solution)/shard_map/all_to_all | solution.py:549
  86.1 1.9 %merge.1 = bf16[1,16384]{1,0:T(2,128)(2,1)} custom-call(bf16[8,4,40,128]{3,2,1,0:T(8,128)(2,1)} %bitcast.6), custom_call_target="tpu_custom_call" | custom-call | flops 400000000 | bytes 500000 | tf_op jit(solution)/shard_map/merge/pallas_call | solution.py:380
  (44 shorter events, 2.6 us)
Async XLA Ops:
  0.0 15.7 %collective-permute-start.2 = (bf16[1024,256]{1,0:T(8,128)(2,1)}, bf16[1024,256]{1,0:T(8,128)(2,1)S(1)}, u32[]{:S(2)}, u32[]{:S(2)}) collective-permute-start(bf16[1024,256]{1,0:T(8,128)(2,1)} %refs_1_.1), channel_id=1, source_target_pairs={{0,4},{4,0},{1,5},{5,1},{2,6},{6,2},{3,7},{7,3},{8,12},{12,8},{9,1... | collective-permute-start | bytes 1572872 | tf_op jit(solution)/shard_map/ppermute | solution.py:396
  0.0 15.7 %collective-permute-start.3 = (bf16[1024,256]{1,0:T(8,128)(2,1)}, bf16[1024,256]{1,0:T(8,128)(2,1)S(1)}, u32[]{:S(2)}, u32[]{:S(2)}) collective-permute-start(bf16[1024,256]{1,0:T(8,128)(2,1)} %refs_3_.1), channel_id=1, source_target_pairs={{0,4},{4,0},{1,5},{5,1},{2,6},{6,2},{3,7},{7,3},{8,12},{12,8},{9,1... | collective-permute-start | bytes 1572872 | tf_op jit(solution)/shard_map/ppermute | solution.py:396
  2.1 11.6 %copy-start.4 = (bf16[512,256]{1,0:T(8,128)(2,1)S(1)}, bf16[512,256]{1,0:T(8,128)(2,1)}, u32[]{:S(2)}) copy-start(bf16[512,256]{1,0:T(8,128)(2,1)} %k.1) | copy-start | bytes 786436
  2.1 11.7 %copy-start.5 = (bf16[512,256]{1,0:T(8,128)(2,1)S(1)}, bf16[512,256]{1,0:T(8,128)(2,1)}, u32[]{:S(2)}) copy-start(bf16[512,256]{1,0:T(8,128)(2,1)} %v.1) | copy-start | bytes 786436
  2.1 24.6 %all-to-all-start.2 = ((bf16[32,32,128]{2,1,0:T(8,128)(2,1)}), bf16[32,32,128]{2,1,0:T(8,128)(2,1)S(1)}, u32[]{:S(2)}, u32[]{:S(2)}) async-start(bf16[32,32,128]{2,1,0:T(8,128)(2,1)} %bitcast.7), calls=%async_computation.2 | async-start | bytes 524288 | tf_op jit(solution)/shard_map/all_to_all | solution.py:420
  13.7 1.6 %collective-permute-start = (bf16[512,256]{1,0:T(8,128)(2,1)S(1)}, bf16[512,256]{1,0:T(8,128)(2,1)S(1)}, u32[]{:S(2)}, u32[]{:S(2)}) collective-permute-start(bf16[512,256]{1,0:T(8,128)(2,1)S(1)} %copy-done.4), channel_id=1, source_target_pairs={{0,4},{4,0},{1,5},{5,1},{2,6},{6,2},{3,7},{7,3},{8,12},{12,8},{9,1... | collective-permute-start | bytes 786440 | tf_op jit(solution)/shard_map/ppermute | solution.py:396
  13.8 1.9 %collective-permute-start.1 = (bf16[512,256]{1,0:T(8,128)(2,1)S(1)}, bf16[512,256]{1,0:T(8,128)(2,1)S(1)}, u32[]{:S(2)}, u32[]{:S(2)}) collective-permute-start(bf16[512,256]{1,0:T(8,128)(2,1)S(1)} %copy-done.5), channel_id=1, source_target_pairs={{0,4},{4,0},{1,5},{5,1},{2,6},{6,2},{3,7},{7,3},{8,12},{12,8},{9,1... | collective-permute-start | bytes 786440 | tf_op jit(solution)/shard_map/ppermute | solution.py:396
  15.3 7.5 %copy-start.6 = (bf16[512,256]{1,0:T(8,128)(2,1)}, bf16[512,256]{1,0:T(8,128)(2,1)S(1)}, u32[]{:S(2)}) copy-start(bf16[512,256]{1,0:T(8,128)(2,1)S(1)} %collective-permute-done.refs_0_) | copy-start | bytes 786436
  15.7 7.1 %copy-start.7 = (bf16[512,256]{1,0:T(8,128)(2,1)}, bf16[512,256]{1,0:T(8,128)(2,1)S(1)}, u32[]{:S(2)}) copy-start(bf16[512,256]{1,0:T(8,128)(2,1)S(1)} %collective-permute-done.1.refs_1_) | copy-start | bytes 786436
  15.7 20.1 %collective-permute-start.6 = (bf16[512,256]{1,0:T(8,128)(2,1)S(1)}, bf16[512,256]{1,0:T(8,128)(2,1)}, u32[]{:S(2)}, u32[]{:S(2)}) collective-permute-start(bf16[512,256]{1,0:T(8,128)(2,1)S(1)} %copy-done.4), channel_id=1, source_target_pairs={{0,192},{64,0},{128,64},{192,128},{1,193},{65,1},{129,65},{193,129... | collective-permute-start | bytes 786440 | tf_op jit(solution)/shard_map/ppermute | solution.py:396
  16.3 19.5 %collective-permute-start.4 = (bf16[512,256]{1,0:T(8,128)(2,1)S(1)}, bf16[512,256]{1,0:T(8,128)(2,1)}, u32[]{:S(2)}, u32[]{:S(2)}) collective-permute-start(bf16[512,256]{1,0:T(8,128)(2,1)S(1)} %copy-done.4), channel_id=1, source_target_pairs={{0,64},{64,128},{128,192},{192,0},{1,65},{65,129},{129,193},{193,1... | collective-permute-start | bytes 786440 | tf_op jit(solution)/shard_map/ppermute | solution.py:396
  17.8 18.0 %collective-permute-start.7 = (bf16[512,256]{1,0:T(8,128)(2,1)S(1)}, bf16[512,256]{1,0:T(8,128)(2,1)}, u32[]{:S(2)}, u32[]{:S(2)}) collective-permute-start(bf16[512,256]{1,0:T(8,128)(2,1)S(1)} %copy-done.5), channel_id=1, source_target_pairs={{0,192},{64,0},{128,64},{192,128},{1,193},{65,1},{129,65},{193,129... | collective-permute-start | bytes 786440 | tf_op jit(solution)/shard_map/ppermute | solution.py:396
  19.1 16.8 %collective-permute-start.5 = (bf16[512,256]{1,0:T(8,128)(2,1)S(1)}, bf16[512,256]{1,0:T(8,128)(2,1)}, u32[]{:S(2)}, u32[]{:S(2)}) collective-permute-start(bf16[512,256]{1,0:T(8,128)(2,1)S(1)} %copy-done.5), channel_id=1, source_target_pairs={{0,64},{64,128},{128,192},{192,0},{1,65},{65,129},{129,193},{193,1... | collective-permute-start | bytes 786440 | tf_op jit(solution)/shard_map/ppermute | solution.py:396
  28.1 10.0 %all-to-all-start.3 = ((bf16[32,32,128]{2,1,0:T(8,128)(2,1)}), bf16[32,32,128]{2,1,0:T(8,128)(2,1)S(1)}, u32[]{:S(2)}, u32[]{:S(2)}) async-start(bf16[32,32,128]{2,1,0:T(8,128)(2,1)} %select.2), calls=%async_computation.3 | async-start | bytes 524288 | tf_op jit(solution)/shard_map/all_to_all | solution.py:475
  32.9 5.2 %copy-start.3 = (bf16[1024,256]{1,0:T(8,128)(2,1)S(1)}, bf16[1024,256]{1,0:T(8,128)(2,1)}, u32[]{:S(2)}) copy-start(bf16[1024,256]{1,0:T(8,128)(2,1)} %refs_3_.1) | copy-start | bytes 1572868
  35.8 5.9 %collective-permute-start.9 = (bf16[512,256]{1,0:T(8,128)(2,1)}, bf16[512,256]{1,0:T(8,128)(2,1)S(1)}, u32[]{:S(2)}, u32[]{:S(2)}) collective-permute-start(bf16[512,256]{1,0:T(8,128)(2,1)} %collective-permute-done.5.refs_3_), channel_id=1, source_target_pairs={{0,4},{4,0},{1,5},{5,1},{2,6},{6,2},{3,7},{7,3},{8,12},{12,8},{9,1... | collective-permute-start | bytes 786440 | tf_op jit(solution)/shard_map/ppermute | solution.py:396
  35.9 8.9 %collective-permute-start.12 = (bf16[512,256]{1,0:T(8,128)(2,1)}, bf16[512,256]{1,0:T(8,128)(2,1)S(1)}, u32[]{:S(2)}, u32[]{:S(2)}) collective-permute-start(bf16[512,256]{1,0:T(8,128)(2,1)} %collective-permute-done.4.refs_2_), channel_id=1, source_target_pairs={{0,64},{64,128},{128,192},{192,0},{1,65},{65,129},{129,193},{193,1... | collective-permute-start | bytes 786440 | tf_op jit(solution)/shard_map/ppermute | solution.py:396
  37.5 8.7 %collective-permute-start.13 = (bf16[512,256]{1,0:T(8,128)(2,1)}, bf16[512,256]{1,0:T(8,128)(2,1)}, u32[]{:S(2)}, u32[]{:S(2)}) collective-permute-start(bf16[512,256]{1,0:T(8,128)(2,1)} %collective-permute-done.7.refs_7_), channel_id=1, source_target_pairs={{0,192},{64,0},{128,64},{192,128},{1,193},{65,1},{129,65},{193,129... | collective-permute-start | bytes 786440 | tf_op jit(solution)/shard_map/ppermute | solution.py:396
  41.2 10.2 %collective-permute-start.8 = (bf16[512,256]{1,0:T(8,128)(2,1)}, bf16[512,256]{1,0:T(8,128)(2,1)}, u32[]{:S(2)}, u32[]{:S(2)}) collective-permute-start(bf16[512,256]{1,0:T(8,128)(2,1)} %collective-permute-done.4.refs_2_), channel_id=1, source_target_pairs={{0,4},{4,0},{1,5},{5,1},{2,6},{6,2},{3,7},{7,3},{8,12},{12,8},{9,1... | collective-permute-start | bytes 786440 | tf_op jit(solution)/shard_map/ppermute | solution.py:396
  41.2 10.2 %collective-permute-start.11 = (bf16[512,256]{1,0:T(8,128)(2,1)}, bf16[512,256]{1,0:T(8,128)(2,1)}, u32[]{:S(2)}, u32[]{:S(2)}) collective-permute-start(bf16[512,256]{1,0:T(8,128)(2,1)} %collective-permute-done.7.refs_7_), channel_id=1, source_target_pairs={{0,4},{4,0},{1,5},{5,1},{2,6},{6,2},{3,7},{7,3},{8,12},{12,8},{9,1... | collective-permute-start | bytes 786440 | tf_op jit(solution)/shard_map/ppermute | solution.py:396
  41.7 9.7 %collective-permute-start.10 = (bf16[512,256]{1,0:T(8,128)(2,1)}, bf16[512,256]{1,0:T(8,128)(2,1)}, u32[]{:S(2)}, u32[]{:S(2)}) collective-permute-start(bf16[512,256]{1,0:T(8,128)(2,1)} %collective-permute-done.6.refs_6_), channel_id=1, source_target_pairs={{0,4},{4,0},{1,5},{5,1},{2,6},{6,2},{3,7},{7,3},{8,12},{12,8},{9,1... | collective-permute-start | bytes 786440 | tf_op jit(solution)/shard_map/ppermute | solution.py:396
  44.9 6.5 %collective-permute-start.14 = (bf16[512,256]{1,0:T(8,128)(2,1)S(1)}, bf16[512,256]{1,0:T(8,128)(2,1)}, u32[]{:S(2)}, u32[]{:S(2)}) collective-permute-start(bf16[512,256]{1,0:T(8,128)(2,1)S(1)} %collective-permute-done.12.refs_10_), channel_id=1, source_target_pairs={{0,4},{4,0},{1,5},{5,1},{2,6},{6,2},{3,7},{7,3},{8,12},{12,8},{9,1... | collective-permute-start | bytes 786440 | tf_op jit(solution)/shard_map/ppermute | solution.py:396
  46.2 5.3 %collective-permute-start.15 = (bf16[512,256]{1,0:T(8,128)(2,1)}, bf16[512,256]{1,0:T(8,128)(2,1)}, u32[]{:S(2)}, u32[]{:S(2)}) collective-permute-start(bf16[512,256]{1,0:T(8,128)(2,1)} %collective-permute-done.13.refs_11_), channel_id=1, source_target_pairs={{0,4},{4,0},{1,5},{5,1},{2,6},{6,2},{3,7},{7,3},{8,12},{12,8},{9,1... | collective-permute-start | bytes 786440 | tf_op jit(solution)/shard_map/ppermute | solution.py:396
  46.9 13.4 %all-to-all-start.4 = ((bf16[32,40,128]{2,1,0:T(8,128)(2,1)}), bf16[32,40,128]{2,1,0:T(8,128)(2,1)S(1)}, u32[]{:S(2)}, u32[]{:S(2)}) async-start(bf16[32,40,128]{2,1,0:T(8,128)(2,1)} %prefix.2), calls=%async_computation.4 | async-start | bytes 655360 | tf_op jit(solution)/shard_map/all_to_all | solution.py:489
  (4 other events, 11.9 us)

commit v4 on v1

--- a/solution.py
+++ b/solution.py
@@ -122,11 +122,10 @@
 
 def root_part(q_ref, blocks, values, out):
     for g in range(KV):
-        for n, (_, _, v0, v1) in enumerate(blocks):
-            for i, v in enumerate((v0, v1)):
-                rows = slice(n * 1024 + i * 512, n * 1024 + (i + 1) * 512)
-                values[g, rows, :HD] = v[:, g * HD : (g + 1) * HD]
-                values[g, rows, HD:] = jnp.ones((512, HD), BF16)
+        for n, (_, v) in enumerate(blocks):
+            rows = slice(n * 512, (n + 1) * 512)
+            values[g, rows, :HD] = v[:, g * HD : (g + 1) * HD]
+            values[g, rows, HD:] = jnp.ones((512, HD), BF16)
     diagonal = head_diagonal()
     rows = COLUMN // 2
     for h in range(2):
@@ -136,7 +135,7 @@
             heads = slice(g * GROUP, (g + 1) * GROUP)
             lanes = slice(g * HD, (g + 1) * HD)
             query = q_ref[chats, heads, :].reshape(rows * GROUP, HD)
-            scores = [scores_of(query, k[:, lanes]) for block in blocks for k in block[:2]]
+            scores = [scores_of(query, k[:, lanes]) for k, _ in blocks]
             peak = functools.reduce(
                 jnp.maximum, [jnp.max(s, axis=1, keepdims=True) for s in scores]
             )
@@ -197,7 +196,7 @@
 
 
 def near_kernel(
-    length_ref, q_ref, k0, k1, v0, v1, wk, wv, sk, sv, nk, nv, out, share, level, values, wks, wvs, sems
+    length_ref, q_ref, k, v, wk, wv, sk, sv, nk, nv, out, share, level, values, wks, wvs, sems
 ):
     copies = [
         pltpu.make_async_copy(wk, wks, sems.at[0]),
@@ -205,7 +204,7 @@
     ]
     for copy in copies:
         copy.start()
-    root_part(q_ref, [(k0, k1, v0, v1)], values, out)
+    root_part(q_ref, [(k, v)], values, out)
     for copy in copies:
         copy.wait()
     home_part(length_ref, q_ref, wks, wvs, sk, sv, nk, nv, share, level)
@@ -213,7 +212,8 @@
 
 def far_kernel(q_ref, *refs):
     out, values = refs[-2:]
-    root_part(q_ref, [refs[4 * n : 4 * n + 4] for n in range(NX - 1)], values, out)
+    blocks = refs[:-2]
+    root_part(q_ref, list(zip(blocks[::2], blocks[1::2])), values, out)
 
 
 def select_kernel(plan, turn, q_ref, out):
@@ -418,20 +418,8 @@
 
     k_left, v_left = send(root_keys, "x", 1), send(root_values, "x", 1)
     k_right, v_right = send(root_keys, "x", -1), send(root_values, "x", -1)
-    k_far, v_far = send(k_left, "x", 1), send(v_right, "x", -1)
-    (rk, rv, pk, pv), (k_left, v_left, k_right, v_right) = lax.optimization_barrier(
-        (
-            (root_keys, root_values, prefix_keys, prefix_values),
-            (k_left, v_left, k_right, v_right),
-        )
-    )
-    own, *others = [
-        (k, send(k, "c", 1), v, send(v, "c", 1))
-        for k, v in ((rk, rv), (k_left, v_left), (k_right, v_right), (k_far, v_far))
-    ]
-    pk1, pv1 = send(pk, "c", 1), send(pv, "c", 1)
-
     i32 = jnp.int32
+    tenant_of, _ = lax.optimization_barrier((tenant_of, spread))
     plan, rounds = kernel(
         prepare_kernel,
         "prepare",
@@ -453,7 +441,8 @@
         [
             window_len,
             q,
-            *own,
+            root_keys,
+            root_values,
             window_keys,
             window_values,
             sink_keys,
@@ -461,14 +450,14 @@
             new_keys,
             new_values,
         ],
-        in_specs=[SMEM] + [VMEM] * 5 + [anywhere] * 2 + [VMEM] * 4,
+        in_specs=[SMEM] + [VMEM] * 3 + [anywhere] * 2 + [VMEM] * 4,
         scratch=[
-            pltpu.VMEM((KV, 1024, 2 * HD), BF16),
+            pltpu.VMEM((KV, 512, 2 * HD), BF16),
             pltpu.VMEM(window_keys.shape, BF16),
             pltpu.VMEM(window_values.shape, BF16),
             pltpu.SemaphoreType.DMA((2,)),
         ],
-        limit=24,
+        limit=14,
         us=4,
     )
 
@@ -484,17 +473,27 @@
             )
         return kernel(body, name, outs, [plan, turn, *args], scalars=2, **options)
 
-    def prefix_answers(turn):
-        picked = scalar_kernel(
-            select_kernel, "select", shaped(NX * ROOM, HEADS, HD), turn, [q]
-        )
+    def prefix_picked(turn):
+        return scalar_kernel(select_kernel, "select", shaped(NX * ROOM, HEADS, HD), turn, [q])
+
+    picked = prefix_picked(0)
+    tied = (prefix_keys, prefix_values, k_left, v_left, k_right, v_right, plan)
+    pk, pv, k_left, v_left, k_right, v_right, plan = lax.optimization_barrier(tied)
+    k_far, v_far = send(k_left, "x", 1), send(v_right, "x", -1)
+    pk1, pv1 = send(pk, "c", 1), send(pv, "c", 1)
+    rk, rv, _ = lax.optimization_barrier((root_keys, root_values, picked))
+    others = [(send(rk, "c", 1), send(rv, "c", 1))]
+    for k, v in ((k_left, v_left), (k_right, v_right), (k_far, v_far)):
+        others += [(k, v), (send(k, "c", 1), send(v, "c", 1))]
+
+    def prefix_answers(turn, picked):
         asked = lax.all_to_all(picked, "x", split_axis=0, concat_axis=0, tiled=True)
         answer = scalar_kernel(
             prefix_kernel,
             "prefix",
             shaped(NX * ROOM, ROWS, HD),
             turn,
-            [asked, pk, pk1, pv, pv1],
+            [asked, prefix_keys, pk1, prefix_values, pv1],
             scratch=[
                 pltpu.VMEM((2, KV, MEMBER, GROUP, HD), BF16),
                 pltpu.SMEM((2, NX * ROOM + 1), i32),
@@ -510,13 +509,13 @@
             "scatter",
             shaped(COLUMN, ROWS, HD),
             turn,
-            [prefix_answers(turn), before],
+            [prefix_answers(turn, prefix_picked(turn)), before],
         )
         return turn + 1, after
 
     row = lax.broadcasted_iota(i32, (COLUMN, ROWS, HD), 1)
     none = jnp.where(row == HEADS, FLOOR, 0.0).astype(BF16)
-    answers = prefix_answers(0)
+    answers = prefix_answers(0, picked)
     _, later = lax.while_loop(
         lambda state: state[0][0] < rounds[0], more, (jnp.ones((1,), i32), none)
     )
@@ -525,8 +524,8 @@
         "far",
         shaped(COLUMN, ROWS, HD),
         [q, *(ref for block in others for ref in block)],
-        scratch=[pltpu.VMEM((KV, (NX - 1) * 1024, 2 * HD), BF16)],
-        limit=32,
+        scratch=[pltpu.VMEM((KV, (2 * NX - 1) * 512, 2 * HD), BF16)],
+        limit=28,
         us=6,
     )
     merged = kernel(

time: 85.3 us -> 84.5 us (level)
  starting transfers between devices: 32.8 us -> 30.2 us
  blocking collectives: 18.4 us -> 19.5 us
  local copies, waits for them, and re-layouts: 4.59 us -> 3.68 us
    all_to_all x1, starting transfers between devices: 6.6 us -> 3.91 us  [prefix_answers(): asked = lax.all_to_all(picked, 'x', split_axis=0, concat_axis=0, tiled=True)]
    all_to_all x1, waiting for transfers between devices: 0.01 us -> 2.15 us  [prefix_answers(): asked = lax.all_to_all(picked, 'x', split_axis=0, concat_axis=0, tiled=True)]
    unnamed x30, local copies, waits for them, and re-layouts: 3.07 us -> 1.43 us
    all_to_all x1, waiting for transfers between devices: 7.2 us -> 5.87 us  [local(): lax.all_to_all(spread.reshape(COLUMN, HEADS, HD), ('z', 'y'), split_axis=...]
    all_to_all x1, blocking collectives: 18.4 us -> 19.5 us  [local(): lax.all_to_all(merged, ('z', 'y'), split_axis=0, concat_axis=0, tiled=True)]
    all_to_all x1, starting transfers between devices: 10.3 us -> 11.3 us  [local(): lax.all_to_all(spread.reshape(COLUMN, HEADS, HD), ('z', 'y'), split_axis=...]
    ppermute x16, starting transfers between devices: 11.1 us -> 10.1 us  [send(): lax.ppermute(array, axis, [(i, (i + shift) % size) for i in range(size)])]
  transfers between devices with their start and end apart: 19 -> 19, of which waited for: 1 -> 2; matrix products, arithmetic and copies ran while one was open for 2% -> 3% of each run, Pallas kernels for 22% -> 22%
where the time goes in v4:
time: 84.5 us; the launch traced here: 83.9 us
  starting transfers between devices  30.2 us (36%)
  Pallas kernels  20.5 us (24%)
  blocking collectives  19.5 us (23%)
  waiting for transfers between devices  8.06 us (10%)
  local copies, waits for them, and re-layouts  3.68 us (4%)
  other arithmetic  1.02 us (1%)
    pallas_call x7, Pallas kernels, kernel(): pl.pallas_call(body, out_shape=outs, in_specs=in_specs or [SMEM] * scalar...  20.5 us
    all_to_all x1, blocking collectives, local(): lax.all_to_all(merged, ('z', 'y'), split_axis=0, concat_axis=0, tiled=True)  19.5 us
    all_to_all x1, starting transfers between devices, local(): lax.all_to_all(spread.reshape(COLUMN, HEADS, HD), ('z', 'y'), split_axis=...  11.3 us
    ppermute x16, starting transfers between devices, send(): lax.ppermute(array, axis, [(i, (i + shift) % size) for i in range(size)])  10.1 us
    all_to_all x1, waiting for transfers between devices, local(): lax.all_to_all(spread.reshape(COLUMN, HEADS, HD), ('z', 'y'), split_axis=...  5.87 us
    all_to_all x1, starting transfers between devices, prefix_answers(): return lax.all_to_all(answer, 'x', split_axis=0, concat_axis=0, tiled=True)  4.87 us
    all_to_all x1, starting transfers between devices, prefix_answers(): asked = lax.all_to_all(picked, 'x', split_axis=0, concat_axis=0, tiled=True)  3.91 us
    all_to_all x1, waiting for transfers between devices, prefix_answers(): asked = lax.all_to_all(picked, 'x', split_axis=0, concat_axis=0, tiled=True)  2.15 us
  transfers between devices with their start and end apart: 19, of which 2 were waited for; matrix products, arithmetic and copies ran while one was open for 3% of the time, Pallas kernels for 22%

profile of v4, /device:TPU:2, one launch (start us, length us, event | category | flops | bytes accessed | tf_op | source)
XLA Modules:
  0.0 83.9 jit_solution(14781916765878136756)
XLA Ops:
  0.0 1.5 %collective-permute-start = (bf16[512,256]{1,0:T(8,128)(2,1)}, bf16[512,256]{1,0:T(8,128)(2,1)S(1)}, u32[]{:S(2)}, u32[]{:S(2)}) collective-permute-start(bf16[512,256]{1,0:T(8,128)(2,1)} %k.1), channel_id=1, source_target_pairs={{0,64},{64,128},{128,192},{192,0},{1,65},{65,129},{129,193},{193,1... | collective-permute-start | bytes 786440 | tf_op jit(solution)/shard_map/ppermute | solution.py:391
  1.5 1.2 %collective-permute-start.1 = (bf16[512,256]{1,0:T(8,128)(2,1)}, bf16[512,256]{1,0:T(8,128)(2,1)S(1)}, u32[]{:S(2)}, u32[]{:S(2)}) collective-permute-start(bf16[512,256]{1,0:T(8,128)(2,1)} %v.1), channel_id=1, source_target_pairs={{0,64},{64,128},{128,192},{192,0},{1,65},{65,129},{129,193},{193,1... | collective-permute-start | bytes 786440 | tf_op jit(solution)/shard_map/ppermute | solution.py:391
  2.7 0.8 collective-permute-start.2
  3.5 2.0 %collective-permute-start.3 = (bf16[512,256]{1,0:T(8,128)(2,1)}, bf16[512,256]{1,0:T(8,128)(2,1)}, u32[]{:S(2)}, u32[]{:S(2)}) collective-permute-start(bf16[512,256]{1,0:T(8,128)(2,1)} %v.1), channel_id=1, source_target_pairs={{0,192},{64,0},{128,64},{192,128},{1,193},{65,1},{129,65},{193,129... | collective-permute-start | bytes 786440 | tf_op jit(solution)/shard_map/ppermute | solution.py:391
  5.5 1.0 %reduce = bf16[16384]{0:T(1024)(128)(2,1)S(1)} reduce(bf16[1,16384]{1,0:T(2,128)(2,1)} %param.16, bf16[]{:T(256)} %constant.18), dimensions={0}, to_apply=%param.16.reduce_sub_computation | reduce | bytes 65538 | tf_op args[0]
  6.6 0.7 broadcast_in_dim.16
  7.3 11.3 %all-to-all-start.2 = ((bf16[32,32,128]{2,1,0:T(8,128)(2,1)}), bf16[32,32,128]{2,1,0:T(8,128)(2,1)}, u32[]{:S(2)}, u32[]{:S(2)}) async-start(bf16[32,32,128]{2,1,0:T(8,128)(2,1)} %bitcast.3), calls=%async_computation.2 | async-start | bytes 524288 | tf_op jit(solution)/shard_map/all_to_all | solution.py:415
  18.7 0.7 copy-done.10
  19.3 2.8 %prepare.1 = (s32[9,33]{1,0:T(8,128)S(1)}, s32[1]{0:T(128)}) custom-call(s32[256]{0:T(256)S(1)} %copy-done.10, s32[64]{0:T(128)S(1)} %copy-done.11, s32[1,256]{1,0:T(1,128)S(1)} %bitcast.8, s32[1,64]{1,0:T(1,128)S(1)} %bitcast.9), custom_call_target="tpu_custom_call" | custom-call | flops 1600000000 | bytes 2000000 | tf_op jit(solution)/shard_map/prepare/pallas_call | solution.py:375
  23.1 1.7 %collective-permute-start.11 = (bf16[512,256]{1,0:T(8,128)(2,1)}, bf16[512,256]{1,0:T(8,128)(2,1)}, u32[]{:S(2)}, u32[]{:S(2)}) collective-permute-start(bf16[512,256]{1,0:T(8,128)(2,1)} %collective-permute-done.3.refs_7_), channel_id=1, source_target_pairs={{0,192},{64,0},{128,64},{192,128},{1,193},{65,1},{129,65},{193,129... | collective-permute-start | bytes 786440 | tf_op jit(solution)/shard_map/ppermute | solution.py:391
  24.8 5.9 %all-to-all-done.2.q_ref.refs_0_ = bf16[32,32,128]{2,1,0:T(8,128)(2,1)} async-done(((bf16[32,32,128]{2,1,0:T(8,128)(2,1)}), bf16[32,32,128]{2,1,0:T(8,128)(2,1)}, u32[]{:S(2)}, u32[]{:S(2)}) %all-to-all-start.2) | async-done | bytes 262176 | tf_op jit(solution)/shard_map/all_to_all | solution.py:415
  30.7 1.8 %select.2 = bf16[32,32,128]{2,1,0:T(8,128)(2,1)} custom-call(s32[9,33]{1,0:T(8,128)S(1)} %get-tuple-element.152.plan, bf16[32,32,128]{2,1,0:T(8,128)(2,1)} %all-to-all-done.2.q_ref.refs_0_), custom_call_target="tpu_custom_call" | custom-call | flops 400000000 | bytes 500000 | tf_op jit(solution)/shard_map/select/pallas_call | solution.py:375
  33.1 3.9 %all-to-all-start.3 = ((bf16[32,32,128]{2,1,0:T(8,128)(2,1)}), bf16[32,32,128]{2,1,0:T(8,128)(2,1)S(1)}, u32[]{:S(2)}, u32[]{:S(2)}) async-start(bf16[32,32,128]{2,1,0:T(8,128)(2,1)} %select.2), calls=%async_computation.3 | async-start | bytes 524288 | tf_op jit(solution)/shard_map/all_to_all | solution.py:490
  37.1 2.8 %near.1 = (bf16[32,40,128]{2,1,0:T(8,128)(2,1)S(1)}, f32[4,32,128]{2,1,0:T(8,128)S(1)}, f32[4,128]{1,0:T(4,128)S(1)}) custom-call(s32[4]{0:T(128)S(1)} %copy-done.12, bf16[32,32,128]{2,1,0:T(8,128)(2,1)} %all-to-all-done.2.q_ref.refs_0_, bf16[512,256]{1,0:T(8,128)(2,1)S(1)} %copy-done.2, bf16[512,256]{1,0:T(8,128)(2,1)S(1)} %copy-done.3, ...), custom_call_target="tpu_custom_call" | custom-call | flops 3200000000 | bytes 4000000 | tf_op jit(solution)/shard_map/near/pallas_call | solution.py:375
  39.9 0.7 copy-done.13
  40.6 2.2 %all-to-all-done.3.refs_0_ = bf16[32,32,128]{2,1,0:T(8,128)(2,1)S(1)} async-done(((bf16[32,32,128]{2,1,0:T(8,128)(2,1)}), bf16[32,32,128]{2,1,0:T(8,128)(2,1)S(1)}, u32[]{:S(2)}, u32[]{:S(2)}) %all-to-all-start.3) | async-done | bytes 262176 | tf_op jit(solution)/shard_map/all_to_all | solution.py:490
  42.8 3.9 %prefix.2 = bf16[32,40,128]{2,1,0:T(8,128)(2,1)} custom-call(s32[9,33]{1,0:T(8,128)S(1)} %get-tuple-element.152.plan, bf16[32,32,128]{2,1,0:T(8,128)(2,1)S(1)} %all-to-all-done.3.refs_0_, bf16[1024,256]{1,0:T(8,128)(2,1)} %refs_1_.1, bf16[1024,256]{1,0:T(8,128)(2,1)} %collective-permute-done.14.refs_2_, bf16[1024,256]{1,0:T(8,128)(2,1)} %refs_3_.1, ...), custom_call_target="tpu_custom_call" | custom-call | flops 1600000000 | bytes 2000000 | tf_op jit(solution)/shard_map/prefix/pallas_call | solution.py:375
  48.1 0.8 iota.7
  49.0 0.7 while.10
  49.7 4.9 %all-to-all-start.4 = ((bf16[32,40,128]{2,1,0:T(8,128)(2,1)}), bf16[32,40,128]{2,1,0:T(8,128)(2,1)S(1)}, u32[]{:S(2)}, u32[]{:S(2)}) async-start(bf16[32,40,128]{2,1,0:T(8,128)(2,1)} %prefix.2), calls=%async_computation.4 | async-start | bytes 655360 | tf_op jit(solution)/shard_map/all_to_all | solution.py:503
  54.6 7.1 %far.1 = bf16[32,40,128]{2,1,0:T(8,128)(2,1)S(1)} custom-call(bf16[32,32,128]{2,1,0:T(8,128)(2,1)} %all-to-all-done.2.q_ref.refs_0_, bf16[512,256]{1,0:T(8,128)(2,1)S(1)} %collective-permute-done.4.refs_0_, bf16[512,256]{1,0:T(8,128)(2,1)S(1)} %collective-permute-done.5.refs_1_, bf16[512,256]{1,0:T(8,128)(2,1)S(1)} %collective-permute-done.refs_2_, ...), custom_call_target="tpu_custom_call" | custom-call | flops 4800000000 | bytes 6000000 | tf_op jit(solution)/shard_map/far/pallas_call | solution.py:375
  61.7 1.8 %merge_row.1 = bf16[32,40,128]{2,1,0:T(8,128)(2,1)S(1)} custom-call(s32[9,33]{1,0:T(8,128)S(1)} %get-tuple-element.200, bf16[32,40,128]{2,1,0:T(8,128)(2,1)S(1)} %copy-done.14, bf16[32,40,128]{2,1,0:T(8,128)(2,1)S(1)} %far.1, bf16[32,40,128]{2,1,0:T(8,128)(2,1)S(1)} %all-to-all-done.4.back, bf16[32,40,128]{2,1,0:T(8,128)(2,1)} %get-tuple-element.81.before, ...), custom_call_target="tpu_custom_call" | custom-call | flops 1200000000 | bytes 1500000 | tf_op jit(solution)/shard_map/merge_row/pallas_call | solution.py:375
  63.5 19.5 %all_to_all.30 = bf16[32,40,128]{2,1,0:T(8,128)(2,1)S(1)} all-to-all(bf16[32,40,128]{2,1,0:T(8,128)(2,1)S(1)} %merge_row.1), channel_id=1, replica_groups=mesh['x'=4,'z'=8,'c'=2,'y'=4] {'z','y'}, dimensions={0} | all-to-all | bytes 655360 | tf_op jit(solution)/shard_map/all_to_all | solution.py:544
  83.2 0.7 reshape.22
  (58 shorter events, 3.2 us)
Async XLA Ops:
  0.0 22.2 %collective-permute-start = (bf16[512,256]{1,0:T(8,128)(2,1)}, bf16[512,256]{1,0:T(8,128)(2,1)S(1)}, u32[]{:S(2)}, u32[]{:S(2)}) collective-permute-start(bf16[512,256]{1,0:T(8,128)(2,1)} %k.1), channel_id=1, source_target_pairs={{0,64},{64,128},{128,192},{192,0},{1,65},{65,129},{129,193},{193,1... | collective-permute-start | bytes 786440 | tf_op jit(solution)/shard_map/ppermute | solution.py:391
  1.5 20.7 %collective-permute-start.1 = (bf16[512,256]{1,0:T(8,128)(2,1)}, bf16[512,256]{1,0:T(8,128)(2,1)S(1)}, u32[]{:S(2)}, u32[]{:S(2)}) collective-permute-start(bf16[512,256]{1,0:T(8,128)(2,1)} %v.1), channel_id=1, source_target_pairs={{0,64},{64,128},{128,192},{192,0},{1,65},{65,129},{129,193},{193,1... | collective-permute-start | bytes 786440 | tf_op jit(solution)/shard_map/ppermute | solution.py:391
  2.7 19.5 %collective-permute-start.2 = (bf16[512,256]{1,0:T(8,128)(2,1)}, bf16[512,256]{1,0:T(8,128)(2,1)S(1)}, u32[]{:S(2)}, u32[]{:S(2)}) collective-permute-start(bf16[512,256]{1,0:T(8,128)(2,1)} %k.1), channel_id=1, source_target_pairs={{0,192},{64,0},{128,64},{192,128},{1,193},{65,1},{129,65},{193,129... | collective-permute-start | bytes 786440 | tf_op jit(solution)/shard_map/ppermute | solution.py:391
  3.5 18.7 %collective-permute-start.3 = (bf16[512,256]{1,0:T(8,128)(2,1)}, bf16[512,256]{1,0:T(8,128)(2,1)}, u32[]{:S(2)}, u32[]{:S(2)}) collective-permute-start(bf16[512,256]{1,0:T(8,128)(2,1)} %v.1), channel_id=1, source_target_pairs={{0,192},{64,0},{128,64},{192,128},{1,193},{65,1},{129,65},{193,129... | collective-permute-start | bytes 786440 | tf_op jit(solution)/shard_map/ppermute | solution.py:391
  7.3 23.4 %all-to-all-start.2 = ((bf16[32,32,128]{2,1,0:T(8,128)(2,1)}), bf16[32,32,128]{2,1,0:T(8,128)(2,1)}, u32[]{:S(2)}, u32[]{:S(2)}) async-start(bf16[32,32,128]{2,1,0:T(8,128)(2,1)} %bitcast.3), calls=%async_computation.2 | async-start | bytes 524288 | tf_op jit(solution)/shard_map/all_to_all | solution.py:415
  19.3 17.7 %copy-start.1 = (bf16[4,512,256]{2,1,0:T(8,128)(2,1)S(1)}, bf16[4,512,256]{2,1,0:T(8,128)(2,1)}, u32[]{:S(2)}) copy-start(bf16[4,512,256]{2,1,0:T(8,128)(2,1)} %wv.1) | copy-start | bytes 3145732
  22.2 14.9 %copy-start = (bf16[4,512,256]{2,1,0:T(8,128)(2,1)S(1)}, bf16[4,512,256]{2,1,0:T(8,128)(2,1)}, u32[]{:S(2)}) copy-start(bf16[4,512,256]{2,1,0:T(8,128)(2,1)} %wk.1) | copy-start | bytes 3145732
  22.2 10.3 %copy-start.4 = (bf16[512,256]{1,0:T(8,128)(2,1)}, bf16[512,256]{1,0:T(8,128)(2,1)S(1)}, u32[]{:S(2)}) copy-start(bf16[512,256]{1,0:T(8,128)(2,1)S(1)} %collective-permute-done.2.refs_6_) | copy-start | bytes 786436
  22.2 10.3 %collective-permute-start.14 = (bf16[1024,256]{1,0:T(8,128)(2,1)}, bf16[1024,256]{1,0:T(8,128)(2,1)}, u32[]{:S(2)}, u32[]{:S(2)}) collective-permute-start(bf16[1024,256]{1,0:T(8,128)(2,1)} %refs_1_.1), channel_id=1, source_target_pairs={{0,4},{4,0},{1,5},{5,1},{2,6},{6,2},{3,7},{7,3},{8,12},{12,8},{9,1... | collective-permute-start | bytes 1572872 | tf_op jit(solution)/shard_map/ppermute | solution.py:391
  22.3 10.3 %collective-permute-start.15 = (bf16[1024,256]{1,0:T(8,128)(2,1)}, bf16[1024,256]{1,0:T(8,128)(2,1)}, u32[]{:S(2)}, u32[]{:S(2)}) collective-permute-start(bf16[1024,256]{1,0:T(8,128)(2,1)} %refs_3_.1), channel_id=1, source_target_pairs={{0,4},{4,0},{1,5},{5,1},{2,6},{6,2},{3,7},{7,3},{8,12},{12,8},{9,1... | collective-permute-start | bytes 1572872 | tf_op jit(solution)/shard_map/ppermute | solution.py:391
  22.8 23.9 %collective-permute-start.10 = (bf16[512,256]{1,0:T(8,128)(2,1)S(1)}, bf16[512,256]{1,0:T(8,128)(2,1)}, u32[]{:S(2)}, u32[]{:S(2)}) collective-permute-start(bf16[512,256]{1,0:T(8,128)(2,1)S(1)} %collective-permute-done.refs_2_), channel_id=1, source_target_pairs={{0,64},{64,128},{128,192},{192,0},{1,65},{65,129},{129,193},{193,1... | collective-permute-start | bytes 786440 | tf_op jit(solution)/shard_map/ppermute | solution.py:391
  23.1 24.4 %collective-permute-start.6 = (bf16[512,256]{1,0:T(8,128)(2,1)S(1)}, bf16[512,256]{1,0:T(8,128)(2,1)}, u32[]{:S(2)}, u32[]{:S(2)}) collective-permute-start(bf16[512,256]{1,0:T(8,128)(2,1)S(1)} %collective-permute-done.refs_2_), channel_id=1, source_target_pairs={{0,4},{4,0},{1,5},{5,1},{2,6},{6,2},{3,7},{7,3},{8,12},{12,8},{9,1... | collective-permute-start | bytes 786440 | tf_op jit(solution)/shard_map/ppermute | solution.py:391
  23.1 23.9 %collective-permute-start.11 = (bf16[512,256]{1,0:T(8,128)(2,1)}, bf16[512,256]{1,0:T(8,128)(2,1)}, u32[]{:S(2)}, u32[]{:S(2)}) collective-permute-start(bf16[512,256]{1,0:T(8,128)(2,1)} %collective-permute-done.3.refs_7_), channel_id=1, source_target_pairs={{0,192},{64,0},{128,64},{192,128},{1,193},{65,1},{129,65},{193,129... | collective-permute-start | bytes 786440 | tf_op jit(solution)/shard_map/ppermute | solution.py:391
  30.7 6.3 %copy-start.12 = (s32[4]{0:T(128)S(1)}, s32[4]{0:T(128)}, u32[]{:S(2)}) copy-start(s32[4]{0:T(128)} %length_ref.1) | copy-start | bytes 52
  32.5 15.1 %collective-permute-start.9 = (bf16[512,256]{1,0:T(8,128)(2,1)}, bf16[512,256]{1,0:T(8,128)(2,1)}, u32[]{:S(2)}, u32[]{:S(2)}) collective-permute-start(bf16[512,256]{1,0:T(8,128)(2,1)} %collective-permute-done.3.refs_7_), channel_id=1, source_target_pairs={{0,4},{4,0},{1,5},{5,1},{2,6},{6,2},{3,7},{7,3},{8,12},{12,8},{9,1... | collective-permute-start | bytes 786440 | tf_op jit(solution)/shard_map/ppermute | solution.py:391
  32.6 15.4 %collective-permute-start.7 = (bf16[512,256]{1,0:T(8,128)(2,1)S(1)}, bf16[512,256]{1,0:T(8,128)(2,1)}, u32[]{:S(2)}, u32[]{:S(2)}) collective-permute-start(bf16[512,256]{1,0:T(8,128)(2,1)S(1)} %collective-permute-done.1.refs_3_), channel_id=1, source_target_pairs={{0,4},{4,0},{1,5},{5,1},{2,6},{6,2},{3,7},{7,3},{8,12},{12,8},{9,1... | collective-permute-start | bytes 786440 | tf_op jit(solution)/shard_map/ppermute | solution.py:391
  33.1 9.7 %all-to-all-start.3 = ((bf16[32,32,128]{2,1,0:T(8,128)(2,1)}), bf16[32,32,128]{2,1,0:T(8,128)(2,1)S(1)}, u32[]{:S(2)}, u32[]{:S(2)}) async-start(bf16[32,32,128]{2,1,0:T(8,128)(2,1)} %select.2), calls=%async_computation.3 | async-start | bytes 524288 | tf_op jit(solution)/shard_map/all_to_all | solution.py:490
  46.7 7.8 %collective-permute-start.8 = (bf16[512,256]{1,0:T(8,128)(2,1)S(1)}, bf16[512,256]{1,0:T(8,128)(2,1)S(1)}, u32[]{:S(2)}, u32[]{:S(2)}) collective-permute-start(bf16[512,256]{1,0:T(8,128)(2,1)S(1)} %copy-done.5), channel_id=1, source_target_pairs={{0,4},{4,0},{1,5},{5,1},{2,6},{6,2},{3,7},{7,3},{8,12},{12,8},{9,1... | collective-permute-start | bytes 786440 | tf_op jit(solution)/shard_map/ppermute | solution.py:391
  47.0 7.5 %collective-permute-start.4 = (bf16[512,256]{1,0:T(8,128)(2,1)S(1)}, bf16[512,256]{1,0:T(8,128)(2,1)S(1)}, u32[]{:S(2)}, u32[]{:S(2)}) collective-permute-start(bf16[512,256]{1,0:T(8,128)(2,1)S(1)} %copy-done.2), channel_id=1, source_target_pairs={{0,4},{4,0},{1,5},{5,1},{2,6},{6,2},{3,7},{7,3},{8,12},{12,8},{9,1... | collective-permute-start | bytes 786440 | tf_op jit(solution)/shard_map/ppermute | solution.py:391
  47.5 7.0 %collective-permute-start.5 = (bf16[512,256]{1,0:T(8,128)(2,1)S(1)}, bf16[512,256]{1,0:T(8,128)(2,1)S(1)}, u32[]{:S(2)}, u32[]{:S(2)}) collective-permute-start(bf16[512,256]{1,0:T(8,128)(2,1)S(1)} %copy-done.3), channel_id=1, source_target_pairs={{0,4},{4,0},{1,5},{5,1},{2,6},{6,2},{3,7},{7,3},{8,12},{12,8},{9,1... | collective-permute-start | bytes 786440 | tf_op jit(solution)/shard_map/ppermute | solution.py:391
  47.6 6.9 %collective-permute-start.12 = (bf16[512,256]{1,0:T(8,128)(2,1)}, bf16[512,256]{1,0:T(8,128)(2,1)S(1)}, u32[]{:S(2)}, u32[]{:S(2)}) collective-permute-start(bf16[512,256]{1,0:T(8,128)(2,1)} %collective-permute-done.10.refs_10_), channel_id=1, source_target_pairs={{0,4},{4,0},{1,5},{5,1},{2,6},{6,2},{3,7},{7,3},{8,12},{12,8},{9,1... | collective-permute-start | bytes 786440 | tf_op jit(solution)/shard_map/ppermute | solution.py:391
  48.0 6.5 %collective-permute-start.13 = (bf16[512,256]{1,0:T(8,128)(2,1)}, bf16[512,256]{1,0:T(8,128)(2,1)S(1)}, u32[]{:S(2)}, u32[]{:S(2)}) collective-permute-start(bf16[512,256]{1,0:T(8,128)(2,1)} %collective-permute-done.11.refs_11_), channel_id=1, source_target_pairs={{0,4},{4,0},{1,5},{5,1},{2,6},{6,2},{3,7},{7,3},{8,12},{12,8},{9,1... | collective-permute-start | bytes 786440 | tf_op jit(solution)/shard_map/ppermute | solution.py:391
  49.7 12.0 %all-to-all-start.4 = ((bf16[32,40,128]{2,1,0:T(8,128)(2,1)}), bf16[32,40,128]{2,1,0:T(8,128)(2,1)S(1)}, u32[]{:S(2)}, u32[]{:S(2)}) async-start(bf16[32,40,128]{2,1,0:T(8,128)(2,1)} %prefix.2), calls=%async_computation.4 | async-start | bytes 655360 | tf_op jit(solution)/shard_map/all_to_all | solution.py:503
  54.5 7.2 %copy-start.14 = (bf16[32,40,128]{2,1,0:T(8,128)(2,1)S(1)}, bf16[32,40,128]{2,1,0:T(8,128)(2,1)}, u32[]{:S(2)}) copy-start(bf16[32,40,128]{2,1,0:T(8,128)(2,1)} %copy-done.13) | copy-start | bytes 983044
  (10 other events, 42.6 us)

commit v5 on v4

--- a/solution.py
+++ b/solution.py
@@ -141,7 +141,7 @@
             )
             numer = None
             for n, s in enumerate(scores):
-                weights = jnp.exp2((s - peak) * SCALE2).astype(BF16)
+                weights = jnp.exp2(((s - peak) * SCALE2).astype(BF16))
                 part = dot(weights, values[g, n * 512 : (n + 1) * 512, :])
                 numer = part if numer is None else numer + part
             total = numer[:, HD:]

time: 84.5 us -> 85 us (level)
  no operation moved by 1% of the time
where the time goes in v5:
time: 85 us; the launch traced here: 84 us
  starting transfers between devices  30.3 us (36%)
  Pallas kernels  20.6 us (24%)
  blocking collectives  19.5 us (23%)
  waiting for transfers between devices  8.05 us (9%)
  local copies, waits for them, and re-layouts  3.68 us (4%)
  other arithmetic  1.02 us (1%)
    pallas_call x7, Pallas kernels, kernel(): pl.pallas_call(body, out_shape=outs, in_specs=in_specs or [SMEM] * scalar...  20.6 us
    all_to_all x1, blocking collectives, local(): lax.all_to_all(merged, ('z', 'y'), split_axis=0, concat_axis=0, tiled=True)  19.5 us
    all_to_all x1, starting transfers between devices, local(): lax.all_to_all(spread.reshape(COLUMN, HEADS, HD), ('z', 'y'), split_axis=...  11.3 us
    ppermute x16, starting transfers between devices, send(): lax.ppermute(array, axis, [(i, (i + shift) % size) for i in range(size)])  10.1 us
    all_to_all x1, waiting for transfers between devices, local(): lax.all_to_all(spread.reshape(COLUMN, HEADS, HD), ('z', 'y'), split_axis=...  5.87 us
    all_to_all x1, starting transfers between devices, prefix_answers(): return lax.all_to_all(answer, 'x', split_axis=0, concat_axis=0, tiled=True)  4.93 us
    all_to_all x1, starting transfers between devices, prefix_answers(): asked = lax.all_to_all(picked, 'x', split_axis=0, concat_axis=0, tiled=True)  3.91 us
    all_to_all x1, waiting for transfers between devices, prefix_answers(): asked = lax.all_to_all(picked, 'x', split_axis=0, concat_axis=0, tiled=True)  2.14 us
  transfers between devices with their start and end apart: 19, of which 2 were waited for; matrix products, arithmetic and copies ran while one was open for 3% of the time, Pallas kernels for 22%

profile of v5, /device:TPU:2, one launch (start us, length us, event | category | flops | bytes accessed | tf_op | source)
XLA Modules:
  0.0 84.0 jit_solution(11312204508825770696)
XLA Ops:
  0.0 1.5 %collective-permute-start = (bf16[512,256]{1,0:T(8,128)(2,1)}, bf16[512,256]{1,0:T(8,128)(2,1)S(1)}, u32[]{:S(2)}, u32[]{:S(2)}) collective-permute-start(bf16[512,256]{1,0:T(8,128)(2,1)} %k.1), channel_id=1, source_target_pairs={{0,64},{64,128},{128,192},{192,0},{1,65},{65,129},{129,193},{193,1... | collective-permute-start | bytes 786440 | tf_op jit(solution)/shard_map/ppermute | solution.py:391
  1.5 1.2 %collective-permute-start.1 = (bf16[512,256]{1,0:T(8,128)(2,1)}, bf16[512,256]{1,0:T(8,128)(2,1)S(1)}, u32[]{:S(2)}, u32[]{:S(2)}) collective-permute-start(bf16[512,256]{1,0:T(8,128)(2,1)} %v.1), channel_id=1, source_target_pairs={{0,64},{64,128},{128,192},{192,0},{1,65},{65,129},{129,193},{193,1... | collective-permute-start | bytes 786440 | tf_op jit(solution)/shard_map/ppermute | solution.py:391
  2.7 0.8 collective-permute-start.2
  3.5 2.0 %collective-permute-start.3 = (bf16[512,256]{1,0:T(8,128)(2,1)}, bf16[512,256]{1,0:T(8,128)(2,1)}, u32[]{:S(2)}, u32[]{:S(2)}) collective-permute-start(bf16[512,256]{1,0:T(8,128)(2,1)} %v.1), channel_id=1, source_target_pairs={{0,192},{64,0},{128,64},{192,128},{1,193},{65,1},{129,65},{193,129... | collective-permute-start | bytes 786440 | tf_op jit(solution)/shard_map/ppermute | solution.py:391
  5.5 1.0 %reduce = bf16[16384]{0:T(1024)(128)(2,1)S(1)} reduce(bf16[1,16384]{1,0:T(2,128)(2,1)} %param.16, bf16[]{:T(256)} %constant.18), dimensions={0}, to_apply=%param.16.reduce_sub_computation | reduce | bytes 65538 | tf_op args[0]
  6.6 0.7 broadcast_in_dim.16
  7.3 11.3 %all-to-all-start.2 = ((bf16[32,32,128]{2,1,0:T(8,128)(2,1)}), bf16[32,32,128]{2,1,0:T(8,128)(2,1)}, u32[]{:S(2)}, u32[]{:S(2)}) async-start(bf16[32,32,128]{2,1,0:T(8,128)(2,1)} %bitcast.3), calls=%async_computation.2 | async-start | bytes 524288 | tf_op jit(solution)/shard_map/all_to_all | solution.py:415
  18.7 0.7 copy-done.10
  19.3 2.8 %prepare.1 = (s32[9,33]{1,0:T(8,128)S(1)}, s32[1]{0:T(128)}) custom-call(s32[256]{0:T(256)S(1)} %copy-done.10, s32[64]{0:T(128)S(1)} %copy-done.11, s32[1,256]{1,0:T(1,128)S(1)} %bitcast.8, s32[1,64]{1,0:T(1,128)S(1)} %bitcast.9), custom_call_target="tpu_custom_call" | custom-call | flops 1600000000 | bytes 2000000 | tf_op jit(solution)/shard_map/prepare/pallas_call | solution.py:375
  23.1 1.7 %collective-permute-start.11 = (bf16[512,256]{1,0:T(8,128)(2,1)}, bf16[512,256]{1,0:T(8,128)(2,1)}, u32[]{:S(2)}, u32[]{:S(2)}) collective-permute-start(bf16[512,256]{1,0:T(8,128)(2,1)} %collective-permute-done.3.refs_7_), channel_id=1, source_target_pairs={{0,192},{64,0},{128,64},{192,128},{1,193},{65,1},{129,65},{193,129... | collective-permute-start | bytes 786440 | tf_op jit(solution)/shard_map/ppermute | solution.py:391
  24.8 5.9 %all-to-all-done.2.q_ref.refs_0_ = bf16[32,32,128]{2,1,0:T(8,128)(2,1)} async-done(((bf16[32,32,128]{2,1,0:T(8,128)(2,1)}), bf16[32,32,128]{2,1,0:T(8,128)(2,1)}, u32[]{:S(2)}, u32[]{:S(2)}) %all-to-all-start.2) | async-done | bytes 262176 | tf_op jit(solution)/shard_map/all_to_all | solution.py:415
  30.7 1.8 %select.2 = bf16[32,32,128]{2,1,0:T(8,128)(2,1)} custom-call(s32[9,33]{1,0:T(8,128)S(1)} %get-tuple-element.152.plan, bf16[32,32,128]{2,1,0:T(8,128)(2,1)} %all-to-all-done.2.q_ref.refs_0_), custom_call_target="tpu_custom_call" | custom-call | flops 400000000 | bytes 500000 | tf_op jit(solution)/shard_map/select/pallas_call | solution.py:375
  33.1 3.9 %all-to-all-start.3 = ((bf16[32,32,128]{2,1,0:T(8,128)(2,1)}), bf16[32,32,128]{2,1,0:T(8,128)(2,1)S(1)}, u32[]{:S(2)}, u32[]{:S(2)}) async-start(bf16[32,32,128]{2,1,0:T(8,128)(2,1)} %select.2), calls=%async_computation.3 | async-start | bytes 524288 | tf_op jit(solution)/shard_map/all_to_all | solution.py:490
  37.1 2.8 %near.1 = (bf16[32,40,128]{2,1,0:T(8,128)(2,1)S(1)}, f32[4,32,128]{2,1,0:T(8,128)S(1)}, f32[4,128]{1,0:T(4,128)S(1)}) custom-call(s32[4]{0:T(128)S(1)} %copy-done.12, bf16[32,32,128]{2,1,0:T(8,128)(2,1)} %all-to-all-done.2.q_ref.refs_0_, bf16[512,256]{1,0:T(8,128)(2,1)S(1)} %copy-done.2, bf16[512,256]{1,0:T(8,128)(2,1)S(1)} %copy-done.3, ...), custom_call_target="tpu_custom_call" | custom-call | flops 3200000000 | bytes 4000000 | tf_op jit(solution)/shard_map/near/pallas_call | solution.py:375
  39.9 0.7 copy-done.13
  40.6 2.1 %all-to-all-done.3.refs_0_ = bf16[32,32,128]{2,1,0:T(8,128)(2,1)S(1)} async-done(((bf16[32,32,128]{2,1,0:T(8,128)(2,1)}), bf16[32,32,128]{2,1,0:T(8,128)(2,1)S(1)}, u32[]{:S(2)}, u32[]{:S(2)}) %all-to-all-start.3) | async-done | bytes 262176 | tf_op jit(solution)/shard_map/all_to_all | solution.py:490
  42.8 3.9 %prefix.2 = bf16[32,40,128]{2,1,0:T(8,128)(2,1)} custom-call(s32[9,33]{1,0:T(8,128)S(1)} %get-tuple-element.152.plan, bf16[32,32,128]{2,1,0:T(8,128)(2,1)S(1)} %all-to-all-done.3.refs_0_, bf16[1024,256]{1,0:T(8,128)(2,1)} %refs_1_.1, bf16[1024,256]{1,0:T(8,128)(2,1)} %collective-permute-done.14.refs_2_, bf16[1024,256]{1,0:T(8,128)(2,1)} %refs_3_.1, ...), custom_call_target="tpu_custom_call" | custom-call | flops 1600000000 | bytes 2000000 | tf_op jit(solution)/shard_map/prefix/pallas_call | solution.py:375
  48.1 0.8 iota.7
  48.9 0.7 while.10
  49.6 4.9 %all-to-all-start.4 = ((bf16[32,40,128]{2,1,0:T(8,128)(2,1)}), bf16[32,40,128]{2,1,0:T(8,128)(2,1)S(1)}, u32[]{:S(2)}, u32[]{:S(2)}) async-start(bf16[32,40,128]{2,1,0:T(8,128)(2,1)} %prefix.2), calls=%async_computation.4 | async-start | bytes 655360 | tf_op jit(solution)/shard_map/all_to_all | solution.py:503
  54.6 7.3 %far.1 = bf16[32,40,128]{2,1,0:T(8,128)(2,1)S(1)} custom-call(bf16[32,32,128]{2,1,0:T(8,128)(2,1)} %all-to-all-done.2.q_ref.refs_0_, bf16[512,256]{1,0:T(8,128)(2,1)S(1)} %collective-permute-done.4.refs_0_, bf16[512,256]{1,0:T(8,128)(2,1)S(1)} %collective-permute-done.5.refs_1_, bf16[512,256]{1,0:T(8,128)(2,1)S(1)} %collective-permute-done.refs_2_, ...), custom_call_target="tpu_custom_call" | custom-call | flops 4800000000 | bytes 6000000 | tf_op jit(solution)/shard_map/far/pallas_call | solution.py:375
  61.9 1.7 %merge_row.1 = bf16[32,40,128]{2,1,0:T(8,128)(2,1)S(1)} custom-call(s32[9,33]{1,0:T(8,128)S(1)} %get-tuple-element.200, bf16[32,40,128]{2,1,0:T(8,128)(2,1)S(1)} %copy-done.14, bf16[32,40,128]{2,1,0:T(8,128)(2,1)S(1)} %far.1, bf16[32,40,128]{2,1,0:T(8,128)(2,1)S(1)} %all-to-all-done.4.back, bf16[32,40,128]{2,1,0:T(8,128)(2,1)} %get-tuple-element.81.before, ...), custom_call_target="tpu_custom_call" | custom-call | flops 1200000000 | bytes 1500000 | tf_op jit(solution)/shard_map/merge_row/pallas_call | solution.py:375
  63.6 19.5 %all_to_all.30 = bf16[32,40,128]{2,1,0:T(8,128)(2,1)S(1)} all-to-all(bf16[32,40,128]{2,1,0:T(8,128)(2,1)S(1)} %merge_row.1), channel_id=1, replica_groups=mesh['x'=4,'z'=8,'c'=2,'y'=4] {'z','y'}, dimensions={0} | all-to-all | bytes 655360 | tf_op jit(solution)/shard_map/all_to_all | solution.py:544
  83.4 0.7 reshape.22
  (58 shorter events, 3.2 us)
Async XLA Ops:
  0.0 22.2 %collective-permute-start = (bf16[512,256]{1,0:T(8,128)(2,1)}, bf16[512,256]{1,0:T(8,128)(2,1)S(1)}, u32[]{:S(2)}, u32[]{:S(2)}) collective-permute-start(bf16[512,256]{1,0:T(8,128)(2,1)} %k.1), channel_id=1, source_target_pairs={{0,64},{64,128},{128,192},{192,0},{1,65},{65,129},{129,193},{193,1... | collective-permute-start | bytes 786440 | tf_op jit(solution)/shard_map/ppermute | solution.py:391
  1.5 20.7 %collective-permute-start.1 = (bf16[512,256]{1,0:T(8,128)(2,1)}, bf16[512,256]{1,0:T(8,128)(2,1)S(1)}, u32[]{:S(2)}, u32[]{:S(2)}) collective-permute-start(bf16[512,256]{1,0:T(8,128)(2,1)} %v.1), channel_id=1, source_target_pairs={{0,64},{64,128},{128,192},{192,0},{1,65},{65,129},{129,193},{193,1... | collective-permute-start | bytes 786440 | tf_op jit(solution)/shard_map/ppermute | solution.py:391
  2.7 19.5 %collective-permute-start.2 = (bf16[512,256]{1,0:T(8,128)(2,1)}, bf16[512,256]{1,0:T(8,128)(2,1)S(1)}, u32[]{:S(2)}, u32[]{:S(2)}) collective-permute-start(bf16[512,256]{1,0:T(8,128)(2,1)} %k.1), channel_id=1, source_target_pairs={{0,192},{64,0},{128,64},{192,128},{1,193},{65,1},{129,65},{193,129... | collective-permute-start | bytes 786440 | tf_op jit(solution)/shard_map/ppermute | solution.py:391
  3.5 18.7 %collective-permute-start.3 = (bf16[512,256]{1,0:T(8,128)(2,1)}, bf16[512,256]{1,0:T(8,128)(2,1)}, u32[]{:S(2)}, u32[]{:S(2)}) collective-permute-start(bf16[512,256]{1,0:T(8,128)(2,1)} %v.1), channel_id=1, source_target_pairs={{0,192},{64,0},{128,64},{192,128},{1,193},{65,1},{129,65},{193,129... | collective-permute-start | bytes 786440 | tf_op jit(solution)/shard_map/ppermute | solution.py:391
  7.3 23.4 %all-to-all-start.2 = ((bf16[32,32,128]{2,1,0:T(8,128)(2,1)}), bf16[32,32,128]{2,1,0:T(8,128)(2,1)}, u32[]{:S(2)}, u32[]{:S(2)}) async-start(bf16[32,32,128]{2,1,0:T(8,128)(2,1)} %bitcast.3), calls=%async_computation.2 | async-start | bytes 524288 | tf_op jit(solution)/shard_map/all_to_all | solution.py:415
  19.3 17.7 %copy-start.1 = (bf16[4,512,256]{2,1,0:T(8,128)(2,1)S(1)}, bf16[4,512,256]{2,1,0:T(8,128)(2,1)}, u32[]{:S(2)}) copy-start(bf16[4,512,256]{2,1,0:T(8,128)(2,1)} %wv.1) | copy-start | bytes 3145732
  22.2 14.9 %copy-start = (bf16[4,512,256]{2,1,0:T(8,128)(2,1)S(1)}, bf16[4,512,256]{2,1,0:T(8,128)(2,1)}, u32[]{:S(2)}) copy-start(bf16[4,512,256]{2,1,0:T(8,128)(2,1)} %wk.1) | copy-start | bytes 3145732
  22.2 10.3 %copy-start.4 = (bf16[512,256]{1,0:T(8,128)(2,1)}, bf16[512,256]{1,0:T(8,128)(2,1)S(1)}, u32[]{:S(2)}) copy-start(bf16[512,256]{1,0:T(8,128)(2,1)S(1)} %collective-permute-done.2.refs_6_) | copy-start | bytes 786436
  22.2 10.3 %collective-permute-start.14 = (bf16[1024,256]{1,0:T(8,128)(2,1)}, bf16[1024,256]{1,0:T(8,128)(2,1)}, u32[]{:S(2)}, u32[]{:S(2)}) collective-permute-start(bf16[1024,256]{1,0:T(8,128)(2,1)} %refs_1_.1), channel_id=1, source_target_pairs={{0,4},{4,0},{1,5},{5,1},{2,6},{6,2},{3,7},{7,3},{8,12},{12,8},{9,1... | collective-permute-start | bytes 1572872 | tf_op jit(solution)/shard_map/ppermute | solution.py:391
  22.3 10.3 %collective-permute-start.15 = (bf16[1024,256]{1,0:T(8,128)(2,1)}, bf16[1024,256]{1,0:T(8,128)(2,1)}, u32[]{:S(2)}, u32[]{:S(2)}) collective-permute-start(bf16[1024,256]{1,0:T(8,128)(2,1)} %refs_3_.1), channel_id=1, source_target_pairs={{0,4},{4,0},{1,5},{5,1},{2,6},{6,2},{3,7},{7,3},{8,12},{12,8},{9,1... | collective-permute-start | bytes 1572872 | tf_op jit(solution)/shard_map/ppermute | solution.py:391
  22.8 23.9 %collective-permute-start.10 = (bf16[512,256]{1,0:T(8,128)(2,1)S(1)}, bf16[512,256]{1,0:T(8,128)(2,1)}, u32[]{:S(2)}, u32[]{:S(2)}) collective-permute-start(bf16[512,256]{1,0:T(8,128)(2,1)S(1)} %collective-permute-done.refs_2_), channel_id=1, source_target_pairs={{0,64},{64,128},{128,192},{192,0},{1,65},{65,129},{129,193},{193,1... | collective-permute-start | bytes 786440 | tf_op jit(solution)/shard_map/ppermute | solution.py:391
  23.1 24.4 %collective-permute-start.6 = (bf16[512,256]{1,0:T(8,128)(2,1)S(1)}, bf16[512,256]{1,0:T(8,128)(2,1)}, u32[]{:S(2)}, u32[]{:S(2)}) collective-permute-start(bf16[512,256]{1,0:T(8,128)(2,1)S(1)} %collective-permute-done.refs_2_), channel_id=1, source_target_pairs={{0,4},{4,0},{1,5},{5,1},{2,6},{6,2},{3,7},{7,3},{8,12},{12,8},{9,1... | collective-permute-start | bytes 786440 | tf_op jit(solution)/shard_map/ppermute | solution.py:391
  23.1 23.9 %collective-permute-start.11 = (bf16[512,256]{1,0:T(8,128)(2,1)}, bf16[512,256]{1,0:T(8,128)(2,1)}, u32[]{:S(2)}, u32[]{:S(2)}) collective-permute-start(bf16[512,256]{1,0:T(8,128)(2,1)} %collective-permute-done.3.refs_7_), channel_id=1, source_target_pairs={{0,192},{64,0},{128,64},{192,128},{1,193},{65,1},{129,65},{193,129... | collective-permute-start | bytes 786440 | tf_op jit(solution)/shard_map/ppermute | solution.py:391
  30.7 6.3 %copy-start.12 = (s32[4]{0:T(128)S(1)}, s32[4]{0:T(128)}, u32[]{:S(2)}) copy-start(s32[4]{0:T(128)} %length_ref.1) | copy-start | bytes 52
  32.5 15.1 %collective-permute-start.9 = (bf16[512,256]{1,0:T(8,128)(2,1)}, bf16[512,256]{1,0:T(8,128)(2,1)}, u32[]{:S(2)}, u32[]{:S(2)}) collective-permute-start(bf16[512,256]{1,0:T(8,128)(2,1)} %collective-permute-done.3.refs_7_), channel_id=1, source_target_pairs={{0,4},{4,0},{1,5},{5,1},{2,6},{6,2},{3,7},{7,3},{8,12},{12,8},{9,1... | collective-permute-start | bytes 786440 | tf_op jit(solution)/shard_map/ppermute | solution.py:391
  32.6 15.4 %collective-permute-start.7 = (bf16[512,256]{1,0:T(8,128)(2,1)S(1)}, bf16[512,256]{1,0:T(8,128)(2,1)}, u32[]{:S(2)}, u32[]{:S(2)}) collective-permute-start(bf16[512,256]{1,0:T(8,128)(2,1)S(1)} %collective-permute-done.1.refs_3_), channel_id=1, source_target_pairs={{0,4},{4,0},{1,5},{5,1},{2,6},{6,2},{3,7},{7,3},{8,12},{12,8},{9,1... | collective-permute-start | bytes 786440 | tf_op jit(solution)/shard_map/ppermute | solution.py:391
  33.1 9.7 %all-to-all-start.3 = ((bf16[32,32,128]{2,1,0:T(8,128)(2,1)}), bf16[32,32,128]{2,1,0:T(8,128)(2,1)S(1)}, u32[]{:S(2)}, u32[]{:S(2)}) async-start(bf16[32,32,128]{2,1,0:T(8,128)(2,1)} %select.2), calls=%async_computation.3 | async-start | bytes 524288 | tf_op jit(solution)/shard_map/all_to_all | solution.py:490
  46.7 7.9 %collective-permute-start.8 = (bf16[512,256]{1,0:T(8,128)(2,1)S(1)}, bf16[512,256]{1,0:T(8,128)(2,1)S(1)}, u32[]{:S(2)}, u32[]{:S(2)}) collective-permute-start(bf16[512,256]{1,0:T(8,128)(2,1)S(1)} %copy-done.5), channel_id=1, source_target_pairs={{0,4},{4,0},{1,5},{5,1},{2,6},{6,2},{3,7},{7,3},{8,12},{12,8},{9,1... | collective-permute-start | bytes 786440 | tf_op jit(solution)/shard_map/ppermute | solution.py:391
  47.0 7.6 %collective-permute-start.4 = (bf16[512,256]{1,0:T(8,128)(2,1)S(1)}, bf16[512,256]{1,0:T(8,128)(2,1)S(1)}, u32[]{:S(2)}, u32[]{:S(2)}) collective-permute-start(bf16[512,256]{1,0:T(8,128)(2,1)S(1)} %copy-done.2), channel_id=1, source_target_pairs={{0,4},{4,0},{1,5},{5,1},{2,6},{6,2},{3,7},{7,3},{8,12},{12,8},{9,1... | collective-permute-start | bytes 786440 | tf_op jit(solution)/shard_map/ppermute | solution.py:391
  47.5 7.1 %collective-permute-start.5 = (bf16[512,256]{1,0:T(8,128)(2,1)S(1)}, bf16[512,256]{1,0:T(8,128)(2,1)S(1)}, u32[]{:S(2)}, u32[]{:S(2)}) collective-permute-start(bf16[512,256]{1,0:T(8,128)(2,1)S(1)} %copy-done.3), channel_id=1, source_target_pairs={{0,4},{4,0},{1,5},{5,1},{2,6},{6,2},{3,7},{7,3},{8,12},{12,8},{9,1... | collective-permute-start | bytes 786440 | tf_op jit(solution)/shard_map/ppermute | solution.py:391
  47.6 7.0 %collective-permute-start.12 = (bf16[512,256]{1,0:T(8,128)(2,1)}, bf16[512,256]{1,0:T(8,128)(2,1)S(1)}, u32[]{:S(2)}, u32[]{:S(2)}) collective-permute-start(bf16[512,256]{1,0:T(8,128)(2,1)} %collective-permute-done.10.refs_10_), channel_id=1, source_target_pairs={{0,4},{4,0},{1,5},{5,1},{2,6},{6,2},{3,7},{7,3},{8,12},{12,8},{9,1... | collective-permute-start | bytes 786440 | tf_op jit(solution)/shard_map/ppermute | solution.py:391
  48.0 6.6 %collective-permute-start.13 = (bf16[512,256]{1,0:T(8,128)(2,1)}, bf16[512,256]{1,0:T(8,128)(2,1)S(1)}, u32[]{:S(2)}, u32[]{:S(2)}) collective-permute-start(bf16[512,256]{1,0:T(8,128)(2,1)} %collective-permute-done.11.refs_11_), channel_id=1, source_target_pairs={{0,4},{4,0},{1,5},{5,1},{2,6},{6,2},{3,7},{7,3},{8,12},{12,8},{9,1... | collective-permute-start | bytes 786440 | tf_op jit(solution)/shard_map/ppermute | solution.py:391
  49.6 12.2 %all-to-all-start.4 = ((bf16[32,40,128]{2,1,0:T(8,128)(2,1)}), bf16[32,40,128]{2,1,0:T(8,128)(2,1)S(1)}, u32[]{:S(2)}, u32[]{:S(2)}) async-start(bf16[32,40,128]{2,1,0:T(8,128)(2,1)} %prefix.2), calls=%async_computation.4 | async-start | bytes 655360 | tf_op jit(solution)/shard_map/all_to_all | solution.py:503
  54.6 7.3 %copy-start.14 = (bf16[32,40,128]{2,1,0:T(8,128)(2,1)S(1)}, bf16[32,40,128]{2,1,0:T(8,128)(2,1)}, u32[]{:S(2)}) copy-start(bf16[32,40,128]{2,1,0:T(8,128)(2,1)} %copy-done.13) | copy-start | bytes 983044
  (10 other events, 42.5 us)

commit v6 on v5

--- a/solution.py
+++ b/solution.py
@@ -127,30 +127,25 @@
             values[g, rows, :HD] = v[:, g * HD : (g + 1) * HD]
             values[g, rows, HD:] = jnp.ones((512, HD), BF16)
     diagonal = head_diagonal()
-    rows = COLUMN // 2
-    for h in range(2):
-        chats = slice(h * rows, (h + 1) * rows)
-        line = None
-        for g in range(KV):
-            heads = slice(g * GROUP, (g + 1) * GROUP)
-            lanes = slice(g * HD, (g + 1) * HD)
-            query = q_ref[chats, heads, :].reshape(rows * GROUP, HD)
-            scores = [scores_of(query, k[:, lanes]) for k, _ in blocks]
-            peak = functools.reduce(
-                jnp.maximum, [jnp.max(s, axis=1, keepdims=True) for s in scores]
-            )
-            numer = None
-            for n, s in enumerate(scores):
-                weights = jnp.exp2(((s - peak) * SCALE2).astype(BF16))
-                part = dot(weights, values[g, n * 512 : (n + 1) * 512, :])
-                numer = part if numer is None else numer + part
-            total = numer[:, HD:]
-            share = (numer[:, :HD] / total).astype(BF16)
-            out[chats, heads, :] = share.reshape(rows, GROUP, HD)
-            level = (peak * SCALE2 + jnp.log2(total)).reshape(rows, GROUP, HD)
-            part = jnp.sum(jnp.where(diagonal[None, heads], level, 0.0), axis=1)
-            line = part if line is None else line + part
-        out[chats, HEADS:, :] = level_parts(line)
+    line = None
+    for g in range(KV):
+        heads = slice(g * GROUP, (g + 1) * GROUP)
+        lanes = slice(g * HD, (g + 1) * HD)
+        query = q_ref[:, heads, :].reshape(COLUMN * GROUP, HD)
+        scores = [scores_of(query, k[:, lanes]) for k, _ in blocks]
+        peak = functools.reduce(jnp.maximum, [jnp.max(s, axis=1, keepdims=True) for s in scores])
+        numer = None
+        for n, s in enumerate(scores):
+            weights = jnp.exp2((s - peak) * SCALE2).astype(BF16)
+            part = dot(weights, values[g, n * 512 : (n + 1) * 512, :])
+            numer = part if numer is None else numer + part
+        total = numer[:, HD:]
+        share = (numer[:, :HD] / total).astype(BF16)
+        out[:, heads, :] = share.reshape(COLUMN, GROUP, HD)
+        level = (peak * SCALE2 + jnp.log2(total)).reshape(COLUMN, GROUP, HD)
+        part = jnp.sum(jnp.where(diagonal[None, heads], level, 0.0), axis=1)
+        line = part if line is None else line + part
+    out[:, HEADS:, :] = level_parts(line)
 
 
 def home_part(length_ref, q_ref, wk, wv, sk, sv, nk, nv, share_ref, level_ref):
@@ -281,6 +276,8 @@
 
 
 def place_answers(plan, start, back, out):
+    row = iota((COLUMN, ROWS, HD), 1)
+    out[...] = jnp.where(row == HEADS, FLOOR, 0.0).astype(BF16)
     for t in range(NX):
 
         def place(e, _, t=t):
@@ -288,11 +285,6 @@
             return 0
 
         lax.fori_loop(0, jnp.clip(plan[2 * NX, t] - start, 0, ROOM), place, 0)
-
-
-def scatter_kernel(plan, turn, back, before, out):
-    out[...] = before[...]
-    place_answers(plan, turn[0] * ROOM, back, out)
 
 
 def weights_of(levels):
@@ -320,9 +312,20 @@
     return dot(high, shares) + dot(low, shares)
 
 
-def merge_row_kernel(plan, near, far, back, before, share_ref, level_ref, out, prefix, lines, levels):
+def more_kernel(plan, turn, back, before, out, prefix):
     diagonal = head_diagonal()
-    prefix[...] = before[...]
+    place_answers(plan, turn[0] * ROOM, back, prefix)
+    weights, total = weights_of([read_level(r) for r in (before, prefix)])
+    line = four_lines(weights)
+    out[:, HEADS:, :] = level_parts(total)
+    empty = jnp.zeros((2 * HEADS, HD), BF16)
+    for i in range(COLUMN):
+        shares = jnp.concatenate([before[i, :HEADS, :], prefix[i, :HEADS, :], empty], axis=0)
+        out[i, :HEADS, :] = mix(diagonal, line[i : i + 1], shares).astype(BF16)
+
+
+def merge_row_kernel(plan, near, far, back, share_ref, level_ref, out, prefix, levels):
+    diagonal = head_diagonal()
     place_answers(plan, 0, back, prefix)
     level = [read_level(r) for r in (near, far, prefix)]
     weights, total = weights_of(level)
@@ -504,20 +507,19 @@
 
     def more(state):
         turn, before = state
-        after = scalar_kernel(
-            scatter_kernel,
-            "scatter",
+        after = kernel(
+            more_kernel,
+            "more",
             shaped(COLUMN, ROWS, HD),
-            turn,
-            [prefix_answers(turn, prefix_picked(turn)), before],
+            [plan, turn, prefix_answers(turn, prefix_picked(turn)), before],
+            scalars=2,
+            scratch=[pltpu.VMEM((COLUMN, ROWS, HD), BF16)],
         )
         return turn + 1, after
 
-    row = lax.broadcasted_iota(i32, (COLUMN, ROWS, HD), 1)
-    none = jnp.where(row == HEADS, FLOOR, 0.0).astype(BF16)
     answers = prefix_answers(0, picked)
-    _, later = lax.while_loop(
-        lambda state: state[0][0] < rounds[0], more, (jnp.ones((1,), i32), none)
+    _, near = lax.while_loop(
+        lambda state: state[0][0] < rounds[0], more, (jnp.ones((1,), i32), near)
     )
     far = kernel(
         far_kernel,
@@ -525,18 +527,17 @@
         shaped(COLUMN, ROWS, HD),
         [q, *(ref for block in others for ref in block)],
         scratch=[pltpu.VMEM((KV, (2 * NX - 1) * 512, 2 * HD), BF16)],
-        limit=28,
+        limit=36,
         us=6,
     )
     merged = kernel(
         merge_row_kernel,
         "merge_row",
         shaped(COLUMN, ROWS, HD),
-        [plan, near, far, answers, later, home_share, home_level],
+        [plan, near, far, answers, home_share, home_level],
         scalars=1,
         scratch=[
             pltpu.VMEM((COLUMN, ROWS, HD), BF16),
-            pltpu.VMEM((COLUMN, HD), F32),
             pltpu.VMEM((3, COLUMN, HD), F32),
         ],
         us=1.5,

time: 85 us -> 83.2 us (0.979)
  local copies, waits for them, and re-layouts: 3.68 us -> 2.12 us
  blocking collectives: 19.5 us -> 18.5 us
    all_to_all x1, blocking collectives: 19.5 us -> 18.5 us  [local(): lax.all_to_all(merged, ('z', 'y'), split_axis=0, concat_axis=0, tiled=True)]
  transfers between devices with their start and end apart: 19 -> 19, of which waited for: 2 -> 2; matrix products, arithmetic and copies ran while one was open for 3% -> 2% of each run, Pallas kernels for 22% -> 24%
where the time goes in v6:
time: 83.2 us; the launch traced here: 82.6 us
  starting transfers between devices  30 us (36%)
  Pallas kernels  21.4 us (26%)
  blocking collectives  18.5 us (22%)
  waiting for transfers between devices  8.65 us (10%)
  local copies, waits for them, and re-layouts  2.12 us (3%)
  other arithmetic  1.02 us (1%)
    pallas_call x7, Pallas kernels, kernel(): pl.pallas_call(body, out_shape=outs, in_specs=in_specs or [SMEM] * scalar...  21.4 us
    all_to_all x1, blocking collectives, local(): lax.all_to_all(merged, ('z', 'y'), split_axis=0, concat_axis=0, tiled=True)  18.5 us
    all_to_all x1, starting transfers between devices, local(): lax.all_to_all(spread.reshape(COLUMN, HEADS, HD), ('z', 'y'), split_axis=...  11.3 us
    ppermute x16, starting transfers between devices, send(): lax.ppermute(array, axis, [(i, (i + shift) % size) for i in range(size)])  9.85 us
    all_to_all x1, waiting for transfers between devices, local(): lax.all_to_all(spread.reshape(COLUMN, HEADS, HD), ('z', 'y'), split_axis=...  5.88 us
    all_to_all x1, starting transfers between devices, prefix_answers(): return lax.all_to_all(answer, 'x', split_axis=0, concat_axis=0, tiled=True)  4.93 us
    all_to_all x1, starting transfers between devices, prefix_answers(): asked = lax.all_to_all(picked, 'x', split_axis=0, concat_axis=0, tiled=True)  3.91 us
    all_to_all x1, waiting for transfers between devices, prefix_answers(): asked = lax.all_to_all(picked, 'x', split_axis=0, concat_axis=0, tiled=True)  2.72 us
  transfers between devices with their start and end apart: 19, of which 2 were waited for; matrix products, arithmetic and copies ran while one was open for 2% of the time, Pallas kernels for 24%

profile of v6, /device:TPU:2, one launch (start us, length us, event | category | flops | bytes accessed | tf_op | source)
XLA Modules:
  0.0 82.6 jit_solution(13323954017564367394)
XLA Ops:
  0.0 1.5 %collective-permute-start = (bf16[512,256]{1,0:T(8,128)(2,1)}, bf16[512,256]{1,0:T(8,128)(2,1)S(1)}, u32[]{:S(2)}, u32[]{:S(2)}) collective-permute-start(bf16[512,256]{1,0:T(8,128)(2,1)} %k.1), channel_id=1, source_target_pairs={{0,64},{64,128},{128,192},{192,0},{1,65},{65,129},{129,193},{193,1... | collective-permute-start | bytes 786440 | tf_op jit(solution)/shard_map/ppermute | solution.py:394
  1.5 1.2 %collective-permute-start.1 = (bf16[512,256]{1,0:T(8,128)(2,1)}, bf16[512,256]{1,0:T(8,128)(2,1)S(1)}, u32[]{:S(2)}, u32[]{:S(2)}) collective-permute-start(bf16[512,256]{1,0:T(8,128)(2,1)} %v.1), channel_id=1, source_target_pairs={{0,64},{64,128},{128,192},{192,0},{1,65},{65,129},{129,193},{193,1... | collective-permute-start | bytes 786440 | tf_op jit(solution)/shard_map/ppermute | solution.py:394
  2.7 0.8 %collective-permute-start.2 = (bf16[512,256]{1,0:T(8,128)(2,1)}, bf16[512,256]{1,0:T(8,128)(2,1)}, u32[]{:S(2)}, u32[]{:S(2)}) collective-permute-start(bf16[512,256]{1,0:T(8,128)(2,1)} %k.1), channel_id=1, source_target_pairs={{0,192},{64,0},{128,64},{192,128},{1,193},{65,1},{129,65},{193,129... | collective-permute-start | bytes 786440 | tf_op jit(solution)/shard_map/ppermute | solution.py:394
  3.5 2.0 %collective-permute-start.3 = (bf16[512,256]{1,0:T(8,128)(2,1)}, bf16[512,256]{1,0:T(8,128)(2,1)}, u32[]{:S(2)}, u32[]{:S(2)}) collective-permute-start(bf16[512,256]{1,0:T(8,128)(2,1)} %v.1), channel_id=1, source_target_pairs={{0,192},{64,0},{128,64},{192,128},{1,193},{65,1},{129,65},{193,129... | collective-permute-start | bytes 786440 | tf_op jit(solution)/shard_map/ppermute | solution.py:394
  5.5 1.0 %reduce = bf16[16384]{0:T(1024)(128)(2,1)S(1)} reduce(bf16[1,16384]{1,0:T(2,128)(2,1)} %param.16, bf16[]{:T(256)} %constant.12), dimensions={0}, to_apply=%param.16.reduce_sub_computation | reduce | bytes 65538 | tf_op args[0]
  6.6 0.7 broadcast_in_dim.8
  7.3 11.3 %all-to-all-start.2 = ((bf16[32,32,128]{2,1,0:T(8,128)(2,1)}), bf16[32,32,128]{2,1,0:T(8,128)(2,1)}, u32[]{:S(2)}, u32[]{:S(2)}) async-start(bf16[32,32,128]{2,1,0:T(8,128)(2,1)} %bitcast.3), calls=%async_computation.2 | async-start | bytes 524288 | tf_op jit(solution)/shard_map/all_to_all | solution.py:418
  18.7 0.7 copy-done.8
  19.3 2.8 %prepare.1 = (s32[9,33]{1,0:T(8,128)S(1)}, s32[1]{0:T(128)}) custom-call(s32[256]{0:T(256)S(1)} %copy-done.8, s32[64]{0:T(128)S(1)} %copy-done.9, s32[1,256]{1,0:T(1,128)S(1)} %bitcast.8, s32[1,64]{1,0:T(1,128)S(1)} %bitcast.9), custom_call_target="tpu_custom_call" | custom-call | flops 1600000000 | bytes 2000000 | tf_op jit(solution)/shard_map/prepare/pallas_call | solution.py:378
  22.8 0.5 collective-permute-start.13
  23.3 1.5 %collective-permute-start.12 = (bf16[512,256]{1,0:T(8,128)(2,1)S(1)}, bf16[512,256]{1,0:T(8,128)(2,1)}, u32[]{:S(2)}, u32[]{:S(2)}) collective-permute-start(bf16[512,256]{1,0:T(8,128)(2,1)S(1)} %collective-permute-done.refs_2_), channel_id=1, source_target_pairs={{0,64},{64,128},{128,192},{192,0},{1,65},{65,129},{129,193},{193,1... | collective-permute-start | bytes 786440 | tf_op jit(solution)/shard_map/ppermute | solution.py:394
  24.8 5.9 %all-to-all-done.2.q_ref.refs_0_ = bf16[32,32,128]{2,1,0:T(8,128)(2,1)} async-done(((bf16[32,32,128]{2,1,0:T(8,128)(2,1)}), bf16[32,32,128]{2,1,0:T(8,128)(2,1)}, u32[]{:S(2)}, u32[]{:S(2)}) %all-to-all-start.2) | async-done | bytes 262176 | tf_op jit(solution)/shard_map/all_to_all | solution.py:418
  30.7 1.7 %select.2 = bf16[32,32,128]{2,1,0:T(8,128)(2,1)} custom-call(s32[9,33]{1,0:T(8,128)S(1)} %get-tuple-element.152.plan, bf16[32,32,128]{2,1,0:T(8,128)(2,1)} %all-to-all-done.2.q_ref.refs_0_), custom_call_target="tpu_custom_call" | custom-call | flops 400000000 | bytes 500000 | tf_op jit(solution)/shard_map/select/pallas_call | solution.py:378
  33.1 3.9 %all-to-all-start.3 = ((bf16[32,32,128]{2,1,0:T(8,128)(2,1)}), bf16[32,32,128]{2,1,0:T(8,128)(2,1)S(1)}, u32[]{:S(2)}, u32[]{:S(2)}) async-start(bf16[32,32,128]{2,1,0:T(8,128)(2,1)} %select.2), calls=%async_computation.3 | async-start | bytes 524288 | tf_op jit(solution)/shard_map/all_to_all | solution.py:493
  37.1 3.0 %near.1 = (bf16[32,40,128]{2,1,0:T(8,128)(2,1)}, f32[4,32,128]{2,1,0:T(8,128)S(1)}, f32[4,128]{1,0:T(4,128)S(1)}) custom-call(s32[4]{0:T(128)S(1)} %copy-done.10, bf16[32,32,128]{2,1,0:T(8,128)(2,1)} %all-to-all-done.2.q_ref.refs_0_, bf16[512,256]{1,0:T(8,128)(2,1)S(1)} %copy-done.2, bf16[512,256]{1,0:T(8,128)(2,1)S(1)} %copy-done.3, ...), custom_call_target="tpu_custom_call" | custom-call | flops 3200000000 | bytes 4000000 | tf_op jit(solution)/shard_map/near/pallas_call | solution.py:378
  40.0 2.7 %all-to-all-done.3.refs_0_ = bf16[32,32,128]{2,1,0:T(8,128)(2,1)S(1)} async-done(((bf16[32,32,128]{2,1,0:T(8,128)(2,1)}), bf16[32,32,128]{2,1,0:T(8,128)(2,1)S(1)}, u32[]{:S(2)}, u32[]{:S(2)}) %all-to-all-start.3) | async-done | bytes 262176 | tf_op jit(solution)/shard_map/all_to_all | solution.py:493
  42.8 3.9 %prefix.2 = bf16[32,40,128]{2,1,0:T(8,128)(2,1)} custom-call(s32[9,33]{1,0:T(8,128)S(1)} %get-tuple-element.152.plan, bf16[32,32,128]{2,1,0:T(8,128)(2,1)S(1)} %all-to-all-done.3.refs_0_, bf16[1024,256]{1,0:T(8,128)(2,1)} %refs_1_.1, bf16[1024,256]{1,0:T(8,128)(2,1)} %collective-permute-done.4.refs_2_, bf16[1024,256]{1,0:T(8,128)(2,1)} %refs_3_.1, ...), custom_call_target="tpu_custom_call" | custom-call | flops 1600000000 | bytes 2000000 | tf_op jit(solution)/shard_map/prefix/pallas_call | solution.py:378
  46.7 0.5 collective-permute-start.6
  47.8 0.7 while.10
  48.5 4.9 %all-to-all-start.4 = ((bf16[32,40,128]{2,1,0:T(8,128)(2,1)}), bf16[32,40,128]{2,1,0:T(8,128)(2,1)S(1)}, u32[]{:S(2)}, u32[]{:S(2)}) async-start(bf16[32,40,128]{2,1,0:T(8,128)(2,1)} %prefix.2), calls=%async_computation.4 | async-start | bytes 655360 | tf_op jit(solution)/shard_map/all_to_all | solution.py:506
  53.4 8.3 %far.1 = bf16[32,40,128]{2,1,0:T(8,128)(2,1)S(1)} custom-call(bf16[32,32,128]{2,1,0:T(8,128)(2,1)} %all-to-all-done.2.q_ref.refs_0_, bf16[512,256]{1,0:T(8,128)(2,1)S(1)} %collective-permute-done.6.refs_0_, bf16[512,256]{1,0:T(8,128)(2,1)S(1)} %collective-permute-done.7.refs_1_, bf16[512,256]{1,0:T(8,128)(2,1)S(1)} %collective-permute-done.refs_2_, ...), custom_call_target="tpu_custom_call" | custom-call | flops 4800000000 | bytes 6000000 | tf_op jit(solution)/shard_map/far/pallas_call | solution.py:378
  61.8 1.4 %merge_row.1 = bf16[32,40,128]{2,1,0:T(8,128)(2,1)S(1)} custom-call(s32[9,33]{1,0:T(8,128)S(1)} %get-tuple-element.198, bf16[32,40,128]{2,1,0:T(8,128)(2,1)S(1)} %get-tuple-element.75.near, bf16[32,40,128]{2,1,0:T(8,128)(2,1)S(1)} %far.1, bf16[32,40,128]{2,1,0:T(8,128)(2,1)S(1)} %all-to-all-done.4.back, f32[4,32,128]{2,1,0:T(8,128)S(1)} %get-tuple-element.82.share_ref, ...), custom_call_target="tpu_custom_call" | custom-call | flops 1200000000 | bytes 1500000 | tf_op jit(solution)/shard_map/merge_row/pallas_call | solution.py:378
  63.2 18.5 %all_to_all.30 = bf16[32,40,128]{2,1,0:T(8,128)(2,1)S(1)} all-to-all(bf16[32,40,128]{2,1,0:T(8,128)(2,1)S(1)} %merge_row.1), channel_id=1, replica_groups=mesh['x'=4,'z'=8,'c'=2,'y'=4] {'z','y'}, dimensions={0} | all-to-all | bytes 655360 | tf_op jit(solution)/shard_map/all_to_all | solution.py:545
  82.0 0.7 reshape.22
  (50 shorter events, 2.2 us)
Async XLA Ops:
  0.0 22.2 %collective-permute-start = (bf16[512,256]{1,0:T(8,128)(2,1)}, bf16[512,256]{1,0:T(8,128)(2,1)S(1)}, u32[]{:S(2)}, u32[]{:S(2)}) collective-permute-start(bf16[512,256]{1,0:T(8,128)(2,1)} %k.1), channel_id=1, source_target_pairs={{0,64},{64,128},{128,192},{192,0},{1,65},{65,129},{129,193},{193,1... | collective-permute-start | bytes 786440 | tf_op jit(solution)/shard_map/ppermute | solution.py:394
  1.5 20.7 %collective-permute-start.1 = (bf16[512,256]{1,0:T(8,128)(2,1)}, bf16[512,256]{1,0:T(8,128)(2,1)S(1)}, u32[]{:S(2)}, u32[]{:S(2)}) collective-permute-start(bf16[512,256]{1,0:T(8,128)(2,1)} %v.1), channel_id=1, source_target_pairs={{0,64},{64,128},{128,192},{192,0},{1,65},{65,129},{129,193},{193,1... | collective-permute-start | bytes 786440 | tf_op jit(solution)/shard_map/ppermute | solution.py:394
  2.7 19.5 %collective-permute-start.2 = (bf16[512,256]{1,0:T(8,128)(2,1)}, bf16[512,256]{1,0:T(8,128)(2,1)}, u32[]{:S(2)}, u32[]{:S(2)}) collective-permute-start(bf16[512,256]{1,0:T(8,128)(2,1)} %k.1), channel_id=1, source_target_pairs={{0,192},{64,0},{128,64},{192,128},{1,193},{65,1},{129,65},{193,129... | collective-permute-start | bytes 786440 | tf_op jit(solution)/shard_map/ppermute | solution.py:394
  3.5 18.7 %collective-permute-start.3 = (bf16[512,256]{1,0:T(8,128)(2,1)}, bf16[512,256]{1,0:T(8,128)(2,1)}, u32[]{:S(2)}, u32[]{:S(2)}) collective-permute-start(bf16[512,256]{1,0:T(8,128)(2,1)} %v.1), channel_id=1, source_target_pairs={{0,192},{64,0},{128,64},{192,128},{1,193},{65,1},{129,65},{193,129... | collective-permute-start | bytes 786440 | tf_op jit(solution)/shard_map/ppermute | solution.py:394
  7.3 23.4 %all-to-all-start.2 = ((bf16[32,32,128]{2,1,0:T(8,128)(2,1)}), bf16[32,32,128]{2,1,0:T(8,128)(2,1)}, u32[]{:S(2)}, u32[]{:S(2)}) async-start(bf16[32,32,128]{2,1,0:T(8,128)(2,1)} %bitcast.3), calls=%async_computation.2 | async-start | bytes 524288 | tf_op jit(solution)/shard_map/all_to_all | solution.py:418
  19.3 17.7 %copy-start.1 = (bf16[4,512,256]{2,1,0:T(8,128)(2,1)S(1)}, bf16[4,512,256]{2,1,0:T(8,128)(2,1)}, u32[]{:S(2)}) copy-start(bf16[4,512,256]{2,1,0:T(8,128)(2,1)} %wv.1) | copy-start | bytes 3145732
  22.2 14.9 %copy-start = (bf16[4,512,256]{2,1,0:T(8,128)(2,1)S(1)}, bf16[4,512,256]{2,1,0:T(8,128)(2,1)}, u32[]{:S(2)}) copy-start(bf16[4,512,256]{2,1,0:T(8,128)(2,1)} %wk.1) | copy-start | bytes 3145732
  22.2 10.3 %collective-permute-start.4 = (bf16[1024,256]{1,0:T(8,128)(2,1)}, bf16[1024,256]{1,0:T(8,128)(2,1)}, u32[]{:S(2)}, u32[]{:S(2)}) collective-permute-start(bf16[1024,256]{1,0:T(8,128)(2,1)} %refs_1_.1), channel_id=1, source_target_pairs={{0,4},{4,0},{1,5},{5,1},{2,6},{6,2},{3,7},{7,3},{8,12},{12,8},{9,1... | collective-permute-start | bytes 1572872 | tf_op jit(solution)/shard_map/ppermute | solution.py:394
  22.3 10.3 %collective-permute-start.5 = (bf16[1024,256]{1,0:T(8,128)(2,1)}, bf16[1024,256]{1,0:T(8,128)(2,1)}, u32[]{:S(2)}, u32[]{:S(2)}) collective-permute-start(bf16[1024,256]{1,0:T(8,128)(2,1)} %refs_3_.1), channel_id=1, source_target_pairs={{0,4},{4,0},{1,5},{5,1},{2,6},{6,2},{3,7},{7,3},{8,12},{12,8},{9,1... | collective-permute-start | bytes 1572872 | tf_op jit(solution)/shard_map/ppermute | solution.py:394
  22.8 23.9 %collective-permute-start.13 = (bf16[512,256]{1,0:T(8,128)(2,1)}, bf16[512,256]{1,0:T(8,128)(2,1)}, u32[]{:S(2)}, u32[]{:S(2)}) collective-permute-start(bf16[512,256]{1,0:T(8,128)(2,1)} %collective-permute-done.3.refs_7_), channel_id=1, source_target_pairs={{0,192},{64,0},{128,64},{192,128},{1,193},{65,1},{129,65},{193,129... | collective-permute-start | bytes 786440 | tf_op jit(solution)/shard_map/ppermute | solution.py:394
  23.3 23.8 %collective-permute-start.11 = (bf16[512,256]{1,0:T(8,128)(2,1)}, bf16[512,256]{1,0:T(8,128)(2,1)}, u32[]{:S(2)}, u32[]{:S(2)}) collective-permute-start(bf16[512,256]{1,0:T(8,128)(2,1)} %collective-permute-done.3.refs_7_), channel_id=1, source_target_pairs={{0,4},{4,0},{1,5},{5,1},{2,6},{6,2},{3,7},{7,3},{8,12},{12,8},{9,1... | collective-permute-start | bytes 786440 | tf_op jit(solution)/shard_map/ppermute | solution.py:394
  23.3 23.3 %collective-permute-start.12 = (bf16[512,256]{1,0:T(8,128)(2,1)S(1)}, bf16[512,256]{1,0:T(8,128)(2,1)}, u32[]{:S(2)}, u32[]{:S(2)}) collective-permute-start(bf16[512,256]{1,0:T(8,128)(2,1)S(1)} %collective-permute-done.refs_2_), channel_id=1, source_target_pairs={{0,64},{64,128},{128,192},{192,0},{1,65},{65,129},{129,193},{193,1... | collective-permute-start | bytes 786440 | tf_op jit(solution)/shard_map/ppermute | solution.py:394
  30.7 6.3 %copy-start.7 = (bf16[4,256]{1,0:T(4,128)(2,1)S(1)}, bf16[4,256]{1,0:T(4,128)(2,1)}, u32[]{:S(2)}) copy-start(bf16[4,256]{1,0:T(4,128)(2,1)} %nv.1) | copy-start | bytes 6148
  30.7 6.3 %copy-start.10 = (s32[4]{0:T(128)S(1)}, s32[4]{0:T(128)}, u32[]{:S(2)}) copy-start(s32[4]{0:T(128)} %length_ref.1) | copy-start | bytes 52
  32.5 14.8 %collective-permute-start.8 = (bf16[512,256]{1,0:T(8,128)(2,1)S(1)}, bf16[512,256]{1,0:T(8,128)(2,1)}, u32[]{:S(2)}, u32[]{:S(2)}) collective-permute-start(bf16[512,256]{1,0:T(8,128)(2,1)S(1)} %collective-permute-done.refs_2_), channel_id=1, source_target_pairs={{0,4},{4,0},{1,5},{5,1},{2,6},{6,2},{3,7},{7,3},{8,12},{12,8},{9,1... | collective-permute-start | bytes 786440 | tf_op jit(solution)/shard_map/ppermute | solution.py:394
  32.6 15.1 %collective-permute-start.10 = (bf16[512,256]{1,0:T(8,128)(2,1)}, bf16[512,256]{1,0:T(8,128)(2,1)}, u32[]{:S(2)}, u32[]{:S(2)}) collective-permute-start(bf16[512,256]{1,0:T(8,128)(2,1)} %collective-permute-done.2.refs_6_), channel_id=1, source_target_pairs={{0,4},{4,0},{1,5},{5,1},{2,6},{6,2},{3,7},{7,3},{8,12},{12,8},{9,1... | collective-permute-start | bytes 786440 | tf_op jit(solution)/shard_map/ppermute | solution.py:394
  33.1 9.7 %all-to-all-start.3 = ((bf16[32,32,128]{2,1,0:T(8,128)(2,1)}), bf16[32,32,128]{2,1,0:T(8,128)(2,1)S(1)}, u32[]{:S(2)}, u32[]{:S(2)}) async-start(bf16[32,32,128]{2,1,0:T(8,128)(2,1)} %select.2), calls=%async_computation.3 | async-start | bytes 524288 | tf_op jit(solution)/shard_map/all_to_all | solution.py:493
  40.0 7.8 %copy-start.11 = (bf16[32,40,128]{2,1,0:T(8,128)(2,1)S(1)}, bf16[32,40,128]{2,1,0:T(8,128)(2,1)}, u32[]{:S(2)}) copy-start(bf16[32,40,128]{2,1,0:T(8,128)(2,1)} %get-tuple-element.150) | copy-start | bytes 983044
  46.6 6.8 %collective-permute-start.9 = (bf16[512,256]{1,0:T(8,128)(2,1)S(1)}, bf16[512,256]{1,0:T(8,128)(2,1)S(1)}, u32[]{:S(2)}, u32[]{:S(2)}) collective-permute-start(bf16[512,256]{1,0:T(8,128)(2,1)S(1)} %collective-permute-done.1.refs_3_), channel_id=1, source_target_pairs={{0,4},{4,0},{1,5},{5,1},{2,6},{6,2},{3,7},{7,3},{8,12},{12,8},{9,1... | collective-permute-start | bytes 786440 | tf_op jit(solution)/shard_map/ppermute | solution.py:394
  46.7 6.8 %collective-permute-start.6 = (bf16[512,256]{1,0:T(8,128)(2,1)S(1)}, bf16[512,256]{1,0:T(8,128)(2,1)S(1)}, u32[]{:S(2)}, u32[]{:S(2)}) collective-permute-start(bf16[512,256]{1,0:T(8,128)(2,1)S(1)} %copy-done.2), channel_id=1, source_target_pairs={{0,4},{4,0},{1,5},{5,1},{2,6},{6,2},{3,7},{7,3},{8,12},{12,8},{9,1... | collective-permute-start | bytes 786440 | tf_op jit(solution)/shard_map/ppermute | solution.py:394
  47.2 6.3 %collective-permute-start.7 = (bf16[512,256]{1,0:T(8,128)(2,1)S(1)}, bf16[512,256]{1,0:T(8,128)(2,1)S(1)}, u32[]{:S(2)}, u32[]{:S(2)}) collective-permute-start(bf16[512,256]{1,0:T(8,128)(2,1)S(1)} %copy-done.3), channel_id=1, source_target_pairs={{0,4},{4,0},{1,5},{5,1},{2,6},{6,2},{3,7},{7,3},{8,12},{12,8},{9,1... | collective-permute-start | bytes 786440 | tf_op jit(solution)/shard_map/ppermute | solution.py:394
  47.3 6.2 %collective-permute-start.14 = (bf16[512,256]{1,0:T(8,128)(2,1)}, bf16[512,256]{1,0:T(8,128)(2,1)S(1)}, u32[]{:S(2)}, u32[]{:S(2)}) collective-permute-start(bf16[512,256]{1,0:T(8,128)(2,1)} %collective-permute-done.12.refs_10_), channel_id=1, source_target_pairs={{0,4},{4,0},{1,5},{5,1},{2,6},{6,2},{3,7},{7,3},{8,12},{12,8},{9,1... | collective-permute-start | bytes 786440 | tf_op jit(solution)/shard_map/ppermute | solution.py:394
  47.7 5.8 %collective-permute-start.15 = (bf16[512,256]{1,0:T(8,128)(2,1)}, bf16[512,256]{1,0:T(8,128)(2,1)S(1)}, u32[]{:S(2)}, u32[]{:S(2)}) collective-permute-start(bf16[512,256]{1,0:T(8,128)(2,1)} %collective-permute-done.13.refs_11_), channel_id=1, source_target_pairs={{0,4},{4,0},{1,5},{5,1},{2,6},{6,2},{3,7},{7,3},{8,12},{12,8},{9,1... | collective-permute-start | bytes 786440 | tf_op jit(solution)/shard_map/ppermute | solution.py:394
  48.5 13.3 %all-to-all-start.4 = ((bf16[32,40,128]{2,1,0:T(8,128)(2,1)}), bf16[32,40,128]{2,1,0:T(8,128)(2,1)S(1)}, u32[]{:S(2)}, u32[]{:S(2)}) async-start(bf16[32,40,128]{2,1,0:T(8,128)(2,1)} %prefix.2), calls=%async_computation.4 | async-start | bytes 655360 | tf_op jit(solution)/shard_map/all_to_all | solution.py:506
  (7 other events, 29.4 us)

commit v7 on v4

--- a/solution.py
+++ b/solution.py
@@ -136,9 +136,7 @@
             lanes = slice(g * HD, (g + 1) * HD)
             query = q_ref[chats, heads, :].reshape(rows * GROUP, HD)
             scores = [scores_of(query, k[:, lanes]) for k, _ in blocks]
-            peak = functools.reduce(
-                jnp.maximum, [jnp.max(s, axis=1, keepdims=True) for s in scores]
-            )
+            peak = jnp.max(functools.reduce(jnp.maximum, scores), axis=1, keepdims=True)
             numer = None
             for n, s in enumerate(scores):
                 weights = jnp.exp2((s - peak) * SCALE2).astype(BF16)
@@ -281,6 +279,8 @@
 
 
 def place_answers(plan, start, back, out):
+    row = iota((COLUMN, ROWS, HD), 1)
+    out[...] = jnp.where(row == HEADS, FLOOR, 0.0).astype(BF16)
     for t in range(NX):
 
         def place(e, _, t=t):
@@ -288,11 +288,6 @@
             return 0
 
         lax.fori_loop(0, jnp.clip(plan[2 * NX, t] - start, 0, ROOM), place, 0)
-
-
-def scatter_kernel(plan, turn, back, before, out):
-    out[...] = before[...]
-    place_answers(plan, turn[0] * ROOM, back, out)
 
 
 def weights_of(levels):
@@ -320,9 +315,20 @@
     return dot(high, shares) + dot(low, shares)
 
 
-def merge_row_kernel(plan, near, far, back, before, share_ref, level_ref, out, prefix, lines, levels):
+def more_kernel(plan, turn, back, before, out, prefix):
     diagonal = head_diagonal()
-    prefix[...] = before[...]
+    place_answers(plan, turn[0] * ROOM, back, prefix)
+    weights, total = weights_of([read_level(r) for r in (before, prefix)])
+    line = four_lines(weights)
+    out[:, HEADS:, :] = level_parts(total)
+    empty = jnp.zeros((2 * HEADS, HD), BF16)
+    for i in range(COLUMN):
+        shares = jnp.concatenate([before[i, :HEADS, :], prefix[i, :HEADS, :], empty], axis=0)
+        out[i, :HEADS, :] = mix(diagonal, line[i : i + 1], shares).astype(BF16)
+
+
+def merge_row_kernel(plan, near, far, back, share_ref, level_ref, out, prefix, levels):
+    diagonal = head_diagonal()
     place_answers(plan, 0, back, prefix)
     level = [read_level(r) for r in (near, far, prefix)]
     weights, total = weights_of(level)
@@ -504,20 +510,19 @@
 
     def more(state):
         turn, before = state
-        after = scalar_kernel(
-            scatter_kernel,
-            "scatter",
+        after = kernel(
+            more_kernel,
+            "more",
             shaped(COLUMN, ROWS, HD),
-            turn,
-            [prefix_answers(turn, prefix_picked(turn)), before],
+            [plan, turn, prefix_answers(turn, prefix_picked(turn)), before],
+            scalars=2,
+            scratch=[pltpu.VMEM((COLUMN, ROWS, HD), BF16)],
         )
         return turn + 1, after
 
-    row = lax.broadcasted_iota(i32, (COLUMN, ROWS, HD), 1)
-    none = jnp.where(row == HEADS, FLOOR, 0.0).astype(BF16)
     answers = prefix_answers(0, picked)
-    _, later = lax.while_loop(
-        lambda state: state[0][0] < rounds[0], more, (jnp.ones((1,), i32), none)
+    _, near = lax.while_loop(
+        lambda state: state[0][0] < rounds[0], more, (jnp.ones((1,), i32), near)
     )
     far = kernel(
         far_kernel,
@@ -532,11 +537,10 @@
         merge_row_kernel,
         "merge_row",
         shaped(COLUMN, ROWS, HD),
-        [plan, near, far, answers, later, home_share, home_level],
+        [plan, near, far, answers, home_share, home_level],
         scalars=1,
         scratch=[
             pltpu.VMEM((COLUMN, ROWS, HD), BF16),
-            pltpu.VMEM((COLUMN, HD), F32),
             pltpu.VMEM((3, COLUMN, HD), F32),
         ],
         us=1.5,

time: 84.5 us -> 82.9 us (0.981)
  local copies, waits for them, and re-layouts: 3.68 us -> 2.12 us
  transfers between devices with their start and end apart: 19 -> 19, of which waited for: 2 -> 2; matrix products, arithmetic and copies ran while one was open for 3% -> 2% of each run, Pallas kernels for 22% -> 23%
where the time goes in v7:
time: 82.9 us; the launch traced here: 82.2 us
  starting transfers between devices  30 us (36%)
  Pallas kernels  20.2 us (24%)
  blocking collectives  19.1 us (23%)
  waiting for transfers between devices  8.72 us (11%)
  local copies, waits for them, and re-layouts  2.12 us (3%)
  other arithmetic  1.02 us (1%)
    pallas_call x7, Pallas kernels, kernel(): pl.pallas_call(body, out_shape=outs, in_specs=in_specs or [SMEM] * scalar...  20.2 us
    all_to_all x1, blocking collectives, local(): lax.all_to_all(merged, ('z', 'y'), split_axis=0, concat_axis=0, tiled=True)  19.1 us
    all_to_all x1, starting transfers between devices, local(): lax.all_to_all(spread.reshape(COLUMN, HEADS, HD), ('z', 'y'), split_axis=...  11.3 us
    ppermute x16, starting transfers between devices, send(): lax.ppermute(array, axis, [(i, (i + shift) % size) for i in range(size)])  9.85 us
    all_to_all x1, waiting for transfers between devices, local(): lax.all_to_all(spread.reshape(COLUMN, HEADS, HD), ('z', 'y'), split_axis=...  5.88 us
    all_to_all x1, starting transfers between devices, prefix_answers(): return lax.all_to_all(answer, 'x', split_axis=0, concat_axis=0, tiled=True)  4.91 us
    all_to_all x1, starting transfers between devices, prefix_answers(): asked = lax.all_to_all(picked, 'x', split_axis=0, concat_axis=0, tiled=True)  3.91 us
    all_to_all x1, waiting for transfers between devices, prefix_answers(): asked = lax.all_to_all(picked, 'x', split_axis=0, concat_axis=0, tiled=True)  2.8 us
  transfers between devices with their start and end apart: 19, of which 2 were waited for; matrix products, arithmetic and copies ran while one was open for 2% of the time, Pallas kernels for 23%

profile of v7, /device:TPU:2, one launch (start us, length us, event | category | flops | bytes accessed | tf_op | source)
XLA Modules:
  0.0 82.2 jit_solution(4464877689571097336)
XLA Ops:
  0.0 1.5 %collective-permute-start = (bf16[512,256]{1,0:T(8,128)(2,1)}, bf16[512,256]{1,0:T(8,128)(2,1)S(1)}, u32[]{:S(2)}, u32[]{:S(2)}) collective-permute-start(bf16[512,256]{1,0:T(8,128)(2,1)} %k.1), channel_id=1, source_target_pairs={{0,64},{64,128},{128,192},{192,0},{1,65},{65,129},{129,193},{193,1... | collective-permute-start | bytes 786440 | tf_op jit(solution)/shard_map/ppermute | solution.py:397
  1.5 1.2 %collective-permute-start.1 = (bf16[512,256]{1,0:T(8,128)(2,1)}, bf16[512,256]{1,0:T(8,128)(2,1)S(1)}, u32[]{:S(2)}, u32[]{:S(2)}) collective-permute-start(bf16[512,256]{1,0:T(8,128)(2,1)} %v.1), channel_id=1, source_target_pairs={{0,64},{64,128},{128,192},{192,0},{1,65},{65,129},{129,193},{193,1... | collective-permute-start | bytes 786440 | tf_op jit(solution)/shard_map/ppermute | solution.py:397
  2.7 0.8 %collective-permute-start.2 = (bf16[512,256]{1,0:T(8,128)(2,1)}, bf16[512,256]{1,0:T(8,128)(2,1)}, u32[]{:S(2)}, u32[]{:S(2)}) collective-permute-start(bf16[512,256]{1,0:T(8,128)(2,1)} %k.1), channel_id=1, source_target_pairs={{0,192},{64,0},{128,64},{192,128},{1,193},{65,1},{129,65},{193,129... | collective-permute-start | bytes 786440 | tf_op jit(solution)/shard_map/ppermute | solution.py:397
  3.5 2.0 %collective-permute-start.3 = (bf16[512,256]{1,0:T(8,128)(2,1)}, bf16[512,256]{1,0:T(8,128)(2,1)}, u32[]{:S(2)}, u32[]{:S(2)}) collective-permute-start(bf16[512,256]{1,0:T(8,128)(2,1)} %v.1), channel_id=1, source_target_pairs={{0,192},{64,0},{128,64},{192,128},{1,193},{65,1},{129,65},{193,129... | collective-permute-start | bytes 786440 | tf_op jit(solution)/shard_map/ppermute | solution.py:397
  5.5 1.0 %reduce = bf16[16384]{0:T(1024)(128)(2,1)S(1)} reduce(bf16[1,16384]{1,0:T(2,128)(2,1)} %param.16, bf16[]{:T(256)} %constant.12), dimensions={0}, to_apply=%param.16.reduce_sub_computation | reduce | bytes 65538 | tf_op args[0]
  6.6 0.7 broadcast_in_dim.8
  7.3 11.3 %all-to-all-start.2 = ((bf16[32,32,128]{2,1,0:T(8,128)(2,1)}), bf16[32,32,128]{2,1,0:T(8,128)(2,1)}, u32[]{:S(2)}, u32[]{:S(2)}) async-start(bf16[32,32,128]{2,1,0:T(8,128)(2,1)} %bitcast.3), calls=%async_computation.2 | async-start | bytes 524288 | tf_op jit(solution)/shard_map/all_to_all | solution.py:421
  18.7 0.7 copy-done.8
  19.3 2.8 %prepare.1 = (s32[9,33]{1,0:T(8,128)S(1)}, s32[1]{0:T(128)}) custom-call(s32[256]{0:T(256)S(1)} %copy-done.8, s32[64]{0:T(128)S(1)} %copy-done.9, s32[1,256]{1,0:T(1,128)S(1)} %bitcast.8, s32[1,64]{1,0:T(1,128)S(1)} %bitcast.9), custom_call_target="tpu_custom_call" | custom-call | flops 1600000000 | bytes 2000000 | tf_op jit(solution)/shard_map/prepare/pallas_call | solution.py:381
  22.8 0.5 collective-permute-start.13
  23.3 1.5 %collective-permute-start.12 = (bf16[512,256]{1,0:T(8,128)(2,1)S(1)}, bf16[512,256]{1,0:T(8,128)(2,1)}, u32[]{:S(2)}, u32[]{:S(2)}) collective-permute-start(bf16[512,256]{1,0:T(8,128)(2,1)S(1)} %collective-permute-done.refs_2_), channel_id=1, source_target_pairs={{0,64},{64,128},{128,192},{192,0},{1,65},{65,129},{129,193},{193,1... | collective-permute-start | bytes 786440 | tf_op jit(solution)/shard_map/ppermute | solution.py:397
  24.8 5.9 %all-to-all-done.2.q_ref.refs_0_ = bf16[32,32,128]{2,1,0:T(8,128)(2,1)} async-done(((bf16[32,32,128]{2,1,0:T(8,128)(2,1)}), bf16[32,32,128]{2,1,0:T(8,128)(2,1)}, u32[]{:S(2)}, u32[]{:S(2)}) %all-to-all-start.2) | async-done | bytes 262176 | tf_op jit(solution)/shard_map/all_to_all | solution.py:421
  30.7 1.7 %select.2 = bf16[32,32,128]{2,1,0:T(8,128)(2,1)} custom-call(s32[9,33]{1,0:T(8,128)S(1)} %get-tuple-element.152.plan, bf16[32,32,128]{2,1,0:T(8,128)(2,1)} %all-to-all-done.2.q_ref.refs_0_), custom_call_target="tpu_custom_call" | custom-call | flops 400000000 | bytes 500000 | tf_op jit(solution)/shard_map/select/pallas_call | solution.py:381
  33.1 3.9 %all-to-all-start.3 = ((bf16[32,32,128]{2,1,0:T(8,128)(2,1)}), bf16[32,32,128]{2,1,0:T(8,128)(2,1)S(1)}, u32[]{:S(2)}, u32[]{:S(2)}) async-start(bf16[32,32,128]{2,1,0:T(8,128)(2,1)} %select.2), calls=%async_computation.3 | async-start | bytes 524288 | tf_op jit(solution)/shard_map/all_to_all | solution.py:496
  37.1 2.9 %near.1 = (bf16[32,40,128]{2,1,0:T(8,128)(2,1)}, f32[4,32,128]{2,1,0:T(8,128)S(1)}, f32[4,128]{1,0:T(4,128)S(1)}) custom-call(s32[4]{0:T(128)S(1)} %copy-done.10, bf16[32,32,128]{2,1,0:T(8,128)(2,1)} %all-to-all-done.2.q_ref.refs_0_, bf16[512,256]{1,0:T(8,128)(2,1)S(1)} %copy-done.2, bf16[512,256]{1,0:T(8,128)(2,1)S(1)} %copy-done.3, ...), custom_call_target="tpu_custom_call" | custom-call | flops 3200000000 | bytes 4000000 | tf_op jit(solution)/shard_map/near/pallas_call | solution.py:381
  40.0 2.8 %all-to-all-done.3.refs_0_ = bf16[32,32,128]{2,1,0:T(8,128)(2,1)S(1)} async-done(((bf16[32,32,128]{2,1,0:T(8,128)(2,1)}), bf16[32,32,128]{2,1,0:T(8,128)(2,1)S(1)}, u32[]{:S(2)}, u32[]{:S(2)}) %all-to-all-start.3) | async-done | bytes 262176 | tf_op jit(solution)/shard_map/all_to_all | solution.py:496
  42.8 3.9 %prefix.2 = bf16[32,40,128]{2,1,0:T(8,128)(2,1)} custom-call(s32[9,33]{1,0:T(8,128)S(1)} %get-tuple-element.152.plan, bf16[32,32,128]{2,1,0:T(8,128)(2,1)S(1)} %all-to-all-done.3.refs_0_, bf16[1024,256]{1,0:T(8,128)(2,1)} %refs_1_.1, bf16[1024,256]{1,0:T(8,128)(2,1)} %collective-permute-done.4.refs_2_, bf16[1024,256]{1,0:T(8,128)(2,1)} %refs_3_.1, ...), custom_call_target="tpu_custom_call" | custom-call | flops 1600000000 | bytes 2000000 | tf_op jit(solution)/shard_map/prefix/pallas_call | solution.py:381
  46.7 0.5 collective-permute-start.6
  47.8 0.7 while.10
  48.5 4.9 %all-to-all-start.4 = ((bf16[32,40,128]{2,1,0:T(8,128)(2,1)}), bf16[32,40,128]{2,1,0:T(8,128)(2,1)S(1)}, u32[]{:S(2)}, u32[]{:S(2)}) async-start(bf16[32,40,128]{2,1,0:T(8,128)(2,1)} %prefix.2), calls=%async_computation.4 | async-start | bytes 655360 | tf_op jit(solution)/shard_map/all_to_all | solution.py:509
  53.4 7.2 %far.1 = bf16[32,40,128]{2,1,0:T(8,128)(2,1)S(1)} custom-call(bf16[32,32,128]{2,1,0:T(8,128)(2,1)} %all-to-all-done.2.q_ref.refs_0_, bf16[512,256]{1,0:T(8,128)(2,1)S(1)} %collective-permute-done.6.refs_0_, bf16[512,256]{1,0:T(8,128)(2,1)S(1)} %collective-permute-done.7.refs_1_, bf16[512,256]{1,0:T(8,128)(2,1)S(1)} %collective-permute-done.refs_2_, ...), custom_call_target="tpu_custom_call" | custom-call | flops 4800000000 | bytes 6000000 | tf_op jit(solution)/shard_map/far/pallas_call | solution.py:381
  60.7 1.4 %merge_row.1 = bf16[32,40,128]{2,1,0:T(8,128)(2,1)S(1)} custom-call(s32[9,33]{1,0:T(8,128)S(1)} %get-tuple-element.198, bf16[32,40,128]{2,1,0:T(8,128)(2,1)S(1)} %get-tuple-element.75.near, bf16[32,40,128]{2,1,0:T(8,128)(2,1)S(1)} %far.1, bf16[32,40,128]{2,1,0:T(8,128)(2,1)S(1)} %all-to-all-done.4.back, f32[4,32,128]{2,1,0:T(8,128)S(1)} %get-tuple-element.82.share_ref, ...), custom_call_target="tpu_custom_call" | custom-call | flops 1200000000 | bytes 1500000 | tf_op jit(solution)/shard_map/merge_row/pallas_call | solution.py:381
  62.1 19.1 %all_to_all.30 = bf16[32,40,128]{2,1,0:T(8,128)(2,1)S(1)} all-to-all(bf16[32,40,128]{2,1,0:T(8,128)(2,1)S(1)} %merge_row.1), channel_id=1, replica_groups=mesh['x'=4,'z'=8,'c'=2,'y'=4] {'z','y'}, dimensions={0} | all-to-all | bytes 655360 | tf_op jit(solution)/shard_map/all_to_all | solution.py:548
  81.5 0.7 reshape.22
  (50 shorter events, 2.2 us)
Async XLA Ops:
  0.0 22.2 %collective-permute-start = (bf16[512,256]{1,0:T(8,128)(2,1)}, bf16[512,256]{1,0:T(8,128)(2,1)S(1)}, u32[]{:S(2)}, u32[]{:S(2)}) collective-permute-start(bf16[512,256]{1,0:T(8,128)(2,1)} %k.1), channel_id=1, source_target_pairs={{0,64},{64,128},{128,192},{192,0},{1,65},{65,129},{129,193},{193,1... | collective-permute-start | bytes 786440 | tf_op jit(solution)/shard_map/ppermute | solution.py:397
  1.5 20.7 %collective-permute-start.1 = (bf16[512,256]{1,0:T(8,128)(2,1)}, bf16[512,256]{1,0:T(8,128)(2,1)S(1)}, u32[]{:S(2)}, u32[]{:S(2)}) collective-permute-start(bf16[512,256]{1,0:T(8,128)(2,1)} %v.1), channel_id=1, source_target_pairs={{0,64},{64,128},{128,192},{192,0},{1,65},{65,129},{129,193},{193,1... | collective-permute-start | bytes 786440 | tf_op jit(solution)/shard_map/ppermute | solution.py:397
  2.7 19.5 %collective-permute-start.2 = (bf16[512,256]{1,0:T(8,128)(2,1)}, bf16[512,256]{1,0:T(8,128)(2,1)}, u32[]{:S(2)}, u32[]{:S(2)}) collective-permute-start(bf16[512,256]{1,0:T(8,128)(2,1)} %k.1), channel_id=1, source_target_pairs={{0,192},{64,0},{128,64},{192,128},{1,193},{65,1},{129,65},{193,129... | collective-permute-start | bytes 786440 | tf_op jit(solution)/shard_map/ppermute | solution.py:397
  3.5 18.7 %collective-permute-start.3 = (bf16[512,256]{1,0:T(8,128)(2,1)}, bf16[512,256]{1,0:T(8,128)(2,1)}, u32[]{:S(2)}, u32[]{:S(2)}) collective-permute-start(bf16[512,256]{1,0:T(8,128)(2,1)} %v.1), channel_id=1, source_target_pairs={{0,192},{64,0},{128,64},{192,128},{1,193},{65,1},{129,65},{193,129... | collective-permute-start | bytes 786440 | tf_op jit(solution)/shard_map/ppermute | solution.py:397
  7.3 23.4 %all-to-all-start.2 = ((bf16[32,32,128]{2,1,0:T(8,128)(2,1)}), bf16[32,32,128]{2,1,0:T(8,128)(2,1)}, u32[]{:S(2)}, u32[]{:S(2)}) async-start(bf16[32,32,128]{2,1,0:T(8,128)(2,1)} %bitcast.3), calls=%async_computation.2 | async-start | bytes 524288 | tf_op jit(solution)/shard_map/all_to_all | solution.py:421
  19.3 17.7 %copy-start.1 = (bf16[4,512,256]{2,1,0:T(8,128)(2,1)S(1)}, bf16[4,512,256]{2,1,0:T(8,128)(2,1)}, u32[]{:S(2)}) copy-start(bf16[4,512,256]{2,1,0:T(8,128)(2,1)} %wv.1) | copy-start | bytes 3145732
  22.2 14.9 %copy-start = (bf16[4,512,256]{2,1,0:T(8,128)(2,1)S(1)}, bf16[4,512,256]{2,1,0:T(8,128)(2,1)}, u32[]{:S(2)}) copy-start(bf16[4,512,256]{2,1,0:T(8,128)(2,1)} %wk.1) | copy-start | bytes 3145732
  22.2 10.3 %collective-permute-start.4 = (bf16[1024,256]{1,0:T(8,128)(2,1)}, bf16[1024,256]{1,0:T(8,128)(2,1)}, u32[]{:S(2)}, u32[]{:S(2)}) collective-permute-start(bf16[1024,256]{1,0:T(8,128)(2,1)} %refs_1_.1), channel_id=1, source_target_pairs={{0,4},{4,0},{1,5},{5,1},{2,6},{6,2},{3,7},{7,3},{8,12},{12,8},{9,1... | collective-permute-start | bytes 1572872 | tf_op jit(solution)/shard_map/ppermute | solution.py:397
  22.3 10.3 %collective-permute-start.5 = (bf16[1024,256]{1,0:T(8,128)(2,1)}, bf16[1024,256]{1,0:T(8,128)(2,1)}, u32[]{:S(2)}, u32[]{:S(2)}) collective-permute-start(bf16[1024,256]{1,0:T(8,128)(2,1)} %refs_3_.1), channel_id=1, source_target_pairs={{0,4},{4,0},{1,5},{5,1},{2,6},{6,2},{3,7},{7,3},{8,12},{12,8},{9,1... | collective-permute-start | bytes 1572872 | tf_op jit(solution)/shard_map/ppermute | solution.py:397
  22.8 23.9 %collective-permute-start.13 = (bf16[512,256]{1,0:T(8,128)(2,1)}, bf16[512,256]{1,0:T(8,128)(2,1)}, u32[]{:S(2)}, u32[]{:S(2)}) collective-permute-start(bf16[512,256]{1,0:T(8,128)(2,1)} %collective-permute-done.3.refs_7_), channel_id=1, source_target_pairs={{0,192},{64,0},{128,64},{192,128},{1,193},{65,1},{129,65},{193,129... | collective-permute-start | bytes 786440 | tf_op jit(solution)/shard_map/ppermute | solution.py:397
  23.3 23.8 %collective-permute-start.11 = (bf16[512,256]{1,0:T(8,128)(2,1)}, bf16[512,256]{1,0:T(8,128)(2,1)}, u32[]{:S(2)}, u32[]{:S(2)}) collective-permute-start(bf16[512,256]{1,0:T(8,128)(2,1)} %collective-permute-done.3.refs_7_), channel_id=1, source_target_pairs={{0,4},{4,0},{1,5},{5,1},{2,6},{6,2},{3,7},{7,3},{8,12},{12,8},{9,1... | collective-permute-start | bytes 786440 | tf_op jit(solution)/shard_map/ppermute | solution.py:397
  23.3 23.3 %collective-permute-start.12 = (bf16[512,256]{1,0:T(8,128)(2,1)S(1)}, bf16[512,256]{1,0:T(8,128)(2,1)}, u32[]{:S(2)}, u32[]{:S(2)}) collective-permute-start(bf16[512,256]{1,0:T(8,128)(2,1)S(1)} %collective-permute-done.refs_2_), channel_id=1, source_target_pairs={{0,64},{64,128},{128,192},{192,0},{1,65},{65,129},{129,193},{193,1... | collective-permute-start | bytes 786440 | tf_op jit(solution)/shard_map/ppermute | solution.py:397
  30.7 6.3 %copy-start.7 = (bf16[4,256]{1,0:T(4,128)(2,1)S(1)}, bf16[4,256]{1,0:T(4,128)(2,1)}, u32[]{:S(2)}) copy-start(bf16[4,256]{1,0:T(4,128)(2,1)} %nv.1) | copy-start | bytes 6148
  30.7 6.3 %copy-start.10 = (s32[4]{0:T(128)S(1)}, s32[4]{0:T(128)}, u32[]{:S(2)}) copy-start(s32[4]{0:T(128)} %length_ref.1) | copy-start | bytes 52
  32.5 14.8 %collective-permute-start.8 = (bf16[512,256]{1,0:T(8,128)(2,1)S(1)}, bf16[512,256]{1,0:T(8,128)(2,1)}, u32[]{:S(2)}, u32[]{:S(2)}) collective-permute-start(bf16[512,256]{1,0:T(8,128)(2,1)S(1)} %collective-permute-done.refs_2_), channel_id=1, source_target_pairs={{0,4},{4,0},{1,5},{5,1},{2,6},{6,2},{3,7},{7,3},{8,12},{12,8},{9,1... | collective-permute-start | bytes 786440 | tf_op jit(solution)/shard_map/ppermute | solution.py:397
  32.6 15.1 %collective-permute-start.10 = (bf16[512,256]{1,0:T(8,128)(2,1)}, bf16[512,256]{1,0:T(8,128)(2,1)}, u32[]{:S(2)}, u32[]{:S(2)}) collective-permute-start(bf16[512,256]{1,0:T(8,128)(2,1)} %collective-permute-done.2.refs_6_), channel_id=1, source_target_pairs={{0,4},{4,0},{1,5},{5,1},{2,6},{6,2},{3,7},{7,3},{8,12},{12,8},{9,1... | collective-permute-start | bytes 786440 | tf_op jit(solution)/shard_map/ppermute | solution.py:397
  33.1 9.7 %all-to-all-start.3 = ((bf16[32,32,128]{2,1,0:T(8,128)(2,1)}), bf16[32,32,128]{2,1,0:T(8,128)(2,1)S(1)}, u32[]{:S(2)}, u32[]{:S(2)}) async-start(bf16[32,32,128]{2,1,0:T(8,128)(2,1)} %select.2), calls=%async_computation.3 | async-start | bytes 524288 | tf_op jit(solution)/shard_map/all_to_all | solution.py:496
  40.0 7.8 %copy-start.11 = (bf16[32,40,128]{2,1,0:T(8,128)(2,1)S(1)}, bf16[32,40,128]{2,1,0:T(8,128)(2,1)}, u32[]{:S(2)}) copy-start(bf16[32,40,128]{2,1,0:T(8,128)(2,1)} %get-tuple-element.150) | copy-start | bytes 983044
  46.6 6.8 %collective-permute-start.9 = (bf16[512,256]{1,0:T(8,128)(2,1)S(1)}, bf16[512,256]{1,0:T(8,128)(2,1)S(1)}, u32[]{:S(2)}, u32[]{:S(2)}) collective-permute-start(bf16[512,256]{1,0:T(8,128)(2,1)S(1)} %collective-permute-done.1.refs_3_), channel_id=1, source_target_pairs={{0,4},{4,0},{1,5},{5,1},{2,6},{6,2},{3,7},{7,3},{8,12},{12,8},{9,1... | collective-permute-start | bytes 786440 | tf_op jit(solution)/shard_map/ppermute | solution.py:397
  46.7 6.7 %collective-permute-start.6 = (bf16[512,256]{1,0:T(8,128)(2,1)S(1)}, bf16[512,256]{1,0:T(8,128)(2,1)S(1)}, u32[]{:S(2)}, u32[]{:S(2)}) collective-permute-start(bf16[512,256]{1,0:T(8,128)(2,1)S(1)} %copy-done.2), channel_id=1, source_target_pairs={{0,4},{4,0},{1,5},{5,1},{2,6},{6,2},{3,7},{7,3},{8,12},{12,8},{9,1... | collective-permute-start | bytes 786440 | tf_op jit(solution)/shard_map/ppermute | solution.py:397
  47.2 6.2 %collective-permute-start.7 = (bf16[512,256]{1,0:T(8,128)(2,1)S(1)}, bf16[512,256]{1,0:T(8,128)(2,1)S(1)}, u32[]{:S(2)}, u32[]{:S(2)}) collective-permute-start(bf16[512,256]{1,0:T(8,128)(2,1)S(1)} %copy-done.3), channel_id=1, source_target_pairs={{0,4},{4,0},{1,5},{5,1},{2,6},{6,2},{3,7},{7,3},{8,12},{12,8},{9,1... | collective-permute-start | bytes 786440 | tf_op jit(solution)/shard_map/ppermute | solution.py:397
  47.3 6.1 %collective-permute-start.14 = (bf16[512,256]{1,0:T(8,128)(2,1)}, bf16[512,256]{1,0:T(8,128)(2,1)S(1)}, u32[]{:S(2)}, u32[]{:S(2)}) collective-permute-start(bf16[512,256]{1,0:T(8,128)(2,1)} %collective-permute-done.12.refs_10_), channel_id=1, source_target_pairs={{0,4},{4,0},{1,5},{5,1},{2,6},{6,2},{3,7},{7,3},{8,12},{12,8},{9,1... | collective-permute-start | bytes 786440 | tf_op jit(solution)/shard_map/ppermute | solution.py:397
  47.7 5.7 %collective-permute-start.15 = (bf16[512,256]{1,0:T(8,128)(2,1)}, bf16[512,256]{1,0:T(8,128)(2,1)S(1)}, u32[]{:S(2)}, u32[]{:S(2)}) collective-permute-start(bf16[512,256]{1,0:T(8,128)(2,1)} %collective-permute-done.13.refs_11_), channel_id=1, source_target_pairs={{0,4},{4,0},{1,5},{5,1},{2,6},{6,2},{3,7},{7,3},{8,12},{12,8},{9,1... | collective-permute-start | bytes 786440 | tf_op jit(solution)/shard_map/ppermute | solution.py:397
  48.5 12.2 %all-to-all-start.4 = ((bf16[32,40,128]{2,1,0:T(8,128)(2,1)}), bf16[32,40,128]{2,1,0:T(8,128)(2,1)S(1)}, u32[]{:S(2)}, u32[]{:S(2)}) async-start(bf16[32,40,128]{2,1,0:T(8,128)(2,1)} %prefix.2), calls=%async_computation.4 | async-start | bytes 655360 | tf_op jit(solution)/shard_map/all_to_all | solution.py:509
  (7 other events, 29.4 us)

commit v8 on v7

--- a/solution.py
+++ b/solution.py
@@ -240,42 +240,50 @@
         n0, n1 = lax.fori_loop(0, left, scan, (n0, n1))
     slots = ((pk0, pv0, n0), (pk1, pv1, n1))
 
-    def step(b, _):
-        results = []
-        for i, (pk, pv, count) in enumerate(slots):
-            last = jnp.maximum(count - 1, 0)
-            chats = [lists[i, jnp.minimum(b * MEMBER + j, last)] for j in range(MEMBER)]
-            line = None
-            shares = []
+    def part(i, base, size):
+        pk, pv, count = slots[i]
+        last = jnp.maximum(count - 1, 0)
+        chats = [lists[i, jnp.minimum(base + j, last)] for j in range(size)]
+        line = None
+        shares = []
+        for g in range(KV):
+            heads = slice(g * GROUP, (g + 1) * GROUP)
+            lanes = slice(g * HD, (g + 1) * HD)
+            for j, chat in enumerate(chats):
+                qs[i, g, j] = q_ref[chat, heads, :]
+            scores = scores_of(qs[i, g, :size].reshape(size * GROUP, HD), pk[:, lanes])
+            peak = jnp.max(scores, axis=1, keepdims=True)
+            weights = jnp.exp2((scores - peak) * SCALE2)
+            total = jnp.sum(weights, axis=1, keepdims=True)
+            numer = dot(weights.astype(BF16), pv[:, lanes])
+            shares.append((numer / total).astype(BF16))
+            level = jnp.broadcast_to(peak * SCALE2 + jnp.log2(total), (size * GROUP, HD))
+            level = level.reshape(size, GROUP, HD)
+            row = jnp.sum(jnp.where(diagonal[None, heads], level, 0.0), axis=1)
+            line = row if line is None else line + row
+        return chats, shares, level_parts(line)
+
+    def store(chats, shares, parts):
+        for j, chat in enumerate(chats):
             for g in range(KV):
-                heads = slice(g * GROUP, (g + 1) * GROUP)
-                lanes = slice(g * HD, (g + 1) * HD)
-                for j, chat in enumerate(chats):
-                    qs[i, g, j] = q_ref[chat, heads, :]
-                scores = scores_of(qs[i, g].reshape(MEMBER * GROUP, HD), pk[:, lanes])
-                peak = jnp.max(scores, axis=1, keepdims=True)
-                weights = jnp.exp2((scores - peak) * SCALE2)
-                total = jnp.sum(weights, axis=1, keepdims=True)
-                numer = dot(weights.astype(BF16), pv[:, lanes])
-                shares.append((numer / total).astype(BF16))
-                level = jnp.broadcast_to(peak * SCALE2 + jnp.log2(total), (MEMBER * GROUP, HD))
-                level = level.reshape(MEMBER, GROUP, HD)
-                part = jnp.sum(jnp.where(diagonal[None, heads], level, 0.0), axis=1)
-                line = part if line is None else line + part
-            results.append((chats, shares, level_parts(line)))
-        for (chats, shares, parts), (_, _, count) in zip(results, slots):
-
-            @pl.when(b * MEMBER < count)
-            def _(chats=chats, shares=shares, parts=parts):
-                for j, chat in enumerate(chats):
-                    for g in range(KV):
-                        rows = slice(j * GROUP, (j + 1) * GROUP)
-                        out[chat, g * GROUP : (g + 1) * GROUP, :] = shares[g][rows]
-                    out[chat, HEADS:, :] = parts[j]
-
-        return 0
-
-    lax.fori_loop(0, (jnp.maximum(n0, n1) + MEMBER - 1) >> 3, step, 0)
+                rows = slice(j * GROUP, (j + 1) * GROUP)
+                out[chat, g * GROUP : (g + 1) * GROUP, :] = shares[g][rows]
+            out[chat, HEADS:, :] = parts[j]
+
+    @pl.when(jnp.maximum(n0, n1) > 0)
+    def _():
+        results = [part(i, 0, MEMBER) for i in range(2)]
+        for i in range(2):
+            pl.when(slots[i][2] > 0)(functools.partial(store, *results[i]))
+
+    for i in range(2):
+
+        def further(b, _, i=i):
+            store(*part(i, MEMBER + b * (MEMBER // 2), MEMBER // 2))
+            return 0
+
+        left = jnp.maximum(slots[i][2] - MEMBER, 0)
+        lax.fori_loop(0, (left + MEMBER // 2 - 1) >> 2, further, 0)
 
 
 def place_answers(plan, start, back, out):
@@ -492,8 +500,10 @@
     for k, v in ((k_left, v_left), (k_right, v_right), (k_far, v_far)):
         others += [(k, v), (send(k, "c", 1), send(v, "c", 1))]
 
-    def prefix_answers(turn, picked):
-        asked = lax.all_to_all(picked, "x", split_axis=0, concat_axis=0, tiled=True)
+    def over_x(array):
+        return lax.all_to_all(array, "x", split_axis=0, concat_axis=0, tiled=True)
+
+    def prefix_answers(turn, asked):
         answer = scalar_kernel(
             prefix_kernel,
             "prefix",
@@ -506,7 +516,7 @@
             ],
             us=2,
         )
-        return lax.all_to_all(answer, "x", split_axis=0, concat_axis=0, tiled=True)
+        return over_x(answer)
 
     def more(state):
         turn, before = state
@@ -514,13 +524,13 @@
             more_kernel,
             "more",
             shaped(COLUMN, ROWS, HD),
-            [plan, turn, prefix_answers(turn, prefix_picked(turn)), before],
+            [plan, turn, prefix_answers(turn, over_x(prefix_picked(turn))), before],
             scalars=2,
             scratch=[pltpu.VMEM((COLUMN, ROWS, HD), BF16)],
         )
         return turn + 1, after
 
-    answers = prefix_answers(0, picked)
+    answers = prefix_answers(0, over_x(picked))
     _, near = lax.while_loop(
         lambda state: state[0][0] < rounds[0], more, (jnp.ones((1,), i32), near)
     )

time: 82.9 us -> 82.4 us (level)
  no operation moved by 1% of the time
where the time goes in v8:
time: 82.4 us; the launch traced here: 81.9 us
  starting transfers between devices  30 us (36%)
  Pallas kernels  20.4 us (25%)
  blocking collectives  18.6 us (23%)
  waiting for transfers between devices  8.72 us (11%)
  local copies, waits for them, and re-layouts  2.12 us (3%)
  other arithmetic  1.02 us (1%)
    pallas_call x7, Pallas kernels, kernel(): pl.pallas_call(body, out_shape=outs, in_specs=in_specs or [SMEM] * scalar...  20.4 us
    all_to_all x1, blocking collectives, local(): lax.all_to_all(merged, ('z', 'y'), split_axis=0, concat_axis=0, tiled=True)  18.6 us
    all_to_all x1, starting transfers between devices, local(): lax.all_to_all(spread.reshape(COLUMN, HEADS, HD), ('z', 'y'), split_axis=...  11.3 us
    ppermute x16, starting transfers between devices, send(): lax.ppermute(array, axis, [(i, (i + shift) % size) for i in range(size)])  9.85 us
    all_to_all x2, starting transfers between devices, over_x(): return lax.all_to_all(array, 'x', split_axis=0, concat_axis=0, tiled=True)  8.83 us
    all_to_all x1, waiting for transfers between devices, local(): lax.all_to_all(spread.reshape(COLUMN, HEADS, HD), ('z', 'y'), split_axis=...  5.88 us
    all_to_all x2, waiting for transfers between devices, over_x(): return lax.all_to_all(array, 'x', split_axis=0, concat_axis=0, tiled=True)  2.8 us
  transfers between devices with their start and end apart: 19, of which 2 were waited for; matrix products, arithmetic and copies ran while one was open for 2% of the time, Pallas kernels for 23%

profile of v8, /device:TPU:2, one launch (start us, length us, event | category | flops | bytes accessed | tf_op | source)
XLA Modules:
  0.0 81.9 jit_solution(3927101561570197270)
XLA Ops:
  0.0 1.5 %collective-permute-start = (bf16[512,256]{1,0:T(8,128)(2,1)}, bf16[512,256]{1,0:T(8,128)(2,1)S(1)}, u32[]{:S(2)}, u32[]{:S(2)}) collective-permute-start(bf16[512,256]{1,0:T(8,128)(2,1)} %k.1), channel_id=1, source_target_pairs={{0,64},{64,128},{128,192},{192,0},{1,65},{65,129},{129,193},{193,1... | collective-permute-start | bytes 786440 | tf_op jit(solution)/shard_map/ppermute | solution.py:405
  1.5 1.2 %collective-permute-start.1 = (bf16[512,256]{1,0:T(8,128)(2,1)}, bf16[512,256]{1,0:T(8,128)(2,1)S(1)}, u32[]{:S(2)}, u32[]{:S(2)}) collective-permute-start(bf16[512,256]{1,0:T(8,128)(2,1)} %v.1), channel_id=1, source_target_pairs={{0,64},{64,128},{128,192},{192,0},{1,65},{65,129},{129,193},{193,1... | collective-permute-start | bytes 786440 | tf_op jit(solution)/shard_map/ppermute | solution.py:405
  2.7 0.8 %collective-permute-start.2 = (bf16[512,256]{1,0:T(8,128)(2,1)}, bf16[512,256]{1,0:T(8,128)(2,1)}, u32[]{:S(2)}, u32[]{:S(2)}) collective-permute-start(bf16[512,256]{1,0:T(8,128)(2,1)} %k.1), channel_id=1, source_target_pairs={{0,192},{64,0},{128,64},{192,128},{1,193},{65,1},{129,65},{193,129... | collective-permute-start | bytes 786440 | tf_op jit(solution)/shard_map/ppermute | solution.py:405
  3.5 2.0 %collective-permute-start.3 = (bf16[512,256]{1,0:T(8,128)(2,1)}, bf16[512,256]{1,0:T(8,128)(2,1)}, u32[]{:S(2)}, u32[]{:S(2)}) collective-permute-start(bf16[512,256]{1,0:T(8,128)(2,1)} %v.1), channel_id=1, source_target_pairs={{0,192},{64,0},{128,64},{192,128},{1,193},{65,1},{129,65},{193,129... | collective-permute-start | bytes 786440 | tf_op jit(solution)/shard_map/ppermute | solution.py:405
  5.5 1.0 %reduce = bf16[16384]{0:T(1024)(128)(2,1)S(1)} reduce(bf16[1,16384]{1,0:T(2,128)(2,1)} %param.16, bf16[]{:T(256)} %constant.12), dimensions={0}, to_apply=%param.16.reduce_sub_computation | reduce | bytes 65538 | tf_op args[0]
  6.6 0.7 broadcast_in_dim.8
  7.3 11.3 %all-to-all-start.2 = ((bf16[32,32,128]{2,1,0:T(8,128)(2,1)}), bf16[32,32,128]{2,1,0:T(8,128)(2,1)}, u32[]{:S(2)}, u32[]{:S(2)}) async-start(bf16[32,32,128]{2,1,0:T(8,128)(2,1)} %bitcast.3), calls=%async_computation.2 | async-start | bytes 524288 | tf_op jit(solution)/shard_map/all_to_all | solution.py:429
  18.7 0.7 copy-done.8
  19.3 2.8 %prepare.1 = (s32[9,33]{1,0:T(8,128)S(1)}, s32[1]{0:T(128)}) custom-call(s32[256]{0:T(256)S(1)} %copy-done.8, s32[64]{0:T(128)S(1)} %copy-done.9, s32[1,256]{1,0:T(1,128)S(1)} %bitcast.8, s32[1,64]{1,0:T(1,128)S(1)} %bitcast.9), custom_call_target="tpu_custom_call" | custom-call | flops 1600000000 | bytes 2000000 | tf_op jit(solution)/shard_map/prepare/pallas_call | solution.py:389
  22.8 0.5 collective-permute-start.13
  23.3 1.5 %collective-permute-start.12 = (bf16[512,256]{1,0:T(8,128)(2,1)S(1)}, bf16[512,256]{1,0:T(8,128)(2,1)}, u32[]{:S(2)}, u32[]{:S(2)}) collective-permute-start(bf16[512,256]{1,0:T(8,128)(2,1)S(1)} %collective-permute-done.refs_2_), channel_id=1, source_target_pairs={{0,64},{64,128},{128,192},{192,0},{1,65},{65,129},{129,193},{193,1... | collective-permute-start | bytes 786440 | tf_op jit(solution)/shard_map/ppermute | solution.py:405
  24.8 5.9 %all-to-all-done.2.q_ref.refs_0_ = bf16[32,32,128]{2,1,0:T(8,128)(2,1)} async-done(((bf16[32,32,128]{2,1,0:T(8,128)(2,1)}), bf16[32,32,128]{2,1,0:T(8,128)(2,1)}, u32[]{:S(2)}, u32[]{:S(2)}) %all-to-all-start.2) | async-done | bytes 262176 | tf_op jit(solution)/shard_map/all_to_all | solution.py:429
  30.7 1.7 %select.2 = bf16[32,32,128]{2,1,0:T(8,128)(2,1)} custom-call(s32[9,33]{1,0:T(8,128)S(1)} %get-tuple-element.152.plan, bf16[32,32,128]{2,1,0:T(8,128)(2,1)} %all-to-all-done.2.q_ref.refs_0_), custom_call_target="tpu_custom_call" | custom-call | flops 400000000 | bytes 500000 | tf_op jit(solution)/shard_map/select/pallas_call | solution.py:389
  33.1 3.9 %all-to-all-start.3 = ((bf16[32,32,128]{2,1,0:T(8,128)(2,1)}), bf16[32,32,128]{2,1,0:T(8,128)(2,1)S(1)}, u32[]{:S(2)}, u32[]{:S(2)}) async-start(bf16[32,32,128]{2,1,0:T(8,128)(2,1)} %select.2), calls=%async_computation.3 | async-start | bytes 524288 | tf_op jit(solution)/shard_map/all_to_all | solution.py:504
  37.1 2.9 %near.1 = (bf16[32,40,128]{2,1,0:T(8,128)(2,1)}, f32[4,32,128]{2,1,0:T(8,128)S(1)}, f32[4,128]{1,0:T(4,128)S(1)}) custom-call(s32[4]{0:T(128)S(1)} %copy-done.10, bf16[32,32,128]{2,1,0:T(8,128)(2,1)} %all-to-all-done.2.q_ref.refs_0_, bf16[512,256]{1,0:T(8,128)(2,1)S(1)} %copy-done.2, bf16[512,256]{1,0:T(8,128)(2,1)S(1)} %copy-done.3, ...), custom_call_target="tpu_custom_call" | custom-call | flops 3200000000 | bytes 4000000 | tf_op jit(solution)/shard_map/near/pallas_call | solution.py:389
  40.0 2.8 %all-to-all-done.3.refs_0_ = bf16[32,32,128]{2,1,0:T(8,128)(2,1)S(1)} async-done(((bf16[32,32,128]{2,1,0:T(8,128)(2,1)}), bf16[32,32,128]{2,1,0:T(8,128)(2,1)S(1)}, u32[]{:S(2)}, u32[]{:S(2)}) %all-to-all-start.3) | async-done | bytes 262176 | tf_op jit(solution)/shard_map/all_to_all | solution.py:504
  42.8 4.1 %prefix.2 = bf16[32,40,128]{2,1,0:T(8,128)(2,1)} custom-call(s32[9,33]{1,0:T(8,128)S(1)} %get-tuple-element.152.plan, bf16[32,32,128]{2,1,0:T(8,128)(2,1)S(1)} %all-to-all-done.3.refs_0_, bf16[1024,256]{1,0:T(8,128)(2,1)} %refs_1_.1, bf16[1024,256]{1,0:T(8,128)(2,1)} %collective-permute-done.4.refs_2_, bf16[1024,256]{1,0:T(8,128)(2,1)} %refs_3_.1, ...), custom_call_target="tpu_custom_call" | custom-call | flops 1600000000 | bytes 2000000 | tf_op jit(solution)/shard_map/prefix/pallas_call | solution.py:389
  46.8 0.5 collective-permute-start.6
  48.0 0.7 while.10
  48.7 4.9 %all-to-all-start.4 = ((bf16[32,40,128]{2,1,0:T(8,128)(2,1)}), bf16[32,40,128]{2,1,0:T(8,128)(2,1)S(1)}, u32[]{:S(2)}, u32[]{:S(2)}) async-start(bf16[32,40,128]{2,1,0:T(8,128)(2,1)} %prefix.2), calls=%async_computation.4 | async-start | bytes 655360 | tf_op jit(solution)/shard_map/all_to_all | solution.py:504
  53.6 7.2 %far.1 = bf16[32,40,128]{2,1,0:T(8,128)(2,1)S(1)} custom-call(bf16[32,32,128]{2,1,0:T(8,128)(2,1)} %all-to-all-done.2.q_ref.refs_0_, bf16[512,256]{1,0:T(8,128)(2,1)S(1)} %collective-permute-done.6.refs_0_, bf16[512,256]{1,0:T(8,128)(2,1)S(1)} %collective-permute-done.7.refs_1_, bf16[512,256]{1,0:T(8,128)(2,1)S(1)} %collective-permute-done.refs_2_, ...), custom_call_target="tpu_custom_call" | custom-call | flops 4800000000 | bytes 6000000 | tf_op jit(solution)/shard_map/far/pallas_call | solution.py:389
  60.9 1.4 %merge_row.1 = bf16[32,40,128]{2,1,0:T(8,128)(2,1)S(1)} custom-call(s32[9,33]{1,0:T(8,128)S(1)} %get-tuple-element.198, bf16[32,40,128]{2,1,0:T(8,128)(2,1)S(1)} %get-tuple-element.75.near, bf16[32,40,128]{2,1,0:T(8,128)(2,1)S(1)} %far.1, bf16[32,40,128]{2,1,0:T(8,128)(2,1)S(1)} %all-to-all-done.4.back, f32[4,32,128]{2,1,0:T(8,128)S(1)} %get-tuple-element.82.share_ref, ...), custom_call_target="tpu_custom_call" | custom-call | flops 1200000000 | bytes 1500000 | tf_op jit(solution)/shard_map/merge_row/pallas_call | solution.py:389
  62.3 18.6 %all_to_all.30 = bf16[32,40,128]{2,1,0:T(8,128)(2,1)S(1)} all-to-all(bf16[32,40,128]{2,1,0:T(8,128)(2,1)S(1)} %merge_row.1), channel_id=1, replica_groups=mesh['x'=4,'z'=8,'c'=2,'y'=4] {'z','y'}, dimensions={0} | all-to-all | bytes 655360 | tf_op jit(solution)/shard_map/all_to_all | solution.py:558
  81.2 0.7 reshape.22
  (50 shorter events, 2.2 us)
Async XLA Ops:
  0.0 22.2 %collective-permute-start = (bf16[512,256]{1,0:T(8,128)(2,1)}, bf16[512,256]{1,0:T(8,128)(2,1)S(1)}, u32[]{:S(2)}, u32[]{:S(2)}) collective-permute-start(bf16[512,256]{1,0:T(8,128)(2,1)} %k.1), channel_id=1, source_target_pairs={{0,64},{64,128},{128,192},{192,0},{1,65},{65,129},{129,193},{193,1... | collective-permute-start | bytes 786440 | tf_op jit(solution)/shard_map/ppermute | solution.py:405
  1.5 20.7 %collective-permute-start.1 = (bf16[512,256]{1,0:T(8,128)(2,1)}, bf16[512,256]{1,0:T(8,128)(2,1)S(1)}, u32[]{:S(2)}, u32[]{:S(2)}) collective-permute-start(bf16[512,256]{1,0:T(8,128)(2,1)} %v.1), channel_id=1, source_target_pairs={{0,64},{64,128},{128,192},{192,0},{1,65},{65,129},{129,193},{193,1... | collective-permute-start | bytes 786440 | tf_op jit(solution)/shard_map/ppermute | solution.py:405
  2.7 19.5 %collective-permute-start.2 = (bf16[512,256]{1,0:T(8,128)(2,1)}, bf16[512,256]{1,0:T(8,128)(2,1)}, u32[]{:S(2)}, u32[]{:S(2)}) collective-permute-start(bf16[512,256]{1,0:T(8,128)(2,1)} %k.1), channel_id=1, source_target_pairs={{0,192},{64,0},{128,64},{192,128},{1,193},{65,1},{129,65},{193,129... | collective-permute-start | bytes 786440 | tf_op jit(solution)/shard_map/ppermute | solution.py:405
  3.5 18.7 %collective-permute-start.3 = (bf16[512,256]{1,0:T(8,128)(2,1)}, bf16[512,256]{1,0:T(8,128)(2,1)}, u32[]{:S(2)}, u32[]{:S(2)}) collective-permute-start(bf16[512,256]{1,0:T(8,128)(2,1)} %v.1), channel_id=1, source_target_pairs={{0,192},{64,0},{128,64},{192,128},{1,193},{65,1},{129,65},{193,129... | collective-permute-start | bytes 786440 | tf_op jit(solution)/shard_map/ppermute | solution.py:405
  7.3 23.4 %all-to-all-start.2 = ((bf16[32,32,128]{2,1,0:T(8,128)(2,1)}), bf16[32,32,128]{2,1,0:T(8,128)(2,1)}, u32[]{:S(2)}, u32[]{:S(2)}) async-start(bf16[32,32,128]{2,1,0:T(8,128)(2,1)} %bitcast.3), calls=%async_computation.2 | async-start | bytes 524288 | tf_op jit(solution)/shard_map/all_to_all | solution.py:429
  19.3 17.7 %copy-start.1 = (bf16[4,512,256]{2,1,0:T(8,128)(2,1)S(1)}, bf16[4,512,256]{2,1,0:T(8,128)(2,1)}, u32[]{:S(2)}) copy-start(bf16[4,512,256]{2,1,0:T(8,128)(2,1)} %wv.1) | copy-start | bytes 3145732
  22.2 14.9 %copy-start = (bf16[4,512,256]{2,1,0:T(8,128)(2,1)S(1)}, bf16[4,512,256]{2,1,0:T(8,128)(2,1)}, u32[]{:S(2)}) copy-start(bf16[4,512,256]{2,1,0:T(8,128)(2,1)} %wk.1) | copy-start | bytes 3145732
  22.2 10.3 %collective-permute-start.4 = (bf16[1024,256]{1,0:T(8,128)(2,1)}, bf16[1024,256]{1,0:T(8,128)(2,1)}, u32[]{:S(2)}, u32[]{:S(2)}) collective-permute-start(bf16[1024,256]{1,0:T(8,128)(2,1)} %refs_1_.1), channel_id=1, source_target_pairs={{0,4},{4,0},{1,5},{5,1},{2,6},{6,2},{3,7},{7,3},{8,12},{12,8},{9,1... | collective-permute-start | bytes 1572872 | tf_op jit(solution)/shard_map/ppermute | solution.py:405
  22.3 10.3 %collective-permute-start.5 = (bf16[1024,256]{1,0:T(8,128)(2,1)}, bf16[1024,256]{1,0:T(8,128)(2,1)}, u32[]{:S(2)}, u32[]{:S(2)}) collective-permute-start(bf16[1024,256]{1,0:T(8,128)(2,1)} %refs_3_.1), channel_id=1, source_target_pairs={{0,4},{4,0},{1,5},{5,1},{2,6},{6,2},{3,7},{7,3},{8,12},{12,8},{9,1... | collective-permute-start | bytes 1572872 | tf_op jit(solution)/shard_map/ppermute | solution.py:405
  22.8 24.0 %collective-permute-start.13 = (bf16[512,256]{1,0:T(8,128)(2,1)}, bf16[512,256]{1,0:T(8,128)(2,1)}, u32[]{:S(2)}, u32[]{:S(2)}) collective-permute-start(bf16[512,256]{1,0:T(8,128)(2,1)} %collective-permute-done.3.refs_7_), channel_id=1, source_target_pairs={{0,192},{64,0},{128,64},{192,128},{1,193},{65,1},{129,65},{193,129... | collective-permute-start | bytes 786440 | tf_op jit(solution)/shard_map/ppermute | solution.py:405
  23.3 24.0 %collective-permute-start.11 = (bf16[512,256]{1,0:T(8,128)(2,1)}, bf16[512,256]{1,0:T(8,128)(2,1)}, u32[]{:S(2)}, u32[]{:S(2)}) collective-permute-start(bf16[512,256]{1,0:T(8,128)(2,1)} %collective-permute-done.3.refs_7_), channel_id=1, source_target_pairs={{0,4},{4,0},{1,5},{5,1},{2,6},{6,2},{3,7},{7,3},{8,12},{12,8},{9,1... | collective-permute-start | bytes 786440 | tf_op jit(solution)/shard_map/ppermute | solution.py:405
  23.3 23.5 %collective-permute-start.12 = (bf16[512,256]{1,0:T(8,128)(2,1)S(1)}, bf16[512,256]{1,0:T(8,128)(2,1)}, u32[]{:S(2)}, u32[]{:S(2)}) collective-permute-start(bf16[512,256]{1,0:T(8,128)(2,1)S(1)} %collective-permute-done.refs_2_), channel_id=1, source_target_pairs={{0,64},{64,128},{128,192},{192,0},{1,65},{65,129},{129,193},{193,1... | collective-permute-start | bytes 786440 | tf_op jit(solution)/shard_map/ppermute | solution.py:405
  30.7 6.3 %copy-start.7 = (bf16[4,256]{1,0:T(4,128)(2,1)S(1)}, bf16[4,256]{1,0:T(4,128)(2,1)}, u32[]{:S(2)}) copy-start(bf16[4,256]{1,0:T(4,128)(2,1)} %nv.1) | copy-start | bytes 6148
  30.7 6.3 %copy-start.10 = (s32[4]{0:T(128)S(1)}, s32[4]{0:T(128)}, u32[]{:S(2)}) copy-start(s32[4]{0:T(128)} %length_ref.1) | copy-start | bytes 52
  32.5 15.0 %collective-permute-start.8 = (bf16[512,256]{1,0:T(8,128)(2,1)S(1)}, bf16[512,256]{1,0:T(8,128)(2,1)}, u32[]{:S(2)}, u32[]{:S(2)}) collective-permute-start(bf16[512,256]{1,0:T(8,128)(2,1)S(1)} %collective-permute-done.refs_2_), channel_id=1, source_target_pairs={{0,4},{4,0},{1,5},{5,1},{2,6},{6,2},{3,7},{7,3},{8,12},{12,8},{9,1... | collective-permute-start | bytes 786440 | tf_op jit(solution)/shard_map/ppermute | solution.py:405
  32.6 15.3 %collective-permute-start.10 = (bf16[512,256]{1,0:T(8,128)(2,1)}, bf16[512,256]{1,0:T(8,128)(2,1)}, u32[]{:S(2)}, u32[]{:S(2)}) collective-permute-start(bf16[512,256]{1,0:T(8,128)(2,1)} %collective-permute-done.2.refs_6_), channel_id=1, source_target_pairs={{0,4},{4,0},{1,5},{5,1},{2,6},{6,2},{3,7},{7,3},{8,12},{12,8},{9,1... | collective-permute-start | bytes 786440 | tf_op jit(solution)/shard_map/ppermute | solution.py:405
  33.1 9.7 %all-to-all-start.3 = ((bf16[32,32,128]{2,1,0:T(8,128)(2,1)}), bf16[32,32,128]{2,1,0:T(8,128)(2,1)S(1)}, u32[]{:S(2)}, u32[]{:S(2)}) async-start(bf16[32,32,128]{2,1,0:T(8,128)(2,1)} %select.2), calls=%async_computation.3 | async-start | bytes 524288 | tf_op jit(solution)/shard_map/all_to_all | solution.py:504
  40.0 8.0 %copy-start.11 = (bf16[32,40,128]{2,1,0:T(8,128)(2,1)S(1)}, bf16[32,40,128]{2,1,0:T(8,128)(2,1)}, u32[]{:S(2)}) copy-start(bf16[32,40,128]{2,1,0:T(8,128)(2,1)} %get-tuple-element.150) | copy-start | bytes 983044
  46.8 6.8 %collective-permute-start.9 = (bf16[512,256]{1,0:T(8,128)(2,1)S(1)}, bf16[512,256]{1,0:T(8,128)(2,1)S(1)}, u32[]{:S(2)}, u32[]{:S(2)}) collective-permute-start(bf16[512,256]{1,0:T(8,128)(2,1)S(1)} %collective-permute-done.1.refs_3_), channel_id=1, source_target_pairs={{0,4},{4,0},{1,5},{5,1},{2,6},{6,2},{3,7},{7,3},{8,12},{12,8},{9,1... | collective-permute-start | bytes 786440 | tf_op jit(solution)/shard_map/ppermute | solution.py:405
  46.8 6.8 %collective-permute-start.6 = (bf16[512,256]{1,0:T(8,128)(2,1)S(1)}, bf16[512,256]{1,0:T(8,128)(2,1)S(1)}, u32[]{:S(2)}, u32[]{:S(2)}) collective-permute-start(bf16[512,256]{1,0:T(8,128)(2,1)S(1)} %copy-done.2), channel_id=1, source_target_pairs={{0,4},{4,0},{1,5},{5,1},{2,6},{6,2},{3,7},{7,3},{8,12},{12,8},{9,1... | collective-permute-start | bytes 786440 | tf_op jit(solution)/shard_map/ppermute | solution.py:405
  47.3 6.3 %collective-permute-start.7 = (bf16[512,256]{1,0:T(8,128)(2,1)S(1)}, bf16[512,256]{1,0:T(8,128)(2,1)S(1)}, u32[]{:S(2)}, u32[]{:S(2)}) collective-permute-start(bf16[512,256]{1,0:T(8,128)(2,1)S(1)} %copy-done.3), channel_id=1, source_target_pairs={{0,4},{4,0},{1,5},{5,1},{2,6},{6,2},{3,7},{7,3},{8,12},{12,8},{9,1... | collective-permute-start | bytes 786440 | tf_op jit(solution)/shard_map/ppermute | solution.py:405
  47.4 6.2 %collective-permute-start.14 = (bf16[512,256]{1,0:T(8,128)(2,1)}, bf16[512,256]{1,0:T(8,128)(2,1)S(1)}, u32[]{:S(2)}, u32[]{:S(2)}) collective-permute-start(bf16[512,256]{1,0:T(8,128)(2,1)} %collective-permute-done.12.refs_10_), channel_id=1, source_target_pairs={{0,4},{4,0},{1,5},{5,1},{2,6},{6,2},{3,7},{7,3},{8,12},{12,8},{9,1... | collective-permute-start | bytes 786440 | tf_op jit(solution)/shard_map/ppermute | solution.py:405
  47.9 5.8 %collective-permute-start.15 = (bf16[512,256]{1,0:T(8,128)(2,1)}, bf16[512,256]{1,0:T(8,128)(2,1)S(1)}, u32[]{:S(2)}, u32[]{:S(2)}) collective-permute-start(bf16[512,256]{1,0:T(8,128)(2,1)} %collective-permute-done.13.refs_11_), channel_id=1, source_target_pairs={{0,4},{4,0},{1,5},{5,1},{2,6},{6,2},{3,7},{7,3},{8,12},{12,8},{9,1... | collective-permute-start | bytes 786440 | tf_op jit(solution)/shard_map/ppermute | solution.py:405
  48.7 12.2 %all-to-all-start.4 = ((bf16[32,40,128]{2,1,0:T(8,128)(2,1)}), bf16[32,40,128]{2,1,0:T(8,128)(2,1)S(1)}, u32[]{:S(2)}, u32[]{:S(2)}) async-start(bf16[32,40,128]{2,1,0:T(8,128)(2,1)} %prefix.2), calls=%async_computation.4 | async-start | bytes 655360 | tf_op jit(solution)/shard_map/all_to_all | solution.py:504
  (7 other events, 29.4 us)

commit v9 on v8

--- a/solution.py
+++ b/solution.py
@@ -128,27 +128,40 @@
             values[g, rows, HD:] = jnp.ones((512, HD), BF16)
     diagonal = head_diagonal()
     rows = COLUMN // 2
-    for h in range(2):
+    tiles = [(h, g) for h in range(2) for g in range(KV)]
+
+    def score(tile, n):
+        h, g = tile
+        query = q_ref[h * rows : (h + 1) * rows, g * GROUP : (g + 1) * GROUP, :]
+        return scores_of(
+            query.reshape(rows * GROUP, HD), blocks[n][0][:, g * HD : (g + 1) * HD]
+        )
+
+    count = len(blocks)
+    scores = [score(tiles[0], n) for n in range(count)]
+    highest = functools.reduce(jnp.maximum, scores)
+    line = None
+    for t, (h, g) in enumerate(tiles):
         chats = slice(h * rows, (h + 1) * rows)
-        line = None
-        for g in range(KV):
-            heads = slice(g * GROUP, (g + 1) * GROUP)
-            lanes = slice(g * HD, (g + 1) * HD)
-            query = q_ref[chats, heads, :].reshape(rows * GROUP, HD)
-            scores = [scores_of(query, k[:, lanes]) for k, _ in blocks]
-            peak = jnp.max(functools.reduce(jnp.maximum, scores), axis=1, keepdims=True)
-            numer = None
-            for n, s in enumerate(scores):
-                weights = jnp.exp2((s - peak) * SCALE2).astype(BF16)
-                part = dot(weights, values[g, n * 512 : (n + 1) * 512, :])
-                numer = part if numer is None else numer + part
-            total = numer[:, HD:]
-            share = (numer[:, :HD] / total).astype(BF16)
-            out[chats, heads, :] = share.reshape(rows, GROUP, HD)
-            level = (peak * SCALE2 + jnp.log2(total)).reshape(rows, GROUP, HD)
-            part = jnp.sum(jnp.where(diagonal[None, heads], level, 0.0), axis=1)
-            line = part if line is None else line + part
-        out[chats, HEADS:, :] = level_parts(line)
+        heads = slice(g * GROUP, (g + 1) * GROUP)
+        peak = jnp.max(highest, axis=1, keepdims=True)
+        numer, later, highest = None, [], None
+        for n, s in enumerate(scores):
+            if t + 1 < len(tiles):
+                later.append(score(tiles[t + 1], n))
+                highest = later[0] if n == 0 else jnp.maximum(highest, later[n])
+            weights = jnp.exp2((s - peak) * SCALE2).astype(BF16)
+            part = dot(weights, values[g, n * 512 : (n + 1) * 512, :])
+            numer = part if numer is None else numer + part
+        scores = later
+        total = numer[:, HD:]
+        share = (numer[:, :HD] / total).astype(BF16)
+        out[chats, heads, :] = share.reshape(rows, GROUP, HD)
+        level = (peak * SCALE2 + jnp.log2(total)).reshape(rows, GROUP, HD)
+        part = jnp.sum(jnp.where(diagonal[None, heads], level, 0.0), axis=1)
+        line = part if g == 0 else line + part
+        if g == KV - 1:
+            out[chats, HEADS:, :] = level_parts(line)
 
 
 def home_part(length_ref, q_ref, wk, wv, sk, sv, nk, nv, share_ref, level_ref):

time: 82.4 us -> 81.5 us (0.989)
  transfers between devices with their start and end apart: 19 -> 19, of which waited for: 2 -> 3; matrix products, arithmetic and copies ran while one was open for 2% -> 2% of each run, Pallas kernels for 23% -> 22%
where the time goes in v9:
time: 81.5 us; the launch traced here: 80.7 us
  starting transfers between devices  29.9 us (37%)
  Pallas kernels  19.7 us (24%)
  blocking collectives  18 us (22%)
  waiting for transfers between devices  9.01 us (11%)
  local copies, waits for them, and re-layouts  2.12 us (3%)
  other arithmetic  1.02 us (1%)
    pallas_call x7, Pallas kernels, kernel(): pl.pallas_call(body, out_shape=outs, in_specs=in_specs or [SMEM] * scalar...  19.7 us
    all_to_all x1, blocking collectives, local(): lax.all_to_all(merged, ('z', 'y'), split_axis=0, concat_axis=0, tiled=True)  18 us
    all_to_all x1, starting transfers between devices, local(): lax.all_to_all(spread.reshape(COLUMN, HEADS, HD), ('z', 'y'), split_axis=...  11.3 us
    ppermute x16, starting transfers between devices, send(): lax.ppermute(array, axis, [(i, (i + shift) % size) for i in range(size)])  9.85 us
    all_to_all x2, starting transfers between devices, over_x(): return lax.all_to_all(array, 'x', split_axis=0, concat_axis=0, tiled=True)  8.76 us
    all_to_all x1, waiting for transfers between devices, local(): lax.all_to_all(spread.reshape(COLUMN, HEADS, HD), ('z', 'y'), split_axis=...  5.88 us
    all_to_all x2, waiting for transfers between devices, over_x(): return lax.all_to_all(array, 'x', split_axis=0, concat_axis=0, tiled=True)  3.08 us
  transfers between devices with their start and end apart: 19, of which 3 were waited for; matrix products, arithmetic and copies ran while one was open for 2% of the time, Pallas kernels for 22%

profile of v9, /device:TPU:2, one launch (start us, length us, event | category | flops | bytes accessed | tf_op | source)
XLA Modules:
  0.0 80.7 jit_solution(17901035581523062009)
XLA Ops:
  0.0 1.5 %collective-permute-start = (bf16[512,256]{1,0:T(8,128)(2,1)}, bf16[512,256]{1,0:T(8,128)(2,1)S(1)}, u32[]{:S(2)}, u32[]{:S(2)}) collective-permute-start(bf16[512,256]{1,0:T(8,128)(2,1)} %k.1), channel_id=1, source_target_pairs={{0,64},{64,128},{128,192},{192,0},{1,65},{65,129},{129,193},{193,1... | collective-permute-start | bytes 786440 | tf_op jit(solution)/shard_map/ppermute | solution.py:418
  1.5 1.2 %collective-permute-start.1 = (bf16[512,256]{1,0:T(8,128)(2,1)}, bf16[512,256]{1,0:T(8,128)(2,1)S(1)}, u32[]{:S(2)}, u32[]{:S(2)}) collective-permute-start(bf16[512,256]{1,0:T(8,128)(2,1)} %v.1), channel_id=1, source_target_pairs={{0,64},{64,128},{128,192},{192,0},{1,65},{65,129},{129,193},{193,1... | collective-permute-start | bytes 786440 | tf_op jit(solution)/shard_map/ppermute | solution.py:418
  2.7 0.8 %collective-permute-start.2 = (bf16[512,256]{1,0:T(8,128)(2,1)}, bf16[512,256]{1,0:T(8,128)(2,1)}, u32[]{:S(2)}, u32[]{:S(2)}) collective-permute-start(bf16[512,256]{1,0:T(8,128)(2,1)} %k.1), channel_id=1, source_target_pairs={{0,192},{64,0},{128,64},{192,128},{1,193},{65,1},{129,65},{193,129... | collective-permute-start | bytes 786440 | tf_op jit(solution)/shard_map/ppermute | solution.py:418
  3.5 2.0 %collective-permute-start.3 = (bf16[512,256]{1,0:T(8,128)(2,1)}, bf16[512,256]{1,0:T(8,128)(2,1)}, u32[]{:S(2)}, u32[]{:S(2)}) collective-permute-start(bf16[512,256]{1,0:T(8,128)(2,1)} %v.1), channel_id=1, source_target_pairs={{0,192},{64,0},{128,64},{192,128},{1,193},{65,1},{129,65},{193,129... | collective-permute-start | bytes 786440 | tf_op jit(solution)/shard_map/ppermute | solution.py:418
  5.5 1.0 %reduce = bf16[16384]{0:T(1024)(128)(2,1)S(1)} reduce(bf16[1,16384]{1,0:T(2,128)(2,1)} %param.16, bf16[]{:T(256)} %constant.12), dimensions={0}, to_apply=%param.16.reduce_sub_computation | reduce | bytes 65538 | tf_op args[0]
  6.6 0.7 broadcast_in_dim.8
  7.3 11.3 %all-to-all-start.2 = ((bf16[32,32,128]{2,1,0:T(8,128)(2,1)}), bf16[32,32,128]{2,1,0:T(8,128)(2,1)}, u32[]{:S(2)}, u32[]{:S(2)}) async-start(bf16[32,32,128]{2,1,0:T(8,128)(2,1)} %bitcast.3), calls=%async_computation.2 | async-start | bytes 524288 | tf_op jit(solution)/shard_map/all_to_all | solution.py:442
  18.7 0.7 copy-done.8
  19.3 2.8 %prepare.1 = (s32[9,33]{1,0:T(8,128)S(1)}, s32[1]{0:T(128)}) custom-call(s32[256]{0:T(256)S(1)} %copy-done.8, s32[64]{0:T(128)S(1)} %copy-done.9, s32[1,256]{1,0:T(1,128)S(1)} %bitcast.8, s32[1,64]{1,0:T(1,128)S(1)} %bitcast.9), custom_call_target="tpu_custom_call" | custom-call | flops 1600000000 | bytes 2000000 | tf_op jit(solution)/shard_map/prepare/pallas_call | solution.py:402
  22.8 0.5 collective-permute-start.13
  23.3 1.5 %collective-permute-start.12 = (bf16[512,256]{1,0:T(8,128)(2,1)S(1)}, bf16[512,256]{1,0:T(8,128)(2,1)}, u32[]{:S(2)}, u32[]{:S(2)}) collective-permute-start(bf16[512,256]{1,0:T(8,128)(2,1)S(1)} %collective-permute-done.refs_2_), channel_id=1, source_target_pairs={{0,64},{64,128},{128,192},{192,0},{1,65},{65,129},{129,193},{193,1... | collective-permute-start | bytes 786440 | tf_op jit(solution)/shard_map/ppermute | solution.py:418
  24.8 5.9 %all-to-all-done.2.q_ref.refs_0_ = bf16[32,32,128]{2,1,0:T(8,128)(2,1)} async-done(((bf16[32,32,128]{2,1,0:T(8,128)(2,1)}), bf16[32,32,128]{2,1,0:T(8,128)(2,1)}, u32[]{:S(2)}, u32[]{:S(2)}) %all-to-all-start.2) | async-done | bytes 262176 | tf_op jit(solution)/shard_map/all_to_all | solution.py:442
  30.7 1.7 %select.2 = bf16[32,32,128]{2,1,0:T(8,128)(2,1)} custom-call(s32[9,33]{1,0:T(8,128)S(1)} %get-tuple-element.152.plan, bf16[32,32,128]{2,1,0:T(8,128)(2,1)} %all-to-all-done.2.q_ref.refs_0_), custom_call_target="tpu_custom_call" | custom-call | flops 400000000 | bytes 500000 | tf_op jit(solution)/shard_map/select/pallas_call | solution.py:402
  33.1 3.9 %all-to-all-start.3 = ((bf16[32,32,128]{2,1,0:T(8,128)(2,1)}), bf16[32,32,128]{2,1,0:T(8,128)(2,1)S(1)}, u32[]{:S(2)}, u32[]{:S(2)}) async-start(bf16[32,32,128]{2,1,0:T(8,128)(2,1)} %select.2), calls=%async_computation.3 | async-start | bytes 524288 | tf_op jit(solution)/shard_map/all_to_all | solution.py:517
  37.1 3.0 %near.1 = (bf16[32,40,128]{2,1,0:T(8,128)(2,1)}, f32[4,32,128]{2,1,0:T(8,128)S(1)}, f32[4,128]{1,0:T(4,128)S(1)}) custom-call(s32[4]{0:T(128)S(1)} %copy-done.10, bf16[32,32,128]{2,1,0:T(8,128)(2,1)} %all-to-all-done.2.q_ref.refs_0_, bf16[512,256]{1,0:T(8,128)(2,1)S(1)} %copy-done.2, bf16[512,256]{1,0:T(8,128)(2,1)S(1)} %copy-done.3, ...), custom_call_target="tpu_custom_call" | custom-call | flops 3200000000 | bytes 4000000 | tf_op jit(solution)/shard_map/near/pallas_call | solution.py:402
  40.1 2.7 %all-to-all-done.3.refs_0_ = bf16[32,32,128]{2,1,0:T(8,128)(2,1)S(1)} async-done(((bf16[32,32,128]{2,1,0:T(8,128)(2,1)}), bf16[32,32,128]{2,1,0:T(8,128)(2,1)S(1)}, u32[]{:S(2)}, u32[]{:S(2)}) %all-to-all-start.3) | async-done | bytes 262176 | tf_op jit(solution)/shard_map/all_to_all | solution.py:517
  42.8 4.1 %prefix.2 = bf16[32,40,128]{2,1,0:T(8,128)(2,1)} custom-call(s32[9,33]{1,0:T(8,128)S(1)} %get-tuple-element.152.plan, bf16[32,32,128]{2,1,0:T(8,128)(2,1)S(1)} %all-to-all-done.3.refs_0_, bf16[1024,256]{1,0:T(8,128)(2,1)} %refs_1_.1, bf16[1024,256]{1,0:T(8,128)(2,1)} %collective-permute-done.4.refs_2_, bf16[1024,256]{1,0:T(8,128)(2,1)} %refs_3_.1, ...), custom_call_target="tpu_custom_call" | custom-call | flops 1600000000 | bytes 2000000 | tf_op jit(solution)/shard_map/prefix/pallas_call | solution.py:402
  46.9 0.5 collective-permute-start.6
  48.0 0.7 while.10
  48.7 4.9 %all-to-all-start.4 = ((bf16[32,40,128]{2,1,0:T(8,128)(2,1)}), bf16[32,40,128]{2,1,0:T(8,128)(2,1)S(1)}, u32[]{:S(2)}, u32[]{:S(2)}) async-start(bf16[32,40,128]{2,1,0:T(8,128)(2,1)} %prefix.2), calls=%async_computation.4 | async-start | bytes 655360 | tf_op jit(solution)/shard_map/all_to_all | solution.py:517
  53.6 6.4 %far.1 = bf16[32,40,128]{2,1,0:T(8,128)(2,1)S(1)} custom-call(bf16[32,32,128]{2,1,0:T(8,128)(2,1)} %all-to-all-done.2.q_ref.refs_0_, bf16[512,256]{1,0:T(8,128)(2,1)S(1)} %collective-permute-done.6.refs_0_, bf16[512,256]{1,0:T(8,128)(2,1)S(1)} %collective-permute-done.7.refs_1_, bf16[512,256]{1,0:T(8,128)(2,1)S(1)} %collective-permute-done.refs_2_, ...), custom_call_target="tpu_custom_call" | custom-call | flops 4800000000 | bytes 6000000 | tf_op jit(solution)/shard_map/far/pallas_call | solution.py:402
  60.3 1.4 %merge_row.1 = bf16[32,40,128]{2,1,0:T(8,128)(2,1)S(1)} custom-call(s32[9,33]{1,0:T(8,128)S(1)} %get-tuple-element.198, bf16[32,40,128]{2,1,0:T(8,128)(2,1)S(1)} %get-tuple-element.75.near, bf16[32,40,128]{2,1,0:T(8,128)(2,1)S(1)} %far.1, bf16[32,40,128]{2,1,0:T(8,128)(2,1)S(1)} %all-to-all-done.4.back, f32[4,32,128]{2,1,0:T(8,128)S(1)} %get-tuple-element.82.share_ref, ...), custom_call_target="tpu_custom_call" | custom-call | flops 1200000000 | bytes 1500000 | tf_op jit(solution)/shard_map/merge_row/pallas_call | solution.py:402
  61.8 18.0 %all_to_all.30 = bf16[32,40,128]{2,1,0:T(8,128)(2,1)S(1)} all-to-all(bf16[32,40,128]{2,1,0:T(8,128)(2,1)S(1)} %merge_row.1), channel_id=1, replica_groups=mesh['x'=4,'z'=8,'c'=2,'y'=4] {'z','y'}, dimensions={0} | all-to-all | bytes 655360 | tf_op jit(solution)/shard_map/all_to_all | solution.py:571
  80.0 0.7 reshape.22
  (50 shorter events, 2.5 us)
Async XLA Ops:
  0.0 22.2 %collective-permute-start = (bf16[512,256]{1,0:T(8,128)(2,1)}, bf16[512,256]{1,0:T(8,128)(2,1)S(1)}, u32[]{:S(2)}, u32[]{:S(2)}) collective-permute-start(bf16[512,256]{1,0:T(8,128)(2,1)} %k.1), channel_id=1, source_target_pairs={{0,64},{64,128},{128,192},{192,0},{1,65},{65,129},{129,193},{193,1... | collective-permute-start | bytes 786440 | tf_op jit(solution)/shard_map/ppermute | solution.py:418
  1.5 20.7 %collective-permute-start.1 = (bf16[512,256]{1,0:T(8,128)(2,1)}, bf16[512,256]{1,0:T(8,128)(2,1)S(1)}, u32[]{:S(2)}, u32[]{:S(2)}) collective-permute-start(bf16[512,256]{1,0:T(8,128)(2,1)} %v.1), channel_id=1, source_target_pairs={{0,64},{64,128},{128,192},{192,0},{1,65},{65,129},{129,193},{193,1... | collective-permute-start | bytes 786440 | tf_op jit(solution)/shard_map/ppermute | solution.py:418
  2.7 19.5 %collective-permute-start.2 = (bf16[512,256]{1,0:T(8,128)(2,1)}, bf16[512,256]{1,0:T(8,128)(2,1)}, u32[]{:S(2)}, u32[]{:S(2)}) collective-permute-start(bf16[512,256]{1,0:T(8,128)(2,1)} %k.1), channel_id=1, source_target_pairs={{0,192},{64,0},{128,64},{192,128},{1,193},{65,1},{129,65},{193,129... | collective-permute-start | bytes 786440 | tf_op jit(solution)/shard_map/ppermute | solution.py:418
  3.5 18.7 %collective-permute-start.3 = (bf16[512,256]{1,0:T(8,128)(2,1)}, bf16[512,256]{1,0:T(8,128)(2,1)}, u32[]{:S(2)}, u32[]{:S(2)}) collective-permute-start(bf16[512,256]{1,0:T(8,128)(2,1)} %v.1), channel_id=1, source_target_pairs={{0,192},{64,0},{128,64},{192,128},{1,193},{65,1},{129,65},{193,129... | collective-permute-start | bytes 786440 | tf_op jit(solution)/shard_map/ppermute | solution.py:418
  7.3 23.4 %all-to-all-start.2 = ((bf16[32,32,128]{2,1,0:T(8,128)(2,1)}), bf16[32,32,128]{2,1,0:T(8,128)(2,1)}, u32[]{:S(2)}, u32[]{:S(2)}) async-start(bf16[32,32,128]{2,1,0:T(8,128)(2,1)} %bitcast.3), calls=%async_computation.2 | async-start | bytes 524288 | tf_op jit(solution)/shard_map/all_to_all | solution.py:442
  19.3 17.7 %copy-start.1 = (bf16[4,512,256]{2,1,0:T(8,128)(2,1)S(1)}, bf16[4,512,256]{2,1,0:T(8,128)(2,1)}, u32[]{:S(2)}) copy-start(bf16[4,512,256]{2,1,0:T(8,128)(2,1)} %wv.1) | copy-start | bytes 3145732
  22.2 14.9 %copy-start = (bf16[4,512,256]{2,1,0:T(8,128)(2,1)S(1)}, bf16[4,512,256]{2,1,0:T(8,128)(2,1)}, u32[]{:S(2)}) copy-start(bf16[4,512,256]{2,1,0:T(8,128)(2,1)} %wk.1) | copy-start | bytes 3145732
  22.2 10.3 %collective-permute-start.4 = (bf16[1024,256]{1,0:T(8,128)(2,1)}, bf16[1024,256]{1,0:T(8,128)(2,1)}, u32[]{:S(2)}, u32[]{:S(2)}) collective-permute-start(bf16[1024,256]{1,0:T(8,128)(2,1)} %refs_1_.1), channel_id=1, source_target_pairs={{0,4},{4,0},{1,5},{5,1},{2,6},{6,2},{3,7},{7,3},{8,12},{12,8},{9,1... | collective-permute-start | bytes 1572872 | tf_op jit(solution)/shard_map/ppermute | solution.py:418
  22.3 10.3 %collective-permute-start.5 = (bf16[1024,256]{1,0:T(8,128)(2,1)}, bf16[1024,256]{1,0:T(8,128)(2,1)}, u32[]{:S(2)}, u32[]{:S(2)}) collective-permute-start(bf16[1024,256]{1,0:T(8,128)(2,1)} %refs_3_.1), channel_id=1, source_target_pairs={{0,4},{4,0},{1,5},{5,1},{2,6},{6,2},{3,7},{7,3},{8,12},{12,8},{9,1... | collective-permute-start | bytes 1572872 | tf_op jit(solution)/shard_map/ppermute | solution.py:418
  22.8 24.1 %collective-permute-start.13 = (bf16[512,256]{1,0:T(8,128)(2,1)}, bf16[512,256]{1,0:T(8,128)(2,1)}, u32[]{:S(2)}, u32[]{:S(2)}) collective-permute-start(bf16[512,256]{1,0:T(8,128)(2,1)} %collective-permute-done.3.refs_7_), channel_id=1, source_target_pairs={{0,192},{64,0},{128,64},{192,128},{1,193},{65,1},{129,65},{193,129... | collective-permute-start | bytes 786440 | tf_op jit(solution)/shard_map/ppermute | solution.py:418
  23.3 24.0 %collective-permute-start.11 = (bf16[512,256]{1,0:T(8,128)(2,1)}, bf16[512,256]{1,0:T(8,128)(2,1)}, u32[]{:S(2)}, u32[]{:S(2)}) collective-permute-start(bf16[512,256]{1,0:T(8,128)(2,1)} %collective-permute-done.3.refs_7_), channel_id=1, source_target_pairs={{0,4},{4,0},{1,5},{5,1},{2,6},{6,2},{3,7},{7,3},{8,12},{12,8},{9,1... | collective-permute-start | bytes 786440 | tf_op jit(solution)/shard_map/ppermute | solution.py:418
  23.3 23.5 %collective-permute-start.12 = (bf16[512,256]{1,0:T(8,128)(2,1)S(1)}, bf16[512,256]{1,0:T(8,128)(2,1)}, u32[]{:S(2)}, u32[]{:S(2)}) collective-permute-start(bf16[512,256]{1,0:T(8,128)(2,1)S(1)} %collective-permute-done.refs_2_), channel_id=1, source_target_pairs={{0,64},{64,128},{128,192},{192,0},{1,65},{65,129},{129,193},{193,1... | collective-permute-start | bytes 786440 | tf_op jit(solution)/shard_map/ppermute | solution.py:418
  30.7 6.3 %copy-start.7 = (bf16[4,256]{1,0:T(4,128)(2,1)S(1)}, bf16[4,256]{1,0:T(4,128)(2,1)}, u32[]{:S(2)}) copy-start(bf16[4,256]{1,0:T(4,128)(2,1)} %nv.1) | copy-start | bytes 6148
  30.7 6.3 %copy-start.10 = (s32[4]{0:T(128)S(1)}, s32[4]{0:T(128)}, u32[]{:S(2)}) copy-start(s32[4]{0:T(128)} %length_ref.1) | copy-start | bytes 52
  32.5 15.0 %collective-permute-start.8 = (bf16[512,256]{1,0:T(8,128)(2,1)S(1)}, bf16[512,256]{1,0:T(8,128)(2,1)}, u32[]{:S(2)}, u32[]{:S(2)}) collective-permute-start(bf16[512,256]{1,0:T(8,128)(2,1)S(1)} %collective-permute-done.refs_2_), channel_id=1, source_target_pairs={{0,4},{4,0},{1,5},{5,1},{2,6},{6,2},{3,7},{7,3},{8,12},{12,8},{9,1... | collective-permute-start | bytes 786440 | tf_op jit(solution)/shard_map/ppermute | solution.py:418
  32.6 15.3 %collective-permute-start.10 = (bf16[512,256]{1,0:T(8,128)(2,1)}, bf16[512,256]{1,0:T(8,128)(2,1)}, u32[]{:S(2)}, u32[]{:S(2)}) collective-permute-start(bf16[512,256]{1,0:T(8,128)(2,1)} %collective-permute-done.2.refs_6_), channel_id=1, source_target_pairs={{0,4},{4,0},{1,5},{5,1},{2,6},{6,2},{3,7},{7,3},{8,12},{12,8},{9,1... | collective-permute-start | bytes 786440 | tf_op jit(solution)/shard_map/ppermute | solution.py:418
  33.1 9.7 %all-to-all-start.3 = ((bf16[32,32,128]{2,1,0:T(8,128)(2,1)}), bf16[32,32,128]{2,1,0:T(8,128)(2,1)S(1)}, u32[]{:S(2)}, u32[]{:S(2)}) async-start(bf16[32,32,128]{2,1,0:T(8,128)(2,1)} %select.2), calls=%async_computation.3 | async-start | bytes 524288 | tf_op jit(solution)/shard_map/all_to_all | solution.py:517
  40.0 7.9 %copy-start.11 = (bf16[32,40,128]{2,1,0:T(8,128)(2,1)S(1)}, bf16[32,40,128]{2,1,0:T(8,128)(2,1)}, u32[]{:S(2)}) copy-start(bf16[32,40,128]{2,1,0:T(8,128)(2,1)} %get-tuple-element.150) | copy-start | bytes 983044
  46.8 6.7 %collective-permute-start.9 = (bf16[512,256]{1,0:T(8,128)(2,1)S(1)}, bf16[512,256]{1,0:T(8,128)(2,1)S(1)}, u32[]{:S(2)}, u32[]{:S(2)}) collective-permute-start(bf16[512,256]{1,0:T(8,128)(2,1)S(1)} %collective-permute-done.1.refs_3_), channel_id=1, source_target_pairs={{0,4},{4,0},{1,5},{5,1},{2,6},{6,2},{3,7},{7,3},{8,12},{12,8},{9,1... | collective-permute-start | bytes 786440 | tf_op jit(solution)/shard_map/ppermute | solution.py:418
  46.9 6.7 %collective-permute-start.6 = (bf16[512,256]{1,0:T(8,128)(2,1)S(1)}, bf16[512,256]{1,0:T(8,128)(2,1)S(1)}, u32[]{:S(2)}, u32[]{:S(2)}) collective-permute-start(bf16[512,256]{1,0:T(8,128)(2,1)S(1)} %copy-done.2), channel_id=1, source_target_pairs={{0,4},{4,0},{1,5},{5,1},{2,6},{6,2},{3,7},{7,3},{8,12},{12,8},{9,1... | collective-permute-start | bytes 786440 | tf_op jit(solution)/shard_map/ppermute | solution.py:418
  47.4 6.2 %collective-permute-start.7 = (bf16[512,256]{1,0:T(8,128)(2,1)S(1)}, bf16[512,256]{1,0:T(8,128)(2,1)S(1)}, u32[]{:S(2)}, u32[]{:S(2)}) collective-permute-start(bf16[512,256]{1,0:T(8,128)(2,1)S(1)} %copy-done.3), channel_id=1, source_target_pairs={{0,4},{4,0},{1,5},{5,1},{2,6},{6,2},{3,7},{7,3},{8,12},{12,8},{9,1... | collective-permute-start | bytes 786440 | tf_op jit(solution)/shard_map/ppermute | solution.py:418
  47.5 6.1 %collective-permute-start.14 = (bf16[512,256]{1,0:T(8,128)(2,1)}, bf16[512,256]{1,0:T(8,128)(2,1)S(1)}, u32[]{:S(2)}, u32[]{:S(2)}) collective-permute-start(bf16[512,256]{1,0:T(8,128)(2,1)} %collective-permute-done.12.refs_10_), channel_id=1, source_target_pairs={{0,4},{4,0},{1,5},{5,1},{2,6},{6,2},{3,7},{7,3},{8,12},{12,8},{9,1... | collective-permute-start | bytes 786440 | tf_op jit(solution)/shard_map/ppermute | solution.py:418
  47.9 5.7 %collective-permute-start.15 = (bf16[512,256]{1,0:T(8,128)(2,1)}, bf16[512,256]{1,0:T(8,128)(2,1)S(1)}, u32[]{:S(2)}, u32[]{:S(2)}) collective-permute-start(bf16[512,256]{1,0:T(8,128)(2,1)} %collective-permute-done.13.refs_11_), channel_id=1, source_target_pairs={{0,4},{4,0},{1,5},{5,1},{2,6},{6,2},{3,7},{7,3},{8,12},{12,8},{9,1... | collective-permute-start | bytes 786440 | tf_op jit(solution)/shard_map/ppermute | solution.py:418
  48.7 11.6 %all-to-all-start.4 = ((bf16[32,40,128]{2,1,0:T(8,128)(2,1)}), bf16[32,40,128]{2,1,0:T(8,128)(2,1)S(1)}, u32[]{:S(2)}, u32[]{:S(2)}) async-start(bf16[32,40,128]{2,1,0:T(8,128)(2,1)} %prefix.2), calls=%async_computation.4 | async-start | bytes 655360 | tf_op jit(solution)/shard_map/all_to_all | solution.py:517
  (7 other events, 29.4 us)
